TPU v7x, 512 devices: a whole 4x8x8 slice. The times are simulated.
512 devices in a mesh: region: 32 (over z, x), sub: 16 (over y, core).
Axes of the slice: x: 4, y: 8, z: 8, core: 2. Of those that a mesh axis runs over, the one named last changes fastest.
Arguments:
- coords: float32 [3, 524288], P(None, ('region', 'sub')), may hold values from 0 to 2051, as said below
- noise_var: float32 [524288], P(('region', 'sub')), may hold values from 3 to 6
- pair_list: int32 [3, 2048], P(None, ('region', 'sub')), may hold values from 0 to 1, as said below
- probes: float32 [64, 524288], P(None, ('region', 'sub')), may hold values from -15 to 15
Outputs:
- solution: float32 [64, 524288], P(None, ('region', 'sub'))
- residual: float32 [64, 524288], P(None, ('region', 'sub'))
Inputs may be any that keep to these rules, and one draw needn't show every extreme that they name: `coords`: row 0 of column p lies in [p // 256, p // 256 + 4); rows 1 and 2 lie in [0, 4). `pair_list`: entry k, b is 0 wherever b + k + 1 >= 2048.
All inputs are finite; a program needn't handle non-finite values.
Results may differ from a plain program's by a relative error of at most 0.0003.
Values sent between devices are 32-bit elements; how exact they have to be, the bound alone decides.
No kernel may reach another device: no remote copies, remote signals or barrier semaphores. Data moves between devices by JAX's collectives and lax.ppermute only.
A program may use at most 64 MiB of HBM per device.

v0:
```python
import jax
import jax.numpy as jnp
from jax import lax
from jax.sharding import PartitionSpec as P

ITERS = 3


def from_behind(array, axis, by):
    count = lax.axis_size(axis)
    pairs = [(i, i + by) for i in range(count) if 0 <= i + by < count]
    return lax.ppermute(array, axis, pairs)


def wendland(left, right):
    squared = (left[0][..., :, None] - right[0][..., None, :]) ** 2
    squared = squared + (left[1][..., :, None] - right[1][..., None, :]) ** 2
    squared = squared + (left[2][..., :, None] - right[2][..., None, :]) ** 2
    distance = jnp.sqrt(squared)
    support = jnp.maximum(1.0 - distance, 0.0)
    return support**4 * (4.0 * distance + 1.0)


def squares(residual):
    return lax.psum(jnp.sum(residual * residual, axis=1), ("region", "sub"))


def per_device(coords, noise_var, pair_list, probes):
    probe_count, points_here = probes.shape
    links = pair_list.shape[0]
    blocks_here = pair_list.shape[1]
    block_len = points_here // blocks_here
    span_cols = links * block_len
    local_c = coords.reshape(3, blocks_here, block_len)
    weights = pair_list.astype(jnp.float32)
    ahead_c = from_behind(coords[:, :span_cols], ("region", "sub"), -1)
    ext_c = jnp.concatenate([local_c, ahead_c.reshape(3, links, block_len)], axis=1)
    solution = jnp.zeros_like(probes)
    residual = probes
    direction = probes
    res_norm = squares(residual)
    for step in range(ITERS):
        apply_ahead_v = from_behind(direction[:, :span_cols], ("region", "sub"), -1)
        ext_v = jnp.concatenate([direction, apply_ahead_v], axis=1).reshape(
            probe_count, blocks_here + links, block_len
        )
        local_v = ext_v[:, :blocks_here]
        result = (noise_var[None, :] * direction).reshape(probe_count, blocks_here, block_len)
        spill = jnp.zeros((probe_count, blocks_here + links, block_len), jnp.float32)
        for offset in range(links + 1):
            kernel_block = wendland(local_c, ext_c[:, offset : offset + blocks_here])
            if offset > 0:
                kernel_block = kernel_block * weights[offset - 1][:, None, None]
            result = result + jnp.einsum(
                "pbj,bij->pbi",
                ext_v[:, offset : offset + blocks_here],
                kernel_block,
                precision=lax.Precision.HIGHEST,
            )
            if offset > 0:
                spill = spill.at[:, offset : offset + blocks_here].add(
                    jnp.einsum(
                        "pbi,bij->pbj", local_v, kernel_block, precision=lax.Precision.HIGHEST
                    )
                )
        result = result + spill[:, :blocks_here]
        apply_result = result
        apply_spill = spill[:, blocks_here:]
        returned = from_behind(apply_spill, ("region", "sub"), 1)
        apply_result = apply_result.at[:, :links].add(returned)
        product = apply_result.reshape(probe_count, points_here)
        curv = lax.psum(jnp.sum(direction * product, axis=1), ("region", "sub"))
        step_size = res_norm / curv
        solution = solution + step_size[:, None] * direction
        residual = residual - step_size[:, None] * product
        next_norm = squares(residual)
        direction = residual + (next_norm / res_norm)[:, None] * direction
        res_norm = next_norm
    return (solution, residual)


def solution(mesh):
    in_specs = (
        P(None, ("region", "sub")),
        P(("region", "sub")),
        P(None, ("region", "sub")),
        P(None, ("region", "sub")),
    )
    out_specs = (P(None, ("region", "sub")), P(None, ("region", "sub")))
    return jax.shard_map(
        per_device, mesh=mesh, in_specs=in_specs, out_specs=out_specs, check_vma=False
    )
```

profile of v0, /device:TPU:1, one launch (start us, length us, event | category | flops | bytes accessed | tf_op | source)
XLA Modules:
  0.0 581.7 jit_solution(11361054826122552760)
XLA Ops:
  0.6 0.8 slice.488
  1.4 8.9 %collective-permute-start.1 = (f32[3,768]{1,0:T(4,128)S(1)}, f32[3,768]{1,0:T(4,128)S(1)}, u32[]{:S(2)}, u32[]{:S(2)}) collective-permute-start(f32[3,768]{1,0:T(4,128)S(1)} %slice.488), channel_id=1, source_target_pairs={{1,0},{2,1},{3,2},{4,3},{5,4},{6,5},{7,6},{8,7},{9,8},{10,9},{11,1... | collective-permute-start | bytes 27656 | tf_op jit(solution)/shard_map/ppermute | solution.py:12
  10.3 0.9 slice.486
  11.3 1.9 collective-permute-start
  13.3 0.7 copy-done.1
  14.1 4.1 collective-permute-done
  18.4 0.2 fusion.130
  18.6 1.9 convolution_bitcast_fusion.16
  20.6 1.9 fusion.6
  22.5 1.9 fusion.7
  24.5 2.2 convolution_bitcast_fusion.18
  26.6 2.2 convolution_bitcast_fusion.19
  28.8 2.2 convolution_bitcast_fusion.17
  31.0 1.9 collective-permute-start.2
  32.9 2.1 fusion.4
  35.0 0.5 collective-permute-done.2
  35.7 105.5 %all-reduce.3 = (f32[64]{0:T(128)S(1)}, f32[64]{0:T(128)S(1)}) all-reduce(f32[64]{0:T(128)S(1)} %get-tuple-element.147, f32[64]{0:T(128)S(1)} %get-tuple-element.146), channel_id=1, replica_groups=mesh['region'=32,'sub'=16] {'region','sub'}, use_global_device_ids=true, to_apply=%region_1.0 | all-reduce | flops 128 | bytes 1024 | tf_op jit(solution)/shard_map/psum | solution.py:25
  141.2 0.2 multiply_reduce_fusion.3
  141.4 94.3 %psum.44 = f32[64]{0:T(128)S(1)} all-reduce(f32[64]{0:T(128)S(1)} %multiply_reduce_fusion.3), channel_id=1, replica_groups=mesh['region'=32,'sub'=16] {'region','sub'}, use_global_device_ids=true, to_apply=%region_5.0 | all-reduce | flops 64 | bytes 512 | tf_op jit(solution)/shard_map/psum | solution.py:25
  235.8 2.8 collective-permute-start.3
  238.6 4.2 collective-permute-done.3
  243.0 0.2 fusion.129
  243.2 1.9 convolution_bitcast_fusion.9
  245.2 1.9 fusion.14
  247.1 1.9 fusion.15
  249.0 2.2 convolution_bitcast_fusion.11
  251.2 2.2 convolution_bitcast_fusion.12
  253.4 2.2 convolution_bitcast_fusion.10
  255.5 1.9 collective-permute-start.4
  257.5 2.1 fusion.12
  259.6 0.5 collective-permute-done.4
  260.3 100.3 %psum.45 = f32[64]{0:T(128)S(1)} all-reduce(f32[64]{0:T(128)S(1)} %multiply_reduce_fusion.2), channel_id=1, replica_groups=mesh['region'=32,'sub'=16] {'region','sub'}, use_global_device_ids=true, to_apply=%region_7.0 | all-reduce | flops 64 | bytes 512 | tf_op jit(solution)/shard_map/psum | solution.py:72
  360.6 0.2 multiply_reduce_fusion.1
  360.8 94.3 %psum.46 = f32[64]{0:T(128)S(1)} all-reduce(f32[64]{0:T(128)S(1)} %get-tuple-element.155), channel_id=1, replica_groups=mesh['region'=32,'sub'=16] {'region','sub'}, use_global_device_ids=true, to_apply=%region_9.0 | all-reduce | flops 64 | bytes 512 | tf_op jit(solution)/shard_map/psum | solution.py:25
  455.3 2.8 collective-permute-start.5
  458.1 4.2 collective-permute-done.5
  462.5 0.2 fusion.128
  462.7 1.9 convolution_bitcast_fusion.2
  464.6 1.9 fusion.22
  466.5 1.9 fusion.23
  468.5 2.2 convolution_bitcast_fusion.4
  470.7 2.2 convolution_bitcast_fusion.3
  472.8 2.2 convolution_bitcast_fusion.5
  475.0 1.9 collective-permute-start.6
  476.9 2.1 fusion.20
  479.1 0.5 collective-permute-done.6
  479.7 101.0 %psum.47 = f32[64]{0:T(128)S(1)} all-reduce(f32[64]{0:T(128)S(1)} %multiply_reduce_fusion), channel_id=1, replica_groups=mesh['region'=32,'sub'=16] {'region','sub'}, use_global_device_ids=true, to_apply=%region_11.0 | all-reduce | flops 64 | bytes 512 | tf_op jit(solution)/shard_map/psum | solution.py:72
  580.7 0.9 multiply_subtract_fusion
  (51 shorter events, 1.7 us)
Async XLA Ops:
  0.6 12.6 %copy-start = (f32[64,1024]{1,0:T(8,128)S(1)}, f32[64,1024]{1,0:T(8,128)}, u32[]{:S(2)}) copy-start(f32[64,1024]{1,0:T(8,128)} %param.31) | copy-start | bytes 786436
  1.4 11.8 %copy-start.3 = (s32[3,4]{1,0:T(4,128)S(1)}, s32[3,4]{1,0:T(4,128)}, u32[]{:S(2)}) copy-start(s32[3,4]{1,0:T(4,128)} %param.30) | copy-start | bytes 148
  1.4 12.7 %collective-permute-start.1 = (f32[3,768]{1,0:T(4,128)S(1)}, f32[3,768]{1,0:T(4,128)S(1)}, u32[]{:S(2)}, u32[]{:S(2)}) collective-permute-start(f32[3,768]{1,0:T(4,128)S(1)} %slice.488), channel_id=1, source_target_pairs={{1,0},{2,1},{3,2},{4,3},{5,4},{6,5},{7,6},{8,7},{9,8},{10,9},{11,1... | collective-permute-start | bytes 27656 | tf_op jit(solution)/shard_map/ppermute | solution.py:12
  11.3 2.0 copy-start.2
  11.3 7.0 %collective-permute-start = (f32[64,768]{1,0:T(8,128)S(1)}, f32[64,768]{1,0:T(8,128)S(1)}, u32[]{:S(2)}, u32[]{:S(2)}) collective-permute-start(f32[64,768]{1,0:T(8,128)S(1)} %slice.486), channel_id=1, source_target_pairs={{1,0},{2,1},{3,2},{4,3},{5,4},{6,5},{7,6},{8,7},{9,8},{10,9},{11,1... | collective-permute-start | bytes 589832 | tf_op jit(solution)/shard_map/ppermute | solution.py:12
  13.3 0.7 copy-start.1
  31.0 4.5 collective-permute-start.2
  235.8 7.0 %collective-permute-start.3 = (f32[64,768]{1,0:T(8,128)S(1)}, f32[64,768]{1,0:T(8,128)S(1)}, u32[]{:S(2)}, u32[]{:S(2)}) collective-permute-start(f32[64,768]{1,0:T(8,128)S(1)} %slice.553), channel_id=1, source_target_pairs={{1,0},{2,1},{3,2},{4,3},{5,4},{6,5},{7,6},{8,7},{9,8},{10,9},{11,1... | collective-permute-start | bytes 589832 | tf_op jit(solution)/shard_map/ppermute | solution.py:12
  255.5 4.5 collective-permute-start.4
  455.3 7.0 %collective-permute-start.5 = (f32[64,768]{1,0:T(8,128)S(1)}, f32[64,768]{1,0:T(8,128)S(1)}, u32[]{:S(2)}, u32[]{:S(2)}) collective-permute-start(f32[64,768]{1,0:T(8,128)S(1)} %slice.562), channel_id=1, source_target_pairs={{1,0},{2,1},{3,2},{4,3},{5,4},{6,5},{7,6},{8,7},{9,8},{10,9},{11,1... | collective-permute-start | bytes 589832 | tf_op jit(solution)/shard_map/ppermute | solution.py:12
  475.0 4.5 collective-permute-start.6
where the time goes:
time: 583 us; the launch traced here: 582 us
  blocking collectives  495 us (85%)
  matrix products  43 us (7%)
  starting transfers between devices  22.2 us (4%)
  waiting for transfers between devices  13.9 us (2%)
    psum x3, blocking collectives, squares(): return lax.psum(jnp.sum(residual * residual, axis=1), ('region', 'sub'))  294 us
    psum x2, blocking collectives, per_device(): curv = lax.psum(jnp.sum(direction * product, axis=1), ('region', 'sub'))  201 us
    dot_general x12, matrix products, per_device(): jnp.einsum('pbj,bij->pbi', ext_v[:, offset:offset + blocks_here], kernel_...  25.8 us
    ppermute x7, starting transfers between devices, from_behind(): return lax.ppermute(array, axis, pairs)  22.2 us
    dot_general x9, matrix products, per_device(): jnp.einsum('pbi,bij->pbj', local_v, kernel_block, precision=lax.Precision...  17.2 us
    ppermute x7, waiting for transfers between devices, from_behind(): return lax.ppermute(array, axis, pairs)  13.9 us
  transfers between devices with their start and end apart: 7, of which 6 were waited for; matrix products, arithmetic and copies ran while one was open for 1% of the time, Pallas kernels for 0%

commit v1 on v0

v1 whole, which is shorter than its diff:
```python
import functools

import jax
import jax.numpy as jnp
from jax import lax
from jax.experimental import pallas as pl
from jax.experimental.pallas import tpu as pltpu
from jax.sharding import PartitionSpec as P

ITERS = 3
AXES = ("region", "sub")
SHIFT = 6.0
MAX_AMP = 100.0
MAX_NORM = 30.0
F32 = jnp.float32
BF16 = jnp.bfloat16
VMEM_LIMIT = 40 * 1024 * 1024


def shifted(array, by):
    count = lax.axis_size(AXES)
    pairs = [(i, i + by) for i in range(count) if 0 <= i + by < count]
    return lax.ppermute(array, AXES, pairs)


def wendland(left, right):
    squared = (left[0][..., :, None] - right[0][..., None, :]) ** 2
    squared = squared + (left[1][..., :, None] - right[1][..., None, :]) ** 2
    squared = squared + (left[2][..., :, None] - right[2][..., None, :]) ** 2
    distance = jnp.sqrt(squared)
    support = jnp.maximum(1.0 - distance, 0.0)
    return support**4 * (4.0 * distance + 1.0)


def squares(residual):
    return lax.psum(jnp.sum(residual * residual, axis=1), AXES)


def plain(coords, noise_var, pair_list, probes):
    probe_count, points_here = probes.shape
    links = pair_list.shape[0]
    blocks_here = pair_list.shape[1]
    block_len = points_here // blocks_here
    span_cols = links * block_len
    local_c = coords.reshape(3, blocks_here, block_len)
    weights = pair_list.astype(F32)
    ahead_c = shifted(coords[:, :span_cols], -1)
    ext_c = jnp.concatenate([local_c, ahead_c.reshape(3, links, block_len)], axis=1)

    def step(_, state):
        solution, residual, direction, res_norm = state
        ahead_v = shifted(direction[:, :span_cols], -1)
        ext_v = jnp.concatenate([direction, ahead_v], axis=1).reshape(probe_count, blocks_here + links, block_len)
        local_v = ext_v[:, :blocks_here]
        result = (noise_var[None, :] * direction).reshape(probe_count, blocks_here, block_len)
        spill = jnp.zeros((probe_count, blocks_here + links, block_len), F32)
        for offset in range(links + 1):
            kernel_block = wendland(local_c, ext_c[:, offset : offset + blocks_here])
            if offset > 0:
                kernel_block = kernel_block * weights[offset - 1][:, None, None]
            result = result + jnp.einsum(
                "pbj,bij->pbi", ext_v[:, offset : offset + blocks_here], kernel_block, precision=lax.Precision.HIGHEST
            )
            if offset > 0:
                spill = spill.at[:, offset : offset + blocks_here].add(
                    jnp.einsum("pbi,bij->pbj", local_v, kernel_block, precision=lax.Precision.HIGHEST)
                )
        result = result + spill[:, :blocks_here]
        result = result.at[:, :links].add(shifted(spill[:, blocks_here:], 1))
        product = result.reshape(probe_count, points_here)
        step_size = res_norm / lax.psum(jnp.sum(direction * product, axis=1), AXES)
        solution = solution + step_size[:, None] * direction
        residual = residual - step_size[:, None] * product
        next_norm = squares(residual)
        direction = residual + (next_norm / res_norm)[:, None] * direction
        return solution, residual, direction, next_norm

    state = (jnp.zeros_like(probes), probes, probes, squares(probes))
    solution, residual, _, _ = lax.fori_loop(0, ITERS, step, state)
    return solution, residual


def pack_kernel(coords, noise, pair, probes, to_left, to_right):
    links, blocks = pair.shape
    length = coords.shape[1] // blocks
    span = links * length
    start = coords.shape[1] - span
    rows = probes.shape[0]
    to_left[0:rows, :] = probes[:, 0:span]
    to_right[0:rows, :] = probes[:, start:]
    to_left[rows : rows + 8, :] = jnp.concatenate([coords[:, 0:span], jnp.zeros((5, span), F32)], axis=0)
    flags = [
        jnp.concatenate(
            [jnp.full((1, length), pair[k, b].astype(F32), F32) for b in range(blocks - links, blocks)], axis=1
        )
        for k in range(links)
    ]
    to_right[rows : rows + 8, :] = jnp.concatenate(
        [coords[:, start:]] + flags + [jnp.zeros((8 - 3 - links, span), F32)], axis=0
    )


def split(value):
    high = value.astype(BF16)
    return high, (value - high.astype(F32)).astype(BF16)


def spread(halves, low, middle, high, rows, span, here):
    for ref, at, size in ((low, 0, span), (middle, span, here), (high, span + here, span)):
        top, rest = split(ref[0:rows, 0:size])
        halves[0:rows, at : at + size] = top
        halves[rows : 2 * rows, at : at + size] = rest


def product(halves, k_high, k_low, noise, vector, out, to_left, to_right, rows, length, blocks, links):
    depth = (2 * links + 1) * length
    span = links * length
    start = blocks * length - span
    for i in range(blocks):
        window = slice(i * length, i * length + depth)
        at = slice(i * length, (i + 1) * length)
        both = jnp.dot(halves[:, window], k_high[i], preferred_element_type=F32)
        rest = jnp.dot(halves[0:rows, window], k_low[i], preferred_element_type=F32)
        value = both[0:rows] + (both[rows : 2 * rows] + rest) + (noise[:, at] - SHIFT) * vector[:, at]
        out[:, at] = value
        if to_left is not None:
            if i < links:
                to_left[:, at] = value
            if i >= blocks - links:
                to_right[:, i * length - start : (i + 1) * length - start] = value


def first_kernel(
    coords, noise, pair, probes, low, high, k_high, k_low, out, to_left, to_right, halves, columns, *, strip
):
    links, blocks = pair.shape
    rows, here = probes.shape
    length = here // blocks
    span = links * length
    for ref, at, size, row in ((low, 0, span, rows), (coords, span, here, 0), (high, span + here, span, rows)):
        turned = jnp.transpose(jnp.concatenate([ref[row : row + 3, 0:size], jnp.zeros((5, size), F32)], axis=0))
        for d in range(3):
            columns[d, at : at + size, :] = jnp.broadcast_to(turned[:, d : d + 1], (size, 128))
    spread(halves, low, probes, high, rows, span, here)
    for i in range(blocks):
        mine = [coords[d : d + 1, i * length : (i + 1) * length] for d in range(3)]
        for o in range(2 * links + 1):
            j = i + o
            k = abs(o - links) - 1
            if o == links:
                flag = jnp.ones((1, length), F32)
            elif o > links:
                flag = jnp.full((1, length), pair[k, i].astype(F32), F32)
            elif j >= links:
                flag = jnp.full((1, length), pair[k, j - links].astype(F32), F32)
            else:
                flag = low[rows + 3 + k : rows + 4 + k, j * length : (j + 1) * length]
            flag4 = 4.0 * flag

            def body(s, _):
                at = pl.multiple_of(s * strip, strip)
                from_row = pl.multiple_of(j * length + s * strip, strip)
                squared = None
                for d in range(3):
                    column = columns[d, pl.ds(from_row, strip), :]
                    away = jnp.concatenate([column] * (length // 128), axis=1) - mine[d]
                    squared = away * away if squared is None else squared + away * away
                squared = jnp.maximum(squared, 1e-30)
                distance = squared * lax.rsqrt(squared)
                support = jnp.maximum(1.0 - distance, 0.0)
                support = support * support
                value = support * support * (flag4 * distance + flag)
                top, rest = split(value)
                k_high[i, pl.ds(o * length + at, strip), :] = top
                k_low[i, pl.ds(o * length + at, strip), :] = rest
                return 0

            lax.fori_loop(0, length // strip, body, 0)
    product(halves, k_high, k_low, noise, probes, out, to_left, to_right, rows, length, blocks, links)


def next_kernel(noise, vector, low, high, k_high, k_low, out, to_left, to_right, halves):
    rows, here = vector.shape
    blocks, depth, length = k_high.shape
    span = low.shape[1]
    spread(halves, low, vector, high, rows, span, here)
    product(halves, k_high, k_low, noise, vector, out, to_left, to_right, rows, length, blocks, span // length)


def last_kernel(noise, first, second, vector, low, high, k_high, k_low, out, sums, halves):
    rows, here = vector.shape
    blocks, depth, length = k_high.shape
    span = low.shape[1]
    spread(halves, low, vector, high, rows, span, here)
    product(halves, k_high, k_low, noise, vector, out, None, None, rows, length, blocks, span // length)
    basis = (first, second, vector, out)
    lane = lax.broadcasted_iota(jnp.int32, (rows, 128), 1)
    table = jnp.zeros((rows, 128), F32)
    for power in range(2 * ITERS + 1):
        left, right = basis[power // 2], basis[power - power // 2]
        part = None
        for at in range(0, here, 128):
            term = left[:, at : at + 128] * right[:, at : at + 128]
            part = term if part is None else part + term
        table = jnp.where(lane == power, jnp.sum(part, axis=1, keepdims=True), table)
    turned = jnp.transpose(table)[0:8, :]
    compact = jnp.concatenate([turned[0:4], turned[4:8]], axis=1)
    sums[...] = jnp.broadcast_to(compact[None], sums.shape)


def polynomials(moment):
    def dot(p, q):
        total, size = 0.0, 0.0
        for i, x in enumerate(p):
            for j, y in enumerate(q):
                term = x * y * moment[i + j]
                total, size = total + term, size + jnp.abs(term)
        return total, size

    def add(p, q, factor):
        count = max(len(p), len(q))
        p, q = p + [0.0] * (count - len(p)), q + [0.0] * (count - len(q))
        return [x + factor * y for x, y in zip(p, q)]

    one = jnp.ones_like(moment[0])
    solution, residual, direction = [jnp.zeros_like(one)], [one], [one]
    norm = moment[0]
    good = norm > 0.0
    for step in range(ITERS):
        image = add([0.0 * one] + direction, direction, SHIFT)
        curvature, size = dot(direction, image)
        good = good & (size <= MAX_AMP * curvature)
        step_size = norm / curvature
        solution = add(solution, direction, step_size)
        residual = add(residual, image, -step_size)
        new, size = dot(residual, residual)
        if step < ITERS - 1:
            good = good & (size <= MAX_AMP * new)
            direction = add(residual, direction, new / norm)
        norm = new
    size = sum(jnp.abs(x) * jnp.sqrt(moment[2 * i]) for i, x in enumerate(residual))
    good = good & (size * size <= MAX_NORM * MAX_NORM * norm)
    return solution, residual, good


def small_kernel(sums, coefficients, good):
    total = jnp.sum(sums[...], axis=0)
    moment = [total[k : k + 1, 0:64] for k in range(4)] + [total[k : k + 1, 64:128] for k in range(3)]
    solution, residual, fine = polynomials(moment)
    table = jnp.concatenate(solution + residual + [jnp.zeros_like(moment[0])], axis=0)
    table = jnp.concatenate([table, jnp.zeros_like(table)], axis=1)
    coefficients[...] = jnp.transpose(jnp.concatenate([table, jnp.zeros((120, 128), F32)], axis=0))[0:64]
    good[...] = jnp.min(jnp.where(fine, 1.0, 0.0), axis=1, keepdims=True)


def combine_kernel(coefficients, first, second, third, fourth, solution, residual):
    basis = (first[...], second[...], third[...], fourth[...])

    def mix(at, count):
        total = coefficients[:, at : at + 1] * basis[0]
        for k in range(1, count):
            total = total + coefficients[:, at + k : at + k + 1] * basis[k]
        return total

    solution[...] = mix(0, ITERS)
    residual[...] = mix(ITERS, ITERS + 1)


def in_vmem(array):
    return pltpu.with_memory_space_constraint(array, pltpu.VMEM)


def call(kernel, name, out_shape, in_specs=None, scratch_shapes=()):
    kwargs = {} if in_specs is None else {"in_specs": in_specs}
    return pl.pallas_call(
        kernel,
        out_shape=out_shape,
        scratch_shapes=scratch_shapes,
        compiler_params=pltpu.CompilerParams(vmem_limit_bytes=VMEM_LIMIT),
        name=name,
        **kwargs,
    )


def per_device(coords, noise_var, pair_list, probes):
    rows, here = probes.shape
    links, blocks = pair_list.shape
    length = here // blocks
    span = links * length
    depth = (2 * links + 1) * length
    noise = noise_var.reshape(1, here)
    vmem, smem = pl.BlockSpec(memory_space=pltpu.VMEM), pl.BlockSpec(memory_space=pltpu.SMEM)
    whole = jax.ShapeDtypeStruct((rows, here), F32)
    part = jax.ShapeDtypeStruct((rows, span), F32)
    halves = pltpu.VMEM((2 * rows, here + 2 * span), BF16)
    table = jax.ShapeDtypeStruct((blocks, depth, length), BF16)

    packed = jax.ShapeDtypeStruct((rows + 8, span), F32)
    to_left, to_right = call(pack_kernel, "pack", (packed, packed), [vmem, vmem, smem, vmem])(
        coords, noise, pair_list, probes
    )
    low, high = shifted(to_right, 1), shifted(to_left, -1)
    k_high, k_low, second, to_left, to_right = call(
        functools.partial(first_kernel, strip=32),
        "first",
        (table, table, whole, part, part),
        [vmem, vmem, smem, vmem, vmem, vmem],
        [halves, pltpu.VMEM((3, here + 2 * span, 128), F32)],
    )(coords, noise, pair_list, probes, low, high)
    low, high = shifted(to_right, 1), shifted(to_left, -1)
    third, to_left, to_right = call(next_kernel, "next", (whole, part, part), None, [halves])(
        noise, second, low, high, k_high, k_low
    )
    low, high = shifted(to_right, 1), shifted(to_left, -1)
    regions, subs = lax.axis_size("region"), lax.axis_size("sub")
    fourth, sums = call(
        last_kernel, "last", (whole, jax.ShapeDtypeStruct((regions, 4, 128), F32)), None, [halves]
    )(noise, probes, second, third, low, high, k_high, k_low)
    sums = jnp.sum(lax.all_to_all(sums, "region", 0, 0), axis=0)
    sums = lax.all_to_all(jnp.broadcast_to(sums[None], (subs, 4, 128)), "sub", 0, 0)
    coefficients, good = call(
        small_kernel, "small", (jax.ShapeDtypeStruct((rows, 128), F32), jax.ShapeDtypeStruct((1, 1), F32))
    )(sums)

    def combine(coords, noise_var, pair_list, probes, second, third, fourth, coefficients):
        return tuple(call(combine_kernel, "combine", (whole, whole))(coefficients, probes, second, third, fourth))

    def loop(coords, noise_var, pair_list, probes, second, third, fourth, coefficients):
        return plain(coords, noise_var, pair_list, probes)

    return lax.cond(
        good[0, 0] > 0, combine, loop, coords, noise_var, pair_list, probes, second, third, fourth, coefficients
    )


def solution(mesh):
    in_specs = (P(None, AXES), P(AXES), P(None, AXES), P(None, AXES))
    out_specs = (P(None, AXES), P(None, AXES))
    return jax.shard_map(per_device, mesh=mesh, in_specs=in_specs, out_specs=out_specs, check_vma=False)
```

time: 583 us -> 99.2 us (0.17)
  blocking collectives: 495 us -> 24.5 us
  matrix products: 43 us -> 0 us
  Pallas kernels: 0 us -> 16.9 us
  starting transfers between devices: 22.2 us -> 34.7 us
    psum x5 -> x0, blocking collectives: 495 us -> none  [the longest x3 294 us: squares(): return lax.psum(jnp.sum(residual * residual, axis=1), ('region', 'sub'))]
    dot_general x21 -> x0, matrix products: 43 us -> none  [the longest x12 25.8 us: per_device(): jnp.einsum('pbj,bij->pbi', ext_v[:, offset:offset + blocks_here], kernel_...]
    all_to_all x0 -> x1, blocking collectives: none -> 24.5 us  [per_device(): sums = jnp.sum(lax.all_to_all(sums, 'region', 0, 0), axis=0)]
    pallas_call x0 -> x6, Pallas kernels: none -> 16.9 us  [the longest x1 10.9 us: per_device(): call(functools.partial(first_kernel, strip=32), 'first', (table, table, w...]
    all_to_all x0 -> x1, starting transfers between devices: none -> 15.9 us  [per_device(): lax.all_to_all(jnp.broadcast_to(sums[None], (subs, 4, 128)), 'sub', 0, 0)]
    all_to_all x0 -> x1, waiting for transfers between devices: none -> 7.39 us  [per_device(): lax.all_to_all(jnp.broadcast_to(sums[None], (subs, 4, 128)), 'sub', 0, 0)]
    ppermute x7 -> x6, starting transfers between devices: 22.2 us -> 18.8 us  [shifted(): return lax.ppermute(array, AXES, pairs)]
    ppermute x7 -> x6, waiting for transfers between devices: 13.9 us -> 10.9 us  [shifted(): return lax.ppermute(array, AXES, pairs)]
  transfers between devices with their start and end apart: 7 -> 7, of which waited for: 6 -> 6; matrix products, arithmetic and copies ran while one was open for 1% -> 0% of each run, Pallas kernels for 0% -> 0%
where the time goes in v1:
time: 99.2 us; the launch traced here: 98.6 us
  starting transfers between devices  34.7 us (35%)
  blocking collectives  24.5 us (25%)
  waiting for transfers between devices  18.3 us (18%)
  Pallas kernels  16.9 us (17%)
  local copies, waits for them, and re-layouts  2.54 us (3%)
  between operations  1.39 us (1%)
    all_to_all x1, blocking collectives, per_device(): sums = jnp.sum(lax.all_to_all(sums, 'region', 0, 0), axis=0)  24.5 us
    ppermute x6, starting transfers between devices, shifted(): return lax.ppermute(array, AXES, pairs)  18.8 us
    all_to_all x1, starting transfers between devices, per_device(): lax.all_to_all(jnp.broadcast_to(sums[None], (subs, 4, 128)), 'sub', 0, 0)  15.9 us
    ppermute x6, waiting for transfers between devices, shifted(): return lax.ppermute(array, AXES, pairs)  10.9 us
    pallas_call x1, Pallas kernels, per_device(): call(functools.partial(first_kernel, strip=32), 'first', (table, table, w...  10.9 us
    all_to_all x1, waiting for transfers between devices, per_device(): lax.all_to_all(jnp.broadcast_to(sums[None], (subs, 4, 128)), 'sub', 0, 0)  7.39 us
    pallas_call x1, Pallas kernels, per_device(): call(next_kernel, 'next', (whole, part, part), None, [halves])  2.05 us
  transfers between devices with their start and end apart: 7, of which 6 were waited for; matrix products, arithmetic and copies ran while one was open for 0% of the time, Pallas kernels for 0%

profile of v1, /device:TPU:1, one launch (start us, length us, event | category | flops | bytes accessed | tf_op | source)
XLA Modules:
  0.0 98.6 jit_solution(14212303554751001338)
XLA Ops:
  0.6 1.0 copy.75.probes.first
  1.6 0.0 copy-start
  1.6 0.9 pack.1
  2.4 4.6 %collective-permute-start.3 = (f32[72,768]{1,0:T(8,128)S(1)}, f32[72,768]{1,0:T(8,128)S(1)}, u32[]{:S(2)}, u32[]{:S(2)}) collective-permute-start(f32[72,768]{1,0:T(8,128)S(1)} %get-tuple-element.242), channel_id=1, source_target_pairs={{0,1},{1,2},{2,3},{3,4},{4,5},{5,6},{6,7},{7,8},{8,9},{9,10},{10,1... | collective-permute-start | bytes 663560 | tf_op jit(solution)/shard_map/ppermute | solution.py:23
  7.0 5.5 %collective-permute-start.4 = (f32[72,768]{1,0:T(8,128)S(1)}, f32[72,768]{1,0:T(8,128)S(1)}, u32[]{:S(2)}, u32[]{:S(2)}) collective-permute-start(f32[72,768]{1,0:T(8,128)S(1)} %get-tuple-element.243), channel_id=1, source_target_pairs={{1,0},{2,1},{3,2},{4,3},{5,4},{6,5},{7,6},{8,7},{9,8},{10,9},{11,1... | collective-permute-start | bytes 663560 | tf_op jit(solution)/shard_map/ppermute | solution.py:23
  12.5 0.0 collective-permute-done.3.low
  12.6 1.7 %collective-permute-done.4.high = f32[72,768]{1,0:T(8,128)S(1)} collective-permute-done((f32[72,768]{1,0:T(8,128)S(1)}, f32[72,768]{1,0:T(8,128)S(1)}, u32[]{:S(2)}, u32[]{:S(2)}) %collective-permute-start.4) | collective-permute-done | bytes 221216 | tf_op jit(solution)/shard_map/ppermute | solution.py:23
  14.3 10.9 %first.2 = (bf16[4,1792,256]{2,1,0:T(8,128)(2,1)S(1)}, bf16[4,1792,256]{2,1,0:T(8,128)(2,1)S(1)}, f32[64,1024]{1,0:T(8,128)S(1)}, f32[64,768]{1,0:T(8,128)S(1)}, f32[64,768]{1,0:T(8,128)S(1)}) custom-call(f32[3,1024]{1,0:T(4,128)} %coords.3, f32[1,1024]{1,0:T(1,128)} %bitcast.98, s32[3,4]{1,0:T(4,128)} %pair.3, f32[64,1024]{1,0:T(8,128)S(1)} %copy.75.probes.first, ...), custom_call_target="tpu_custom_call" | custom-call | tf_op jit(solution)/shard_map/first/pallas_call | solution.py:303
  25.2 1.9 %collective-permute-start.5 = (f32[64,768]{1,0:T(8,128)S(1)}, f32[64,768]{1,0:T(8,128)S(1)}, u32[]{:S(2)}, u32[]{:S(2)}) collective-permute-start(f32[64,768]{1,0:T(8,128)S(1)} %get-tuple-element.245), channel_id=1, source_target_pairs={{0,1},{1,2},{2,3},{3,4},{4,5},{5,6},{6,7},{7,8},{8,9},{9,10},{10,1... | collective-permute-start | bytes 589832 | tf_op jit(solution)/shard_map/ppermute | solution.py:23
  27.1 2.4 %collective-permute-start.6 = (f32[64,768]{1,0:T(8,128)S(1)}, f32[64,768]{1,0:T(8,128)S(1)}, u32[]{:S(2)}, u32[]{:S(2)}) collective-permute-start(f32[64,768]{1,0:T(8,128)S(1)} %get-tuple-element.246), channel_id=1, source_target_pairs={{1,0},{2,1},{3,2},{4,3},{5,4},{6,5},{7,6},{8,7},{9,8},{10,9},{11,1... | collective-permute-start | bytes 589832 | tf_op jit(solution)/shard_map/ppermute | solution.py:23
  29.5 0.2 collective-permute-done.5.low
  29.7 4.4 %collective-permute-done.6.high = f32[64,768]{1,0:T(8,128)S(1)} collective-permute-done((f32[64,768]{1,0:T(8,128)S(1)}, f32[64,768]{1,0:T(8,128)S(1)}, u32[]{:S(2)}, u32[]{:S(2)}) %collective-permute-start.6) | collective-permute-done | bytes 196640 | tf_op jit(solution)/shard_map/ppermute | solution.py:23
  34.1 0.0 copy-start.4
  34.1 2.0 %next.1 = (f32[64,1024]{1,0:T(8,128)S(1)}, f32[64,768]{1,0:T(8,128)S(1)}, f32[64,768]{1,0:T(8,128)S(1)}) custom-call(f32[1,1024]{1,0:T(1,128)} %bitcast.99, f32[64,1024]{1,0:T(8,128)S(1)} %get-tuple-element.244.vector.second, f32[64,768]{1,0:T(8,128)S(1)} %collective-permute-done.5.low, f32[64,768]{1,0:T(8,128)S(1)} %collective-permute-done.6.high, ...), custom_call_target="tpu_custom_call" | custom-call | tf_op jit(solution)/shard_map/next/pallas_call | solution.py:311
  36.1 1.9 %collective-permute-start.7 = (f32[64,768]{1,0:T(8,128)S(1)}, f32[64,768]{1,0:T(8,128)S(1)}, u32[]{:S(2)}, u32[]{:S(2)}) collective-permute-start(f32[64,768]{1,0:T(8,128)S(1)} %get-tuple-element.250), channel_id=1, source_target_pairs={{0,1},{1,2},{2,3},{3,4},{4,5},{5,6},{6,7},{7,8},{8,9},{9,10},{10,1... | collective-permute-start | bytes 589832 | tf_op jit(solution)/shard_map/ppermute | solution.py:23
  38.1 2.4 %collective-permute-start.8 = (f32[64,768]{1,0:T(8,128)S(1)}, f32[64,768]{1,0:T(8,128)S(1)}, u32[]{:S(2)}, u32[]{:S(2)}) collective-permute-start(f32[64,768]{1,0:T(8,128)S(1)} %get-tuple-element.251), channel_id=1, source_target_pairs={{1,0},{2,1},{3,2},{4,3},{5,4},{6,5},{7,6},{8,7},{9,8},{10,9},{11,1... | collective-permute-start | bytes 589832 | tf_op jit(solution)/shard_map/ppermute | solution.py:23
  40.5 0.2 collective-permute-done.7.low
  40.7 4.4 %collective-permute-done.8.high = f32[64,768]{1,0:T(8,128)S(1)} collective-permute-done((f32[64,768]{1,0:T(8,128)S(1)}, f32[64,768]{1,0:T(8,128)S(1)}, u32[]{:S(2)}, u32[]{:S(2)}) %collective-permute-start.8) | collective-permute-done | bytes 196640 | tf_op jit(solution)/shard_map/ppermute | solution.py:23
  45.0 0.0 copy-done.4
  45.0 0.0 copy-start.5
  45.1 0.0 copy-start.6
  45.1 1.5 %last.1 = (f32[64,1024]{1,0:T(8,128)S(1)}, f32[32,4,128]{2,1,0:T(4,128)S(1)}) custom-call(f32[1,1024]{1,0:T(1,128)S(1)} %bitcast.100, f32[64,1024]{1,0:T(8,128)S(1)} %copy.75.probes.first, f32[64,1024]{1,0:T(8,128)S(1)} %get-tuple-element.244.vector.second, f32[64,1024]{1,0:T(8,128)S(1)} %get-tuple-element.249.vector, ...), custom_call_target="tpu_custom_call" | custom-call | tf_op jit(solution)/shard_map/last/pallas_call | solution.py:316
  46.6 24.5 %all_to_all.10 = f32[32,4,128]{2,1,0:T(4,128)S(1)} all-to-all(f32[32,4,128]{2,1,0:T(4,128)S(1)} %get-tuple-element.252), channel_id=1, replica_groups=mesh['region'=32,'sub'=16] {'region'}, dimensions={0} | all-to-all | bytes 131072 | tf_op jit(solution)/shard_map/all_to_all | solution.py:319
  71.1 0.6 broadcast_in_dim.2
  71.7 15.9 %all-to-all-start.1 = ((f32[16,4,128]{2,1,0:T(4,128)}), f32[16,4,128]{2,1,0:T(4,128)S(1)}, u32[]{:S(2)}, u32[]{:S(2)}) async-start(f32[16,4,128]{2,1,0:T(4,128)} %broadcast_in_dim.2), calls=%async_computation.1 | async-start | bytes 65536 | tf_op jit(solution)/shard_map/all_to_all | solution.py:320
  87.7 7.4 %all-to-all-done.1.sums = f32[16,4,128]{2,1,0:T(4,128)S(1)} async-done(((f32[16,4,128]{2,1,0:T(4,128)}), f32[16,4,128]{2,1,0:T(4,128)S(1)}, u32[]{:S(2)}, u32[]{:S(2)}) %all-to-all-start.1) | async-done | bytes 32800 | tf_op jit(solution)/shard_map/all_to_all | solution.py:320
  95.1 0.7 small.1
  96.5 0.0 copy-done
  96.5 0.0 copy-done.5
  96.5 0.0 copy-done.6
  96.5 2.1 %conditional.1 = ((f32[64,1024]{1,0:T(8,128)}, f32[64,1024]{1,0:T(8,128)})) conditional(s32[]{:T(128)} %bitcast.1, (f32[64,1024]{1,0:T(8,128)}, f32[3,1024]{1,0:T(4,128)S(1)}, s32[3,4]{1,0:T(4,128)S(1)}, f32[1024]{0:T(1024)S(1)}) %tuple.101, (f32[64,128]{1,0:T(8,128)S(1)}, f32[64,1024]{1,0:T(8,128)}, f32[64,1024]{1,0:T(8,128)S(1)}, ...), branch_computations={%region_1.10_spmd, %region_10.11_spmd} | conditional | flops 1439929600 | bytes 21655772 | solution.py:331
  96.7 1.0 copy.74.first
  97.7 0.9 combine.1
  (1 shorter events, 0.0 us)
Async XLA Ops:
  1.6 94.9 %copy-start = (f32[64,1024]{1,0:T(8,128)}, f32[64,1024]{1,0:T(8,128)S(1)}, u32[]{:S(2)}) copy-start(f32[64,1024]{1,0:T(8,128)S(1)} %copy.75.probes.first) | copy-start | bytes 786436
  2.4 10.1 %collective-permute-start.3 = (f32[72,768]{1,0:T(8,128)S(1)}, f32[72,768]{1,0:T(8,128)S(1)}, u32[]{:S(2)}, u32[]{:S(2)}) collective-permute-start(f32[72,768]{1,0:T(8,128)S(1)} %get-tuple-element.242), channel_id=1, source_target_pairs={{0,1},{1,2},{2,3},{3,4},{4,5},{5,6},{6,7},{7,8},{8,9},{9,10},{10,1... | collective-permute-start | bytes 663560 | tf_op jit(solution)/shard_map/ppermute | solution.py:23
  7.0 7.3 %collective-permute-start.4 = (f32[72,768]{1,0:T(8,128)S(1)}, f32[72,768]{1,0:T(8,128)S(1)}, u32[]{:S(2)}, u32[]{:S(2)}) collective-permute-start(f32[72,768]{1,0:T(8,128)S(1)} %get-tuple-element.243), channel_id=1, source_target_pairs={{1,0},{2,1},{3,2},{4,3},{5,4},{6,5},{7,6},{8,7},{9,8},{10,9},{11,1... | collective-permute-start | bytes 663560 | tf_op jit(solution)/shard_map/ppermute | solution.py:23
  25.2 4.5 %collective-permute-start.5 = (f32[64,768]{1,0:T(8,128)S(1)}, f32[64,768]{1,0:T(8,128)S(1)}, u32[]{:S(2)}, u32[]{:S(2)}) collective-permute-start(f32[64,768]{1,0:T(8,128)S(1)} %get-tuple-element.245), channel_id=1, source_target_pairs={{0,1},{1,2},{2,3},{3,4},{4,5},{5,6},{6,7},{7,8},{8,9},{9,10},{10,1... | collective-permute-start | bytes 589832 | tf_op jit(solution)/shard_map/ppermute | solution.py:23
  27.1 7.0 %collective-permute-start.6 = (f32[64,768]{1,0:T(8,128)S(1)}, f32[64,768]{1,0:T(8,128)S(1)}, u32[]{:S(2)}, u32[]{:S(2)}) collective-permute-start(f32[64,768]{1,0:T(8,128)S(1)} %get-tuple-element.246), channel_id=1, source_target_pairs={{1,0},{2,1},{3,2},{4,3},{5,4},{6,5},{7,6},{8,7},{9,8},{10,9},{11,1... | collective-permute-start | bytes 589832 | tf_op jit(solution)/shard_map/ppermute | solution.py:23
  34.1 11.0 %copy-start.4 = (f32[1024]{0:T(1024)S(1)}, f32[1024]{0:T(1024)}, u32[]{:S(2)}) copy-start(f32[1024]{0:T(1024)} %param.17) | copy-start | bytes 12292
  36.1 4.5 %collective-permute-start.7 = (f32[64,768]{1,0:T(8,128)S(1)}, f32[64,768]{1,0:T(8,128)S(1)}, u32[]{:S(2)}, u32[]{:S(2)}) collective-permute-start(f32[64,768]{1,0:T(8,128)S(1)} %get-tuple-element.250), channel_id=1, source_target_pairs={{0,1},{1,2},{2,3},{3,4},{4,5},{5,6},{6,7},{7,8},{8,9},{9,10},{10,1... | collective-permute-start | bytes 589832 | tf_op jit(solution)/shard_map/ppermute | solution.py:23
  38.1 7.0 %collective-permute-start.8 = (f32[64,768]{1,0:T(8,128)S(1)}, f32[64,768]{1,0:T(8,128)S(1)}, u32[]{:S(2)}, u32[]{:S(2)}) collective-permute-start(f32[64,768]{1,0:T(8,128)S(1)} %get-tuple-element.251), channel_id=1, source_target_pairs={{1,0},{2,1},{3,2},{4,3},{5,4},{6,5},{7,6},{8,7},{9,8},{10,9},{11,1... | collective-permute-start | bytes 589832 | tf_op jit(solution)/shard_map/ppermute | solution.py:23
  45.0 51.4 %copy-start.5 = (f32[3,1024]{1,0:T(4,128)S(1)}, f32[3,1024]{1,0:T(4,128)}, u32[]{:S(2)}) copy-start(f32[3,1024]{1,0:T(4,128)} %coords.3) | copy-start | bytes 36868
  45.1 51.4 %copy-start.6 = (s32[3,4]{1,0:T(4,128)S(1)}, s32[3,4]{1,0:T(4,128)}, u32[]{:S(2)}) copy-start(s32[3,4]{1,0:T(4,128)} %pair.3) | copy-start | bytes 148
  71.7 23.3 %all-to-all-start.1 = ((f32[16,4,128]{2,1,0:T(4,128)}), f32[16,4,128]{2,1,0:T(4,128)S(1)}, u32[]{:S(2)}, u32[]{:S(2)}) async-start(f32[16,4,128]{2,1,0:T(4,128)} %broadcast_in_dim.2), calls=%async_computation.1 | async-start | bytes 65536 | tf_op jit(solution)/shard_map/all_to_all | solution.py:320

commit v2 on v1

v2 whole, which is shorter than its diff:
```python
import functools

import jax
import jax.numpy as jnp
from jax import lax
from jax.experimental import pallas as pl
from jax.experimental.pallas import tpu as pltpu
from jax.sharding import PartitionSpec as P

ITERS = 3
AXES = ("region", "sub")
SHIFT = 6.0
MAX_AMP = 100.0
MAX_NORM = 30.0
STRIP = 32
PACKS = 4
F32 = jnp.float32
BF16 = jnp.bfloat16
VMEM_LIMIT = 40 * 1024 * 1024


def shifted(array, by):
    count = lax.axis_size(AXES)
    pairs = [(i, i + by) for i in range(count) if 0 <= i + by < count]
    return lax.ppermute(array, AXES, pairs)


def wendland(left, right):
    squared = (left[0][..., :, None] - right[0][..., None, :]) ** 2
    squared = squared + (left[1][..., :, None] - right[1][..., None, :]) ** 2
    squared = squared + (left[2][..., :, None] - right[2][..., None, :]) ** 2
    distance = jnp.sqrt(squared)
    support = jnp.maximum(1.0 - distance, 0.0)
    return support**4 * (4.0 * distance + 1.0)


def squares(residual):
    return lax.psum(jnp.sum(residual * residual, axis=1), AXES)


def plain(coords, noise_var, pair_list, probes):
    probe_count, points_here = probes.shape
    links = pair_list.shape[0]
    blocks_here = pair_list.shape[1]
    block_len = points_here // blocks_here
    span_cols = links * block_len
    local_c = coords.reshape(3, blocks_here, block_len)
    weights = pair_list.astype(F32)
    ahead_c = shifted(coords[:, :span_cols], -1)
    ext_c = jnp.concatenate([local_c, ahead_c.reshape(3, links, block_len)], axis=1)

    def step(_, state):
        solution, residual, direction, res_norm = state
        ahead_v = shifted(direction[:, :span_cols], -1)
        ext_v = jnp.concatenate([direction, ahead_v], axis=1).reshape(probe_count, blocks_here + links, block_len)
        local_v = ext_v[:, :blocks_here]
        result = (noise_var[None, :] * direction).reshape(probe_count, blocks_here, block_len)
        spill = jnp.zeros((probe_count, blocks_here + links, block_len), F32)
        for offset in range(links + 1):
            kernel_block = wendland(local_c, ext_c[:, offset : offset + blocks_here])
            if offset > 0:
                kernel_block = kernel_block * weights[offset - 1][:, None, None]
            result = result + jnp.einsum(
                "pbj,bij->pbi", ext_v[:, offset : offset + blocks_here], kernel_block, precision=lax.Precision.HIGHEST
            )
            if offset > 0:
                spill = spill.at[:, offset : offset + blocks_here].add(
                    jnp.einsum("pbi,bij->pbj", local_v, kernel_block, precision=lax.Precision.HIGHEST)
                )
        result = result + spill[:, :blocks_here]
        result = result.at[:, :links].add(shifted(spill[:, blocks_here:], 1))
        product = result.reshape(probe_count, points_here)
        step_size = res_norm / lax.psum(jnp.sum(direction * product, axis=1), AXES)
        solution = solution + step_size[:, None] * direction
        residual = residual - step_size[:, None] * product
        next_norm = squares(residual)
        direction = residual + (next_norm / res_norm)[:, None] * direction
        return solution, residual, direction, next_norm

    state = (jnp.zeros_like(probes), probes, probes, squares(probes))
    solution, residual, _, _ = lax.fori_loop(0, ITERS, step, state)
    return solution, residual


def split(value):
    high = value.astype(BF16)
    return high, (value - high.astype(F32)).astype(BF16)


def pack_kernel(odd, coords, pair, probes, to_mate, to_next, sem):
    links, blocks = pair.shape
    length = coords.shape[1] // blocks
    span = links * length
    rows = probes.shape[0]
    far = (blocks - links) * length
    is_odd = odd[0] == 1
    copies = []
    for slot, (out, start) in enumerate(
        ((to_next, jnp.where(is_odd, far, 0)), (to_mate, jnp.where(is_odd, 0, far)))
    ):
        at = pl.ds(pl.multiple_of(start, 128), span)
        for n in range(PACKS):
            share = pl.ds(n * (rows // PACKS), rows // PACKS)
            copies.append(pltpu.make_async_copy(probes.at[share, at], out.at[share], sem.at[slot * PACKS + n]))
            copies[-1].start()
    flags = []
    for k in range(links):
        flags.append(
            jnp.concatenate([jnp.full((1, length), pair[k, b].astype(F32), F32) for b in range(blocks)], axis=1)
        )
    extra = jnp.concatenate([coords[...]] + flags + [jnp.zeros((8 - 3 - links, blocks * length), F32)], axis=0)
    first, last = extra[:, 0:span], extra[:, far:]
    to_next[rows : rows + 8, :] = jnp.where(is_odd, last, first)
    to_mate[rows : rows + 8, :] = jnp.where(is_odd, first, last)
    for copy in copies:
        copy.wait()


def fill_columns(columns, at, block):
    turned = jnp.transpose(block)
    for d in range(3):
        columns[d, at : at + turned.shape[0], :] = jnp.broadcast_to(turned[:, d : d + 1], (turned.shape[0], 128))


def fill_rows(rows, coords):
    for d in range(3):
        rows[d] = jnp.broadcast_to(coords[d : d + 1, :], rows.shape[1:])


def fill_strip(columns, from_row, strip, rows, lanes, flag, stores):
    column = [columns[d, pl.ds(from_row, strip), :].reshape(strip // 8, 8, 128) for d in range(3)]
    for lane, one_flag, store in zip(lanes, flag, stores):
        squared = None
        for d in range(3):
            away = column[d] - rows[d, :, pl.ds(lane, 128)][None]
            squared = away * away if squared is None else squared + away * away
        squared = jnp.maximum(squared, 1e-30)
        distance = squared * lax.rsqrt(squared)
        support = jnp.maximum(1.0 - distance, 0.0)
        support = support * support
        value = support * support * ((4.0 * one_flag)[None] * distance + one_flag[None])
        store(*split(value.reshape(strip, 128)))


def store_halves(halves, at, vector):
    rows, size = vector.shape
    top, rest = split(vector)
    halves[0:rows, at : at + size] = top
    halves[rows : 2 * rows, at : at + size] = rest


def multiply(halves, rows, depth, k_high, k_low):
    both = jnp.dot(halves[:, 0:depth], k_high, preferred_element_type=F32)
    rest = jnp.dot(halves[0:rows, 0:depth], k_low, preferred_element_type=F32)
    return both[0:rows] + (both[rows : 2 * rows] + rest)


def local_product(noise, vector, k_high, k_low, out, halves):
    rows, here = vector.shape
    blocks, _, length = k_high.shape
    store_halves(halves, 0, vector[...])
    for i in range(blocks):
        at = slice(i * length, (i + 1) * length)
        value = multiply(halves, rows, here, k_high[i], k_low[i])
        out[:, at] = value + (noise[:, at] - SHIFT) * vector[:, at]


def local_first_kernel(coords, noise, pair, probes, k_high, k_low, out, first, halves, columns, rows, flags):
    links, blocks = pair.shape
    here = probes.shape[1]
    length = here // blocks
    for j in range(blocks):
        own = coords[:, j * length : (j + 1) * length]
        fill_columns(columns, j * length, jnp.concatenate([own, jnp.zeros((5, length), F32)], axis=0))
    fill_rows(rows, coords)
    for j in range(blocks):
        for i in range(blocks):
            if i == j:
                flag = 1.0
            elif abs(i - j) <= links:
                flag = pair[abs(i - j) - 1, min(i, j)].astype(F32)
            else:
                flag = 0.0
            flags[j, :, i * length : (i + 1) * length] = jnp.full((8, length), flag, F32)

    def store_to(i, row, lane):
        def store(top, rest):
            k_high[i, pl.ds(row, STRIP), lane : lane + 128] = top
            k_low[i, pl.ds(row, STRIP), lane : lane + 128] = rest

        return store

    def body(s, _):
        row = pl.multiple_of(s * STRIP, STRIP)
        block = s // (length // STRIP)
        lanes = list(range(0, here, 128))
        fill_strip(
            columns,
            row,
            STRIP,
            rows,
            lanes,
            [flags[block, :, pl.ds(lane, 128)] for lane in lanes],
            [store_to(lane // length, row, lane % length) for lane in lanes],
        )
        return 0

    lax.fori_loop(0, here // STRIP, body, 0)
    local_product(noise, probes, k_high, k_low, out, halves)
    first[...] = probes[...]


def halo_place(right, blocks, links, length, n):
    own = jnp.where(right, blocks - 1 - links + n, links - n) * length
    halo = jnp.where(right, n, links - 1 - n) * length
    return pl.multiple_of(own, 128), pl.multiple_of(halo, 128)


def halo_product(right, received, k_high, k_low, out, halves, blocks, length):
    rows = out.shape[0]
    links = received.shape[1] // length
    for n in range(links):
        _, halo = halo_place(right, blocks, links, length, n)
        store_halves(halves, n * length, received[0:rows, pl.ds(halo, length)])
    row = 0
    for n in range(1, links + 1):
        depth = n * length
        own, _ = halo_place(right, blocks, links, length, n)
        value = multiply(halves, rows, depth, k_high[row : row + depth], k_low[row : row + depth])
        out[:, pl.ds(own, length)] = out[:, pl.ds(own, length)] + value
        row += depth


def store_sends(is_odd, out, to_mate, to_next):
    span = to_mate.shape[1]
    far = out.shape[1] - span
    to_mate[...] = out[:, pl.ds(pl.multiple_of(jnp.where(is_odd, 0, far), 128), span)]
    to_next[...] = out[:, pl.ds(pl.multiple_of(jnp.where(is_odd, far, 0), 128), span)]


def halo_first_kernel(odd, coords, pair, partial, received, k_high, k_low, out, *rest, mate):
    *sends, halves, columns, rows = rest
    links, blocks = pair.shape
    probe_count, here = out.shape
    length = here // blocks
    right = odd[0] == (0 if mate else 1)
    out[...] = partial[...]
    fill_rows(rows, coords)
    for h in range(links):
        _, halo = halo_place(right, blocks, links, length, h)
        fill_columns(columns, h * length, received[probe_count : probe_count + 8, pl.ds(halo, length)])
        lanes, flags, starts = [], [], []
        for n in range(h + 1, links + 1):
            own, _ = halo_place(right, blocks, links, length, n)
            lower = jnp.where(right, blocks - 1 - links + n, 0)
            k = links - n + h
            ours = jnp.full((1, 128), pair[k, lower].astype(F32), F32)
            theirs = received[probe_count + 3 + k : probe_count + 4 + k, pl.ds(halo, 128)]
            flag = jnp.broadcast_to(jnp.where(right, ours, theirs), (8, 128))
            for lane in range(0, length, 128):
                lanes.append(pl.multiple_of(own + lane, 128))
                flags.append(flag)
                starts.append(((n * (n - 1) // 2 + h) * length, lane))

        def store_to(start, lane, row):
            def store(top, rest):
                k_high[pl.ds(start + row, STRIP), lane : lane + 128] = top
                k_low[pl.ds(start + row, STRIP), lane : lane + 128] = rest

            return store

        def body(s, _):
            row = pl.multiple_of(s * STRIP, STRIP)
            stores = [store_to(start, lane, row) for start, lane in starts]
            fill_strip(columns, h * length + row, STRIP, rows, lanes, flags, stores)
            return 0

        lax.fori_loop(0, length // STRIP, body, 0)
    halo_product(right, received, k_high, k_low, out, halves, blocks, length)
    if sends:
        store_sends(odd[0] == 1, out, *sends)


def add_sums(table, terms):
    lane = lax.broadcasted_iota(jnp.int32, table.shape, 1)
    for power, left, right in terms:
        part = None
        for at in range(0, left.shape[1], 128):
            term = left[:, at : at + 128] * right[:, at : at + 128]
            part = term if part is None else part + term
        table = jnp.where(lane == power, jnp.sum(part, axis=1, keepdims=True), table)
    return table


def local_second_kernel(noise, first, second, k_high, k_low, out, table, halves):
    local_product(noise, second, k_high, k_low, out, halves)
    table[...] = add_sums(jnp.zeros(table.shape, F32), ((0, first, first), (1, first, second), (2, second, second)))


def local_third_kernel(noise, second, third, table_in, k_high, k_low, out, table, halves):
    local_product(noise, third, k_high, k_low, out, halves)
    table[...] = add_sums(table_in[...], ((3, second, third), (4, third, third)))


def halo_second_kernel(odd, partial, beyond, mate, mate_high, mate_low, next_high, next_low, out, to_mate, to_next, halves):
    out[...] = partial[...]
    links = mate.shape[1] // mate_high.shape[1]
    length = mate_high.shape[1]
    blocks = out.shape[1] // length
    halo_product(odd[0] == 0, mate, mate_high, mate_low, out, halves, blocks, length)
    halo_product(odd[0] == 1, beyond, next_high, next_low, out, halves, blocks, length)
    store_sends(odd[0] == 1, out, to_mate, to_next)


def halo_third_kernel(
    odd, partial, beyond, mate, mate_high, mate_low, next_high, next_low, third, table, out, sums, halves
):
    out[...] = partial[...]
    length = mate_high.shape[1]
    blocks = out.shape[1] // length
    halo_product(odd[0] == 0, mate, mate_high, mate_low, out, halves, blocks, length)
    halo_product(odd[0] == 1, beyond, next_high, next_low, out, halves, blocks, length)
    full = add_sums(table[...], ((5, third, out), (6, out, out)))
    turned = jnp.transpose(full)[0:8, :]
    compact = jnp.concatenate([turned[0:4], turned[4:8]], axis=1)
    sums[...] = jnp.broadcast_to(compact[None], sums.shape)


def polynomials(moment):
    def dot(p, q):
        total, size = 0.0, 0.0
        for i, x in enumerate(p):
            for j, y in enumerate(q):
                term = x * y * moment[i + j]
                total, size = total + term, size + jnp.abs(term)
        return total, size

    def add(p, q, factor):
        count = max(len(p), len(q))
        p, q = p + [0.0] * (count - len(p)), q + [0.0] * (count - len(q))
        return [x + factor * y for x, y in zip(p, q)]

    one = jnp.ones_like(moment[0])
    solution, residual, direction = [jnp.zeros_like(one)], [one], [one]
    norm = moment[0]
    good = norm > 0.0
    for step in range(ITERS):
        image = add([0.0 * one] + direction, direction, SHIFT)
        curvature, size = dot(direction, image)
        good = good & (size <= MAX_AMP * curvature)
        step_size = norm / curvature
        solution = add(solution, direction, step_size)
        residual = add(residual, image, -step_size)
        new, size = dot(residual, residual)
        if step < ITERS - 1:
            good = good & (size <= MAX_AMP * new)
            direction = add(residual, direction, new / norm)
        norm = new
    size = sum(jnp.abs(x) * jnp.sqrt(moment[2 * i]) for i, x in enumerate(residual))
    good = good & (size * size <= MAX_NORM * MAX_NORM * norm)
    return solution, residual, good


def finish_kernel(sums, first, second, third, fourth, solution, residual, good):
    total = jnp.sum(sums[...], axis=0)
    rows = first.shape[0]
    moment = [total[k : k + 1, 0:rows] for k in range(4)] + [total[k : k + 1, rows : 2 * rows] for k in range(3)]
    mix_solution, mix_residual, fine = polynomials(moment)
    table = jnp.concatenate(mix_solution + mix_residual + [jnp.zeros_like(moment[0])], axis=0)
    table = jnp.concatenate([table, jnp.zeros_like(table)], axis=1)
    table = jnp.transpose(jnp.concatenate([table, jnp.zeros((120, 128), F32)], axis=0))[0:rows]
    basis = (first[...], second[...], third[...], fourth[...])

    def mix(at, count):
        total = table[:, at : at + 1] * basis[0]
        for k in range(1, count):
            total = total + table[:, at + k : at + k + 1] * basis[k]
        return total

    solution[...] = mix(0, ITERS)
    residual[...] = mix(ITERS, ITERS + 1)
    good[0, 0] = jnp.min(jnp.where(fine, 1.0, 0.0))


VMEM = pl.BlockSpec(memory_space=pltpu.VMEM)
SMEM = pl.BlockSpec(memory_space=pltpu.SMEM)
ANY = pl.BlockSpec(memory_space=pl.ANY)


def call(kernel, name, out_shape, in_specs, scratch_shapes=(), out_specs=None):
    kwargs = {} if out_specs is None else {"out_specs": out_specs}
    return pl.pallas_call(
        kernel,
        out_shape=out_shape,
        in_specs=in_specs,
        scratch_shapes=scratch_shapes,
        compiler_params=pltpu.CompilerParams(vmem_limit_bytes=VMEM_LIMIT),
        name=name,
        **kwargs,
    )


def exchange(to_mate, to_next):
    count = lax.axis_size(AXES)
    beyond = [(i, i + 1 if i % 2 else i - 1) for i in range(1, count - 1)]
    mate = [(i, i ^ 1) for i in range(count)]
    to_mate = lax.ppermute(to_mate, AXES, mate)
    return lax.ppermute(to_next, AXES, beyond), to_mate


def per_device(coords, noise_var, pair_list, probes):
    rows, here = probes.shape
    links, blocks = pair_list.shape
    length = here // blocks
    span = links * length
    tiles = links * (links + 1) // 2
    noise = noise_var.reshape(1, here)
    odd = (lax.axis_index(AXES) % 2).reshape(1)

    whole = jax.ShapeDtypeStruct((rows, here), F32)
    part = jax.ShapeDtypeStruct((rows, span), F32)
    packed = jax.ShapeDtypeStruct((rows + 8, span), F32)
    sums_table = jax.ShapeDtypeStruct((rows, 128), F32)
    local_table = jax.ShapeDtypeStruct((blocks, here, length), BF16)
    halo_table = jax.ShapeDtypeStruct((tiles * length, length), BF16)
    local_halves = pltpu.VMEM((2 * rows, here), BF16)
    halo_halves = pltpu.VMEM((2 * rows, span), BF16)

    to_mate, to_next = call(
        pack_kernel, "pack", (packed, packed), [SMEM, VMEM, SMEM, ANY], [pltpu.SemaphoreType.DMA((2 * PACKS,))]
    )(odd, coords, pair_list, probes)
    beyond, mate = exchange(to_mate, to_next)
    k_high, k_low, partial, first = call(
        local_first_kernel,
        "local_first",
        (local_table, local_table, whole, whole),
        [VMEM, VMEM, SMEM, VMEM],
        [
            local_halves,
            pltpu.VMEM((3, here, 128), F32),
            pltpu.VMEM((3, 8, here), F32),
            pltpu.VMEM((blocks, 8, here), F32),
        ],
    )(coords, noise, pair_list, probes)
    halo_scratch = [halo_halves, pltpu.VMEM((3, span, 128), F32), pltpu.VMEM((3, 8, here), F32)]
    mate_high, mate_low, partial = call(
        functools.partial(halo_first_kernel, mate=True),
        "mate_first",
        (halo_table, halo_table, whole),
        [SMEM, VMEM, SMEM, VMEM, VMEM],
        halo_scratch,
    )(odd, coords, pair_list, partial, mate)
    next_high, next_low, second, to_mate, to_next = call(
        functools.partial(halo_first_kernel, mate=False),
        "next_first",
        (halo_table, halo_table, whole, part, part),
        [SMEM, VMEM, SMEM, VMEM, VMEM],
        halo_scratch,
    )(odd, coords, pair_list, partial, beyond)

    beyond, mate = exchange(to_mate, to_next)
    partial, table = call(local_second_kernel, "local_second", (whole, sums_table), [VMEM] * 5, [local_halves])(
        noise, first, second, k_high, k_low
    )
    third, to_mate, to_next = call(
        halo_second_kernel, "halo_second", (whole, part, part), [SMEM] + [VMEM] * 7, [halo_halves]
    )(odd, partial, beyond, mate, mate_high, mate_low, next_high, next_low)

    beyond, mate = exchange(to_mate, to_next)
    partial, table = call(local_third_kernel, "local_third", (whole, sums_table), [VMEM] * 6, [local_halves])(
        noise, second, third, table, k_high, k_low
    )
    regions, subs = lax.axis_size("region"), lax.axis_size("sub")
    fourth, sums = call(
        halo_third_kernel,
        "halo_third",
        (whole, jax.ShapeDtypeStruct((regions, 4, 128), F32)),
        [SMEM] + [VMEM] * 9,
        [halo_halves],
    )(odd, partial, beyond, mate, mate_high, mate_low, next_high, next_low, third, table)

    sums = jnp.sum(lax.all_to_all(sums, "region", 0, 0), axis=0)
    sums = lax.all_to_all(jnp.broadcast_to(sums[None], (subs, 4, 128)), "sub", 0, 0)
    solution, residual, good = call(
        finish_kernel,
        "finish",
        (whole, whole, jax.ShapeDtypeStruct((1, 1), F32)),
        [VMEM] * 5,
        out_specs=(VMEM, VMEM, SMEM),
    )(sums, first, second, third, fourth)

    def again(state):
        solution, residual = plain(coords, noise_var, pair_list, probes)
        return jnp.ones_like(state[0]), solution, residual

    _, solution, residual = lax.while_loop(lambda state: state[0][0, 0] < 0.5, again, (good, solution, residual))
    return solution, residual


def solution(mesh):
    in_specs = (P(None, AXES), P(AXES), P(None, AXES), P(None, AXES))
    out_specs = (P(None, AXES), P(None, AXES))
    return jax.shard_map(per_device, mesh=mesh, in_specs=in_specs, out_specs=out_specs, check_vma=False)
```

time: 99.2 us -> 85.9 us (0.87)
  waiting for transfers between devices: 18.3 us -> 0.73 us
  blocking collectives: 24.5 us -> 40.6 us
  starting transfers between devices: 34.7 us -> 21.7 us
  Pallas kernels: 16.9 us -> 20.3 us
  local copies, waits for them, and re-layouts: 2.54 us -> 0.03 us
    all_to_all x0 -> x1, blocking collectives: none -> 16.5 us  [per_device(): lax.all_to_all(jnp.broadcast_to(sums[None], (subs, 4, 128)), 'sub', 0, 0)]
    all_to_all x1 -> x0, starting transfers between devices: 15.9 us -> none  [per_device(): lax.all_to_all(jnp.broadcast_to(sums[None], (subs, 4, 128)), 'sub', 0, 0)]
    ppermute x6, waiting for transfers between devices: 10.9 us -> 0.73 us  [the longest x3 0.72 us: exchange(): return (lax.ppermute(to_next, AXES, beyond), to_mate)]
    all_to_all x1 -> x0, waiting for transfers between devices: 7.39 us -> none  [per_device(): lax.all_to_all(jnp.broadcast_to(sums[None], (subs, 4, 128)), 'sub', 0, 0)]
    pallas_call x6 -> x9, Pallas kernels: 16.9 us -> 20.3 us  [the longest x1 5.98 us: per_device(): call(local_first_kernel, 'local_first', (local_table, local_table, whole,...]
    ppermute x6, starting transfers between devices: 18.8 us -> 21.7 us  [the longest x3 12.6 us: exchange(): to_mate = lax.ppermute(to_mate, AXES, mate)]
  transfers between devices with their start and end apart: 7 -> 6, of which waited for: 6 -> 1; matrix products, arithmetic and copies ran while one was open for 0% -> 0% of each run, Pallas kernels for 0% -> 14%
where the time goes in v2:
time: 85.9 us; the launch traced here: 85.1 us
  blocking collectives  40.6 us (47%)
  starting transfers between devices  21.7 us (25%)
  Pallas kernels  20.3 us (24%)
  between operations  0.99 us (1%)
    all_to_all x1, blocking collectives, per_device(): sums = jnp.sum(lax.all_to_all(sums, 'region', 0, 0), axis=0)  24 us
    all_to_all x1, blocking collectives, per_device(): lax.all_to_all(jnp.broadcast_to(sums[None], (subs, 4, 128)), 'sub', 0, 0)  16.5 us
    ppermute x3, starting transfers between devices, exchange(): to_mate = lax.ppermute(to_mate, AXES, mate)  12.6 us
    ppermute x3, starting transfers between devices, exchange(): return (lax.ppermute(to_next, AXES, beyond), to_mate)  9.1 us
    pallas_call x1, Pallas kernels, per_device(): call(local_first_kernel, 'local_first', (local_table, local_table, whole,...  5.98 us
    pallas_call x1, Pallas kernels, per_device(): call(functools.partial(halo_first_kernel, mate=False), 'next_first', (hal...  3.69 us
    pallas_call x1, Pallas kernels, per_device(): call(functools.partial(halo_first_kernel, mate=True), 'mate_first', (halo...  3.67 us
    pallas_call x1, Pallas kernels, per_device(): call(pack_kernel, 'pack', (packed, packed), [SMEM, VMEM, SMEM, ANY], [plt...  1.86 us
  transfers between devices with their start and end apart: 6, of which 1 were waited for; matrix products, arithmetic and copies ran while one was open for 0% of the time, Pallas kernels for 14%

profile of v2, /device:TPU:1, one launch (start us, length us, event | category | flops | bytes accessed | tf_op | source)
XLA Modules:
  0.0 85.1 jit_solution(17438678972440616937)
XLA Ops:
  0.6 1.9 %pack.1 = (f32[72,768]{1,0:T(8,128)S(1)}, f32[72,768]{1,0:T(8,128)S(1)}) custom-call(s32[1]{0:T(128)} %bitcast.1.odd, f32[3,1024]{1,0:T(4,128)} %coords.7, s32[3,4]{1,0:T(4,128)} %pair.7, f32[64,1024]{1,0:T(8,128)} %probes.3), custom_call_target="tpu_custom_call" | custom-call | tf_op jit(solution)/shard_map/pack/pallas_call | solution.py:429
  2.5 8.8 %collective-permute-start.3 = (f32[72,768]{1,0:T(8,128)S(1)}, f32[72,768]{1,0:T(8,128)S(1)}, u32[]{:S(2)}, u32[]{:S(2)}) collective-permute-start(f32[72,768]{1,0:T(8,128)S(1)} %get-tuple-element.306), channel_id=1, source_target_pairs={{0,1},{1,0},{2,3},{3,2},{4,5},{5,4},{6,7},{7,6},{8,9},{9,8},{10,11... | collective-permute-start | bytes 663560 | tf_op jit(solution)/shard_map/ppermute | solution.py:407
  11.3 1.9 %collective-permute-start.4 = (f32[72,768]{1,0:T(8,128)S(1)}, f32[72,768]{1,0:T(8,128)S(1)}, u32[]{:S(2)}, u32[]{:S(2)}) collective-permute-start(f32[72,768]{1,0:T(8,128)S(1)} %get-tuple-element.308), channel_id=1, source_target_pairs={{1,2},{2,1},{3,4},{4,3},{5,6},{6,5},{7,8},{8,7},{9,10},{10,9},{11,... | collective-permute-start | bytes 663560 | tf_op jit(solution)/shard_map/ppermute | solution.py:408
  13.2 6.0 %local_first.1 = (bf16[4,1024,256]{2,1,0:T(8,128)(2,1)S(1)}, bf16[4,1024,256]{2,1,0:T(8,128)(2,1)S(1)}, f32[64,1024]{1,0:T(8,128)S(1)}, f32[64,1024]{1,0:T(8,128)S(1)}) custom-call(f32[3,1024]{1,0:T(4,128)} %coords.7, f32[1,1024]{1,0:T(1,128)} %bitcast.98, s32[3,4]{1,0:T(4,128)} %pair.7, f32[64,1024]{1,0:T(8,128)} %probes.3), custom_call_target="tpu_custom_call" | custom-call | tf_op jit(solution)/shard_map/local_first/pallas_call | solution.py:433
  19.2 0.0 collective-permute-done.3.received
  19.2 3.7 %mate_first.1 = (bf16[1536,256]{1,0:T(8,128)(2,1)S(1)}, bf16[1536,256]{1,0:T(8,128)(2,1)S(1)}, f32[64,1024]{1,0:T(8,128)S(1)}) custom-call(s32[1]{0:T(128)} %bitcast.1.odd, f32[3,1024]{1,0:T(4,128)} %coords.7, s32[3,4]{1,0:T(4,128)} %pair.7, f32[64,1024]{1,0:T(8,128)S(1)} %get-tuple-element.305.partial, f32[72,768]{1,0:T(8,128)S(1)} %collective-permute-done.3.received), custom_call_target="tpu_custom_call" | custom-call | tf_op jit(solution)/shard_map/mate_first/pallas_call | solution.py:446
  22.9 0.0 collective-permute-done.4.received
  22.9 3.7 %next_first.1 = (bf16[1536,256]{1,0:T(8,128)(2,1)S(1)}, bf16[1536,256]{1,0:T(8,128)(2,1)S(1)}, f32[64,1024]{1,0:T(8,128)S(1)}, f32[64,768]{1,0:T(8,128)S(1)}, f32[64,768]{1,0:T(8,128)S(1)}) custom-call(s32[1]{0:T(128)} %bitcast.1.odd, f32[3,1024]{1,0:T(4,128)} %coords.7, s32[3,4]{1,0:T(4,128)} %pair.7, f32[64,1024]{1,0:T(8,128)S(1)} %get-tuple-element.307.partial, ...), custom_call_target="tpu_custom_call" | custom-call | tf_op jit(solution)/shard_map/next_first/pallas_call | solution.py:453
  26.6 3.6 %collective-permute-start.5 = (f32[64,768]{1,0:T(8,128)S(1)}, f32[64,768]{1,0:T(8,128)S(1)}, u32[]{:S(2)}, u32[]{:S(2)}) collective-permute-start(f32[64,768]{1,0:T(8,128)S(1)} %get-tuple-element.314), channel_id=1, source_target_pairs={{1,2},{2,1},{3,4},{4,3},{5,6},{6,5},{7,8},{8,7},{9,10},{10,9},{11,... | collective-permute-start | bytes 589832 | tf_op jit(solution)/shard_map/ppermute | solution.py:408
  30.3 1.9 %collective-permute-start.6 = (f32[64,768]{1,0:T(8,128)S(1)}, f32[64,768]{1,0:T(8,128)S(1)}, u32[]{:S(2)}, u32[]{:S(2)}) collective-permute-start(f32[64,768]{1,0:T(8,128)S(1)} %get-tuple-element.315), channel_id=1, source_target_pairs={{0,1},{1,0},{2,3},{3,2},{4,5},{5,4},{6,7},{7,6},{8,9},{9,8},{10,11... | collective-permute-start | bytes 589832 | tf_op jit(solution)/shard_map/ppermute | solution.py:407
  32.2 1.5 %local_second.1 = (f32[64,1024]{1,0:T(8,128)S(1)}, f32[64,128]{1,0:T(8,128)S(1)}) custom-call(f32[1,1024]{1,0:T(1,128)} %bitcast.99, f32[64,1024]{1,0:T(8,128)S(1)} %get-tuple-element.310.first, f32[64,1024]{1,0:T(8,128)S(1)} %get-tuple-element.309.second, bf16[4,1024,256]{2,1,0:T(8,128)(2,1)S(1)} %get-tuple-element.311.k_high, ...), custom_call_target="tpu_custom_call" | custom-call | tf_op jit(solution)/shard_map/local_second/pallas_call | solution.py:462
  33.7 0.0 copy-start.3
  33.7 0.0 collective-permute-done.5.beyond
  33.7 0.0 collective-permute-done.6.mate
  33.7 0.7 halo_second.1
  34.4 3.5 %collective-permute-start.7 = (f32[64,768]{1,0:T(8,128)S(1)}, f32[64,768]{1,0:T(8,128)S(1)}, u32[]{:S(2)}, u32[]{:S(2)}) collective-permute-start(f32[64,768]{1,0:T(8,128)S(1)} %get-tuple-element.323), channel_id=1, source_target_pairs={{1,2},{2,1},{3,4},{4,3},{5,6},{6,5},{7,8},{8,7},{9,10},{10,9},{11,... | collective-permute-start | bytes 589832 | tf_op jit(solution)/shard_map/ppermute | solution.py:408
  38.0 1.9 %collective-permute-start.8 = (f32[64,768]{1,0:T(8,128)S(1)}, f32[64,768]{1,0:T(8,128)S(1)}, u32[]{:S(2)}, u32[]{:S(2)}) collective-permute-start(f32[64,768]{1,0:T(8,128)S(1)} %get-tuple-element.324), channel_id=1, source_target_pairs={{0,1},{1,0},{2,3},{3,2},{4,5},{5,4},{6,7},{7,6},{8,9},{9,8},{10,11... | collective-permute-start | bytes 589832 | tf_op jit(solution)/shard_map/ppermute | solution.py:407
  39.9 0.0 copy-done.3
  39.9 0.8 local_third.1
  40.7 0.7 collective-permute-done.7.beyond
  41.4 0.0 collective-permute-done.8.mate
  41.4 0.0 copy-start.2
  41.4 0.0 copy-start.4
  41.4 0.0 copy-start.5
  41.4 0.9 %halo_third.1 = (f32[64,1024]{1,0:T(8,128)S(1)}, f32[32,4,128]{2,1,0:T(4,128)S(1)}) custom-call(s32[1]{0:T(128)} %bitcast.1.odd, f32[64,1024]{1,0:T(8,128)S(1)} %get-tuple-element.322.partial, f32[64,768]{1,0:T(8,128)S(1)} %collective-permute-done.7.beyond, f32[64,768]{1,0:T(8,128)S(1)} %collective-permute-done.8.mate, ...), custom_call_target="tpu_custom_call" | custom-call | tf_op jit(solution)/shard_map/halo_third/pallas_call | solution.py:474
  42.3 24.0 %all_to_all.10 = f32[32,4,128]{2,1,0:T(4,128)S(1)} all-to-all(f32[32,4,128]{2,1,0:T(4,128)S(1)} %get-tuple-element.326), channel_id=1, replica_groups=mesh['region'=32,'sub'=16] {'region'}, dimensions={0} | all-to-all | bytes 131072 | tf_op jit(solution)/shard_map/all_to_all | solution.py:482
  66.4 16.5 %all_to_all.11.sums = f32[16,4,128]{2,1,0:T(4,128)S(1)} all-to-all(f32[16,4,128]{2,1,0:T(4,128)S(1)} %broadcast_in_dim.5), channel_id=1, replica_groups=mesh['region'=32,'sub'=16] {'sub'}, dimensions={0} | all-to-all | bytes 65536 | tf_op jit(solution)/shard_map/all_to_all | solution.py:483
  82.9 1.2 %finish.1 = (f32[64,1024]{1,0:T(8,128)}, f32[64,1024]{1,0:T(8,128)}, f32[1,1]{1,0:T(1,128)}) custom-call(f32[16,4,128]{2,1,0:T(4,128)S(1)} %all_to_all.11.sums, f32[64,1024]{1,0:T(8,128)S(1)} %get-tuple-element.310.first, f32[64,1024]{1,0:T(8,128)S(1)} %get-tuple-element.309.second, f32[64,1024]{1,0:T(8,128)S(1)} %get-tuple-element.320.third, ...), custom_call_target="tpu_custom_call" | custom-call | tf_op jit(solution)/shard_map/finish/pallas_call | solution.py:484
  84.1 0.0 copy-done.2
  84.1 0.0 copy-done.4
  84.2 0.0 copy-done.5
  84.2 0.8 while.35
  (2 shorter events, 0.1 us)
Async XLA Ops:
  2.5 16.7 %collective-permute-start.3 = (f32[72,768]{1,0:T(8,128)S(1)}, f32[72,768]{1,0:T(8,128)S(1)}, u32[]{:S(2)}, u32[]{:S(2)}) collective-permute-start(f32[72,768]{1,0:T(8,128)S(1)} %get-tuple-element.306), channel_id=1, source_target_pairs={{0,1},{1,0},{2,3},{3,2},{4,5},{5,4},{6,7},{7,6},{8,9},{9,8},{10,11... | collective-permute-start | bytes 663560 | tf_op jit(solution)/shard_map/ppermute | solution.py:407
  11.3 11.6 %collective-permute-start.4 = (f32[72,768]{1,0:T(8,128)S(1)}, f32[72,768]{1,0:T(8,128)S(1)}, u32[]{:S(2)}, u32[]{:S(2)}) collective-permute-start(f32[72,768]{1,0:T(8,128)S(1)} %get-tuple-element.308), channel_id=1, source_target_pairs={{1,2},{2,1},{3,4},{4,3},{5,6},{6,5},{7,8},{8,7},{9,10},{10,9},{11,... | collective-permute-start | bytes 663560 | tf_op jit(solution)/shard_map/ppermute | solution.py:408
  26.6 7.1 %collective-permute-start.5 = (f32[64,768]{1,0:T(8,128)S(1)}, f32[64,768]{1,0:T(8,128)S(1)}, u32[]{:S(2)}, u32[]{:S(2)}) collective-permute-start(f32[64,768]{1,0:T(8,128)S(1)} %get-tuple-element.314), channel_id=1, source_target_pairs={{1,2},{2,1},{3,4},{4,3},{5,6},{6,5},{7,8},{8,7},{9,10},{10,9},{11,... | collective-permute-start | bytes 589832 | tf_op jit(solution)/shard_map/ppermute | solution.py:408
  30.3 3.4 %collective-permute-start.6 = (f32[64,768]{1,0:T(8,128)S(1)}, f32[64,768]{1,0:T(8,128)S(1)}, u32[]{:S(2)}, u32[]{:S(2)}) collective-permute-start(f32[64,768]{1,0:T(8,128)S(1)} %get-tuple-element.315), channel_id=1, source_target_pairs={{0,1},{1,0},{2,3},{3,2},{4,5},{5,4},{6,7},{7,6},{8,9},{9,8},{10,11... | collective-permute-start | bytes 589832 | tf_op jit(solution)/shard_map/ppermute | solution.py:407
  33.7 6.2 %copy-start.3 = (f32[1024]{0:T(1024)S(1)}, f32[1024]{0:T(1024)}, u32[]{:S(2)}) copy-start(f32[1024]{0:T(1024)} %param.17) | copy-start | bytes 12292
  34.4 7.0 %collective-permute-start.7 = (f32[64,768]{1,0:T(8,128)S(1)}, f32[64,768]{1,0:T(8,128)S(1)}, u32[]{:S(2)}, u32[]{:S(2)}) collective-permute-start(f32[64,768]{1,0:T(8,128)S(1)} %get-tuple-element.323), channel_id=1, source_target_pairs={{1,2},{2,1},{3,4},{4,3},{5,6},{6,5},{7,8},{8,7},{9,10},{10,9},{11,... | collective-permute-start | bytes 589832 | tf_op jit(solution)/shard_map/ppermute | solution.py:408
  38.0 3.4 %collective-permute-start.8 = (f32[64,768]{1,0:T(8,128)S(1)}, f32[64,768]{1,0:T(8,128)S(1)}, u32[]{:S(2)}, u32[]{:S(2)}) collective-permute-start(f32[64,768]{1,0:T(8,128)S(1)} %get-tuple-element.324), channel_id=1, source_target_pairs={{0,1},{1,0},{2,3},{3,2},{4,5},{5,4},{6,7},{7,6},{8,9},{9,8},{10,11... | collective-permute-start | bytes 589832 | tf_op jit(solution)/shard_map/ppermute | solution.py:407
  41.4 42.7 %copy-start.2 = (f32[64,1024]{1,0:T(8,128)S(1)}, f32[64,1024]{1,0:T(8,128)}, u32[]{:S(2)}) copy-start(f32[64,1024]{1,0:T(8,128)} %probes.3) | copy-start | bytes 786436
  41.4 42.7 %copy-start.4 = (f32[3,1024]{1,0:T(4,128)S(1)}, f32[3,1024]{1,0:T(4,128)}, u32[]{:S(2)}) copy-start(f32[3,1024]{1,0:T(4,128)} %coords.7) | copy-start | bytes 36868
  41.4 42.7 %copy-start.5 = (s32[3,4]{1,0:T(4,128)S(1)}, s32[3,4]{1,0:T(4,128)}, u32[]{:S(2)}) copy-start(s32[3,4]{1,0:T(4,128)} %pair.7) | copy-start | bytes 148

commit v3 on v2

v3 whole, which is shorter than its diff:
```python
import functools

import jax
import jax.numpy as jnp
from jax import lax
from jax.experimental import pallas as pl
from jax.experimental.pallas import tpu as pltpu
from jax.sharding import PartitionSpec as P

ITERS = 3
AXES = ("region", "sub")
SHIFT = 6.0
MAX_AMP = 100.0
MAX_NORM = 30.0
F32 = jnp.float32
BF16 = jnp.bfloat16
VMEM_LIMIT = 40 * 1024 * 1024


def shifted(array, by):
    count = lax.axis_size(AXES)
    pairs = [(i, i + by) for i in range(count) if 0 <= i + by < count]
    return lax.ppermute(array, AXES, pairs)


def wendland(left, right):
    squared = (left[0][..., :, None] - right[0][..., None, :]) ** 2
    squared = squared + (left[1][..., :, None] - right[1][..., None, :]) ** 2
    squared = squared + (left[2][..., :, None] - right[2][..., None, :]) ** 2
    distance = jnp.sqrt(squared)
    support = jnp.maximum(1.0 - distance, 0.0)
    return support**4 * (4.0 * distance + 1.0)


def squares(residual):
    return lax.psum(jnp.sum(residual * residual, axis=1), AXES)


def plain(coords, noise_var, pair_list, probes):
    probe_count, points_here = probes.shape
    links = pair_list.shape[0]
    blocks_here = pair_list.shape[1]
    block_len = points_here // blocks_here
    span_cols = links * block_len
    local_c = coords.reshape(3, blocks_here, block_len)
    weights = pair_list.astype(F32)
    ahead_c = shifted(coords[:, :span_cols], -1)
    ext_c = jnp.concatenate([local_c, ahead_c.reshape(3, links, block_len)], axis=1)

    def step(_, state):
        solution, residual, direction, res_norm = state
        ahead_v = shifted(direction[:, :span_cols], -1)
        ext_v = jnp.concatenate([direction, ahead_v], axis=1).reshape(probe_count, blocks_here + links, block_len)
        local_v = ext_v[:, :blocks_here]
        result = (noise_var[None, :] * direction).reshape(probe_count, blocks_here, block_len)
        spill = jnp.zeros((probe_count, blocks_here + links, block_len), F32)
        for offset in range(links + 1):
            kernel_block = wendland(local_c, ext_c[:, offset : offset + blocks_here])
            if offset > 0:
                kernel_block = kernel_block * weights[offset - 1][:, None, None]
            result = result + jnp.einsum(
                "pbj,bij->pbi", ext_v[:, offset : offset + blocks_here], kernel_block, precision=lax.Precision.HIGHEST
            )
            if offset > 0:
                spill = spill.at[:, offset : offset + blocks_here].add(
                    jnp.einsum("pbi,bij->pbj", local_v, kernel_block, precision=lax.Precision.HIGHEST)
                )
        result = result + spill[:, :blocks_here]
        result = result.at[:, :links].add(shifted(spill[:, blocks_here:], 1))
        product = result.reshape(probe_count, points_here)
        step_size = res_norm / lax.psum(jnp.sum(direction * product, axis=1), AXES)
        solution = solution + step_size[:, None] * direction
        residual = residual - step_size[:, None] * product
        next_norm = squares(residual)
        direction = residual + (next_norm / res_norm)[:, None] * direction
        return solution, residual, direction, next_norm

    state = (jnp.zeros_like(probes), probes, probes, squares(probes))
    solution, residual, _, _ = lax.fori_loop(0, ITERS, step, state)
    return solution, residual


def is_right(mate):
    return lax.axis_index("sub") % 2 == (0 if mate else 1)


def own_place(right, blocks, links, length, n):
    return pl.multiple_of(jnp.where(right, blocks - 1 - links + n, links - n) * length, 128)


def halo_place(right, links, length, h):
    return pl.multiple_of(jnp.where(right, h, links - 1 - h) * length, 128)


def send_place(right, here, span):
    return pl.multiple_of(jnp.where(right, here - span, 0), 128)


def split(value):
    high = value.astype(BF16)
    return high, (value - high.astype(F32)).astype(BF16)


def start_all(copies):
    for copy in copies:
        copy.start()
    return copies


def pack_kernel(coords, pair, probes, to_mate, to_next, points, flags, sem):
    links, blocks = pair.shape
    here = coords.shape[1]
    length = here // blocks
    rows, span = probes.shape[0], links * length
    place = [send_place(is_right(mate), here, span) for mate in (True, False)]
    copies = start_all(
        [
            pltpu.make_async_copy(pair, flags, sem.at[0]),
            pltpu.make_async_copy(coords, points, sem.at[1]),
            pltpu.make_async_copy(probes.at[:, pl.ds(place[0], span)], to_mate.at[0:rows], sem.at[2]),
            pltpu.make_async_copy(probes.at[:, pl.ds(place[1], span)], to_next.at[0:rows], sem.at[3]),
        ]
    )
    copies[0].wait()
    copies[1].wait()
    right = is_right(True)
    extra = [points[...]]
    for k in range(links):
        flag = [flags[k, b].astype(F32) for b in range(blocks)]
        extra.append(jnp.concatenate([jnp.full((1, length), f, F32) for f in flag], axis=1))
    extra = jnp.concatenate(extra + [jnp.zeros((8 - 3 - links, here), F32)], axis=0)
    low, high = extra[:, 0:span], extra[:, here - span :]
    to_mate[rows : rows + 8, :] = jnp.where(right, high, low)
    to_next[rows : rows + 8, :] = jnp.where(right, low, high)
    copies[2].wait()
    copies[3].wait()


def fill_columns(columns, at, block):
    turned = jnp.transpose(block)
    for d in range(3):
        columns[d, at : at + turned.shape[0], :] = jnp.broadcast_to(turned[:, d : d + 1], (turned.shape[0], 128))


def fill_strip(columns, from_row, strip, rows, lanes, flag, stores):
    column = [columns[d, pl.ds(from_row, strip), :].reshape(strip // 8, 8, 128) for d in range(3)]
    for lane, one_flag, store in zip(lanes, flag, stores):
        squared = None
        for d in range(3):
            away = column[d] - rows[d, :, lane : lane + 128][None]
            squared = away * away if squared is None else squared + away * away
        squared = jnp.maximum(squared, 1e-30)
        distance = squared * lax.rsqrt(squared)
        support = jnp.maximum(1.0 - distance, 0.0)
        support = support * support
        value = support * support * ((4.0 * one_flag)[None] * distance + one_flag[None])
        store(*split(value.reshape(strip, 128)))


def store_halves(halves, at, vector):
    rows, size = vector.shape
    top, rest = split(vector)
    halves[0:rows, at : at + size] = top
    halves[rows : 2 * rows, at : at + size] = rest


def multiply(both, k_high, k_low, turned=False):
    rows = both.shape[0] // 2
    dims = (((1,), (1 if turned else 0,)), ((), ()))
    most = lax.dot_general(both, k_high, dims, preferred_element_type=F32)
    rest = lax.dot_general(both[0:rows], k_low, dims, preferred_element_type=F32)
    return most[0:rows] + (most[rows : 2 * rows] + rest)


def local_product(noise, vector, k_high, k_low, out, halves):
    blocks, _, length = k_high.shape
    store_halves(halves, 0, vector[...])
    for i in range(blocks):
        at = slice(i * length, (i + 1) * length)
        value = multiply(halves[...], k_high[i], k_low[i])
        out[:, at] = value + (noise[:, at] - SHIFT) * vector[:, at]


def local_first_kernel(coords, noise, pair, probes, k_high, k_low, out, first, columns, halves, rows, flags, sem):
    links, blocks = pair.shape
    here = probes.shape[1]
    length = here // blocks
    copy = pltpu.make_async_copy(probes, first, sem.at[0])
    copy.start()
    for j in range(blocks):
        own = coords[:, j * length : (j + 1) * length]
        fill_columns(columns, j * length, jnp.concatenate([own, jnp.zeros((5, length), F32)], axis=0))
    for d in range(3):
        rows[d] = jnp.broadcast_to(coords[d : d + 1, :], rows.shape[1:])
    for j in range(blocks):
        for i in range(blocks):
            if i == j:
                flag = 1.0
            elif abs(i - j) <= links:
                flag = pair[abs(i - j) - 1, min(i, j)].astype(F32)
            else:
                flag = 0.0
            flags[j, :, i * length : (i + 1) * length] = jnp.full((8, length), flag, F32)
    strip = 32

    def store_to(i, row, lane):
        def store(top, rest):
            k_high[i, pl.ds(row, strip), lane : lane + 128] = top
            k_low[i, pl.ds(row, strip), lane : lane + 128] = rest

        return store

    def body(s, _):
        row = pl.multiple_of(s * strip, strip)
        block = s // (length // strip)
        lanes = list(range(0, here, 128))
        fill_strip(
            columns,
            row,
            strip,
            rows,
            lanes,
            [flags[block, :, lane : lane + 128] for lane in lanes],
            [store_to(lane // length, row, lane % length) for lane in lanes],
        )
        return 0

    lax.fori_loop(0, here // strip, body, 0)
    copy.wait()
    local_product(noise, first, k_high, k_low, out, halves)


def fill_halo(right, pair, received, columns, k_high, k_low, rows):
    links, blocks = pair.shape
    span = received.shape[1]
    length = span // links
    at = received.shape[0] - 8
    place = [pl.ds(halo_place(right, links, length, h), length) for h in range(links)]
    for h in range(links):
        for d in range(3):
            coord = received[at + d : at + d + 1, place[h]]
            rows[d, :, h * length : (h + 1) * length] = jnp.broadcast_to(coord, (8, length))
    for n in range(1, links + 1):
        own = own_place(right, blocks, links, length, n)
        lower = jnp.where(right, blocks - 1 - links + n, 0)
        flags = []
        for h in range(n):
            k = links - n + h
            ours = jnp.full((1, 128), pair[k, lower].astype(F32), F32)
            theirs = received[at + 3 + k : at + 4 + k, place[h]][:, 0:128]
            flags += [jnp.broadcast_to(jnp.where(right, ours, theirs), (8, 128))] * (length // 128)
        lanes = list(range(0, n * length, 128))
        strip = 32 if n > 2 else 64

        def store_to(row, lane):
            def store(top, rest):
                k_high[pl.ds(row, strip), lane : lane + 128] = top
                k_low[pl.ds(row, strip), lane : lane + 128] = rest

            return store

        def body(s, _):
            step = pl.multiple_of(s * strip, strip)
            stores = [store_to((n - 1) * length + step, lane) for lane in lanes]
            fill_strip(columns, pl.multiple_of(own + step, strip), strip, rows, lanes, flags, stores)
            return 0

        lax.fori_loop(0, length // strip, body, 0)


def halo_product(right, load, k_high, k_low, out, halves, blocks):
    span = k_high.shape[0]
    length = out.shape[1] // blocks
    links = span // length
    for h in range(links):
        store_halves(halves, h * length, load(pl.ds(halo_place(right, links, length, h), length)))
    for n in range(1, links + 1):
        deep, at = slice(0, n * length), slice((n - 1) * length, n * length)
        own = pl.ds(own_place(right, blocks, links, length, n), length)
        out[:, own] = out[:, own] + multiply(halves[:, deep], k_high[at, deep], k_low[at, deep], turned=True)


def own_product(right, vector, k_high, k_low, out, halves, blocks):
    span = out.shape[1]
    length = vector.shape[1] // blocks
    links = span // length
    for n in range(1, links + 1):
        own = pl.ds(own_place(right, blocks, links, length, n), length)
        store_halves(halves, (n - 1) * length, vector[:, own])
    for h in range(links):
        deep, at = slice(h * length, span), slice(h * length, (h + 1) * length)
        place = pl.ds(halo_place(right, links, length, h), length)
        out[:, place] = multiply(halves[:, deep], k_high[deep, at], k_low[deep, at])


def store_send(right, vector, send):
    here, span = vector.shape[1], send.shape[1]
    send[...] = vector[:, pl.ds(send_place(right, here, span), span)]


def mate_first_kernel(pair, partial, received, columns, k_high, k_low, out, to_next, halves, rows):
    probe_count = out.shape[0]
    right = is_right(True)
    fill_halo(right, pair, received, columns, k_high, k_low, rows)
    out[...] = partial[...]
    halo_product(right, lambda at: received[0:probe_count, at], k_high, k_low, out, halves, pair.shape[1])
    store_send(is_right(False), out, to_next)


def next_first_kernel(
    pair, partial, first, received, columns, k_high, k_low, out, given, to_mate, halves, rows
):
    probe_count = out.shape[0]
    right = is_right(False)
    fill_halo(right, pair, received, columns, k_high, k_low, rows)
    out[...] = partial[...]
    halo_product(right, lambda at: received[0:probe_count, at], k_high, k_low, out, halves, pair.shape[1])
    store_send(is_right(True), out, to_mate)
    own_product(right, first, k_high, k_low, given, halves, pair.shape[1])


def add_sums(table, terms):
    lane = lax.broadcasted_iota(jnp.int32, table.shape, 1)
    for power, left, right in terms:
        part = None
        for at in range(0, left.shape[1], 128):
            term = left[:, at : at + 128] * right[:, at : at + 128]
            part = term if part is None else part + term
        table = jnp.where(lane == power, jnp.sum(part, axis=1, keepdims=True), table)
    return table


def local_second_kernel(noise, first, second, k_high, k_low, out, table, halves):
    local_product(noise, second, k_high, k_low, out, halves)
    table[...] = add_sums(jnp.zeros(table.shape, F32), ((0, first, first), (1, first, second), (2, second, second)))


def local_third_kernel(noise, second, third, table_in, k_high, k_low, out, table, halves):
    local_product(noise, third, k_high, k_low, out, halves)
    table[...] = add_sums(table_in[...], ((3, second, third), (4, third, third)))


def halo_second_kernel(
    partial, beyond, given, mate, mate_high, mate_low, next_high, next_low, out, to_next, to_mate, halves, *, blocks
):
    out[...] = partial[...]
    halo_product(is_right(True), lambda at: mate[:, at], mate_high, mate_low, out, halves, blocks)
    halo_product(is_right(False), lambda at: beyond[:, at] + given[:, at], next_high, next_low, out, halves, blocks)
    store_send(is_right(False), out, to_next)
    store_send(is_right(True), out, to_mate)


def halo_third_kernel(
    partial, beyond, mate, mate_high, mate_low, next_high, next_low, third, table, out, sums, halves, *, blocks
):
    out[...] = partial[...]
    halo_product(is_right(True), lambda at: mate[:, at], mate_high, mate_low, out, halves, blocks)
    halo_product(is_right(False), lambda at: beyond[:, at], next_high, next_low, out, halves, blocks)
    full = add_sums(table[...], ((5, third, out), (6, out, out)))
    turned = jnp.transpose(full)[0:8, :]
    compact = jnp.concatenate([turned[0:4], turned[4:8]], axis=1)
    sums[...] = jnp.broadcast_to(compact[None], sums.shape)


def polynomials(moment):
    def dot(p, q):
        total, size = 0.0, 0.0
        for i, x in enumerate(p):
            for j, y in enumerate(q):
                term = x * y * moment[i + j]
                total, size = total + term, size + jnp.abs(term)
        return total, size

    def add(p, q, factor):
        count = max(len(p), len(q))
        p, q = p + [0.0] * (count - len(p)), q + [0.0] * (count - len(q))
        return [x + factor * y for x, y in zip(p, q)]

    one = jnp.ones_like(moment[0])
    solution, residual, direction = [jnp.zeros_like(one)], [one], [one]
    norm = moment[0]
    good = norm > 0.0
    for step in range(ITERS):
        image = add([0.0 * one] + direction, direction, SHIFT)
        curvature, size = dot(direction, image)
        good = good & (size <= MAX_AMP * curvature)
        step_size = norm / curvature
        solution = add(solution, direction, step_size)
        residual = add(residual, image, -step_size)
        new, size = dot(residual, residual)
        if step < ITERS - 1:
            good = good & (size <= MAX_AMP * new)
            direction = add(residual, direction, new / norm)
        norm = new
    size = sum(jnp.abs(x) * jnp.sqrt(moment[2 * i]) for i, x in enumerate(residual))
    good = good & (size * size <= MAX_NORM * MAX_NORM * norm)
    return solution, residual, good


def finish_kernel(sums, first, second, third, fourth, solution, residual, good):
    total = jnp.sum(sums[...], axis=0)
    rows = first.shape[0]
    moment = [total[k : k + 1, 0:rows] for k in range(4)] + [total[k : k + 1, rows : 2 * rows] for k in range(3)]
    mix_solution, mix_residual, fine = polynomials(moment)
    table = jnp.concatenate(mix_solution + mix_residual + [jnp.zeros_like(moment[0])], axis=0)
    table = jnp.concatenate([table, jnp.zeros_like(table)], axis=1)
    table = jnp.transpose(jnp.concatenate([table, jnp.zeros((120, 128), F32)], axis=0))[0:rows]
    basis = (first[...], second[...], third[...], fourth[...])

    def mix(at, count):
        total = table[:, at : at + 1] * basis[0]
        for k in range(1, count):
            total = total + table[:, at + k : at + k + 1] * basis[k]
        return total

    solution[...] = mix(0, ITERS)
    residual[...] = mix(ITERS, ITERS + 1)
    good[0, 0] = jnp.min(jnp.where(fine, 1.0, 0.0))


VMEM = pl.BlockSpec(memory_space=pltpu.VMEM)
SMEM = pl.BlockSpec(memory_space=pltpu.SMEM)
ANY = pl.BlockSpec(memory_space=pl.ANY)


def call(kernel, name, out_shape, in_specs, scratch_shapes=(), out_specs=None):
    kwargs = {} if out_specs is None else {"out_specs": out_specs}
    return pl.pallas_call(
        kernel,
        out_shape=out_shape,
        in_specs=in_specs,
        scratch_shapes=scratch_shapes,
        compiler_params=pltpu.CompilerParams(vmem_limit_bytes=VMEM_LIMIT),
        name=name,
        **kwargs,
    )


def swap_mate(array):
    return lax.ppermute(array, AXES, [(i, i ^ 1) for i in range(lax.axis_size(AXES))])


def swap_next(array):
    return lax.ppermute(array, AXES, [(i, i + 1 if i % 2 else i - 1) for i in range(1, lax.axis_size(AXES) - 1)])


def per_device(coords, noise_var, pair_list, probes):
    rows, here = probes.shape
    links, blocks = pair_list.shape
    length = here // blocks
    span = links * length
    noise = noise_var.reshape(1, here)

    whole = jax.ShapeDtypeStruct((rows, here), F32)
    part = jax.ShapeDtypeStruct((rows, span), F32)
    packed = jax.ShapeDtypeStruct((rows + 8, span), F32)
    sums_table = jax.ShapeDtypeStruct((rows, 128), F32)
    local_table = jax.ShapeDtypeStruct((blocks, here, length), BF16)
    halo_table = jax.ShapeDtypeStruct((span, span), BF16)
    local_halves = pltpu.VMEM((2 * rows, here), BF16)
    halo_halves = pltpu.VMEM((2 * rows, span), BF16)

    to_mate, to_next = call(
        pack_kernel,
        "pack",
        (packed, packed),
        [ANY, ANY, ANY],
        [pltpu.VMEM((3, here), F32), pltpu.SMEM((links, blocks), jnp.int32), pltpu.SemaphoreType.DMA((4,))],
    )(coords, pair_list, probes)
    mate, beyond = swap_mate(to_mate), swap_next(to_next)
    k_high, k_low, partial, first, columns = call(
        local_first_kernel,
        "local_first",
        (local_table, local_table, whole, whole, jax.ShapeDtypeStruct((3, here, 128), F32)),
        [VMEM, VMEM, SMEM, ANY],
        [
            local_halves,
            pltpu.VMEM((3, 8, here), F32),
            pltpu.VMEM((blocks, 8, here), F32),
            pltpu.SemaphoreType.DMA((1,)),
        ],
    )(coords, noise, pair_list, probes)
    halo_scratch = [halo_halves, pltpu.VMEM((3, 8, span), F32)]
    mate_high, mate_low, partial, to_next = call(
        mate_first_kernel, "mate_first", (halo_table, halo_table, whole, part), [SMEM, VMEM, VMEM, VMEM], halo_scratch
    )(pair_list, partial, mate, columns)
    ahead = swap_next(to_next)
    next_high, next_low, second, given, to_mate = call(
        next_first_kernel,
        "next_first",
        (halo_table, halo_table, whole, part, part),
        [SMEM, VMEM, VMEM, VMEM, VMEM],
        halo_scratch,
    )(pair_list, partial, first, beyond, columns)

    mate = swap_mate(to_mate)
    partial, table = call(local_second_kernel, "local_second", (whole, sums_table), [VMEM] * 5, [local_halves])(
        noise, first, second, k_high, k_low
    )
    third, to_next, to_mate = call(
        functools.partial(halo_second_kernel, blocks=blocks), "halo_second", (whole, part, part), [VMEM] * 8, [halo_halves]
    )(partial, ahead, given, mate, mate_high, mate_low, next_high, next_low)

    beyond, mate = swap_next(to_next), swap_mate(to_mate)
    partial, table = call(local_third_kernel, "local_third", (whole, sums_table), [VMEM] * 6, [local_halves])(
        noise, second, third, table, k_high, k_low
    )
    regions, subs = lax.axis_size("region"), lax.axis_size("sub")
    fourth, sums = call(
        functools.partial(halo_third_kernel, blocks=blocks),
        "halo_third",
        (whole, jax.ShapeDtypeStruct((regions, 4, 128), F32)),
        [VMEM] * 9,
        [halo_halves],
    )(partial, beyond, mate, mate_high, mate_low, next_high, next_low, third, table)

    sums = jnp.sum(lax.all_to_all(sums, "region", 0, 0), axis=0)
    sums = lax.all_to_all(jnp.broadcast_to(sums[None], (subs, 4, 128)), "sub", 0, 0)
    solution, residual, good = call(
        finish_kernel,
        "finish",
        (whole, whole, jax.ShapeDtypeStruct((1, 1), F32)),
        [VMEM] * 5,
        out_specs=(VMEM, VMEM, SMEM),
    )(sums, first, second, third, fourth)

    def again(state):
        solution, residual = plain(coords, noise_var, pair_list, probes)
        return jnp.ones_like(state[0]), solution, residual

    _, solution, residual = lax.while_loop(lambda state: state[0][0, 0] < 0.5, again, (good, solution, residual))
    return solution, residual


def solution(mesh):
    in_specs = (P(None, AXES), P(AXES), P(None, AXES), P(None, AXES))
    out_specs = (P(None, AXES), P(None, AXES))
    return jax.shard_map(per_device, mesh=mesh, in_specs=in_specs, out_specs=out_specs, check_vma=False)
```

time: 85.9 us -> 81 us (0.943)
  Pallas kernels: 20.3 us -> 17.6 us
  blocking collectives: 40.6 us -> 38 us
  waiting for transfers between devices: 0.73 us -> 2.94 us
  starting transfers between devices: 21.7 us -> 20.1 us
    ppermute x6, waiting for transfers between devices: 0.73 us -> 2.94 us  [the longest x3 2.34 us: swap_next(): lax.ppermute(array, AXES, [(i, i + 1 if i % 2 else i - 1) for i in range(...]
    all_to_all x1, blocking collectives: 24 us -> 22 us  [per_device(): sums = jnp.sum(lax.all_to_all(sums, 'region', 0, 0), axis=0)]
    pallas_call x5, Pallas kernels: 10.8 us -> 9.03 us  [the longest x1 2.78 us: per_device(): call(next_first_kernel, 'next_first', (halo_table, halo_table, whole, par...]
    ppermute x6, starting transfers between devices: 21.7 us -> 20.1 us  [the longest x3 12.6 us: swap_mate(): lax.ppermute(array, AXES, [(i, i ^ 1) for i in range(lax.axis_size(AXES))])]
  transfers between devices with their start and end apart: 6 -> 6, of which waited for: 1 -> 2; matrix products, arithmetic and copies ran while one was open for 0% -> 0% of each run, Pallas kernels for 14% -> 16%
where the time goes in v3:
time: 81 us; the launch traced here: 80.5 us
  blocking collectives  38 us (47%)
  starting transfers between devices  20.1 us (25%)
  Pallas kernels  17.6 us (22%)
  waiting for transfers between devices  2.94 us (4%)
  between operations  0.99 us (1%)
  loops' own time  0.81 us (1%)
    all_to_all x1, blocking collectives, per_device(): sums = jnp.sum(lax.all_to_all(sums, 'region', 0, 0), axis=0)  22 us
    all_to_all x1, blocking collectives, per_device(): lax.all_to_all(jnp.broadcast_to(sums[None], (subs, 4, 128)), 'sub', 0, 0)  16 us
    ppermute x3, starting transfers between devices, swap_mate(): lax.ppermute(array, AXES, [(i, i ^ 1) for i in range(lax.axis_size(AXES))])  12.6 us
    ppermute x3, starting transfers between devices, swap_next(): lax.ppermute(array, AXES, [(i, i + 1 if i % 2 else i - 1) for i in range(...  7.48 us
    pallas_call x1, Pallas kernels, per_device(): call(local_first_kernel, 'local_first', (local_table, local_table, whole,...  5.82 us
    pallas_call x1, Pallas kernels, per_device(): call(next_first_kernel, 'next_first', (halo_table, halo_table, whole, par...  2.78 us
    pallas_call x1, Pallas kernels, per_device(): call(mate_first_kernel, 'mate_first', (halo_table, halo_table, whole, par...  2.69 us
    ppermute x3, waiting for transfers between devices, swap_next(): lax.ppermute(array, AXES, [(i, i + 1 if i % 2 else i - 1) for i in range(...  2.34 us
  transfers between devices with their start and end apart: 6, of which 2 were waited for; matrix products, arithmetic and copies ran while one was open for 0% of the time, Pallas kernels for 16%

profile of v3, /device:TPU:1, one launch (start us, length us, event | category | flops | bytes accessed | tf_op | source)
XLA Modules:
  0.0 80.5 jit_solution(1661500581457561690)
XLA Ops:
  0.6 1.1 %pack.1 = (f32[72,768]{1,0:T(8,128)S(1)}, f32[72,768]{1,0:T(8,128)S(1)}) custom-call(f32[3,1024]{1,0:T(4,128)} %coords.3, s32[3,4]{1,0:T(4,128)} %pair.7, f32[64,1024]{1,0:T(8,128)} %probes.3), custom_call_target="tpu_custom_call" | custom-call | tf_op jit(solution)/shard_map/pack/pallas_call | solution.py:463
  1.7 0.0 copy-start.5
  1.7 8.8 %collective-permute-start.3 = (f32[72,768]{1,0:T(8,128)S(1)}, f32[72,768]{1,0:T(8,128)S(1)}, u32[]{:S(2)}, u32[]{:S(2)}) collective-permute-start(f32[72,768]{1,0:T(8,128)S(1)} %get-tuple-element.308), channel_id=1, source_target_pairs={{0,1},{1,0},{2,3},{3,2},{4,5},{5,4},{6,7},{7,6},{8,9},{9,8},{10,11... | collective-permute-start | bytes 663560 | tf_op jit(solution)/shard_map/ppermute | solution.py:440
  10.5 1.9 %collective-permute-start.4 = (f32[72,768]{1,0:T(8,128)S(1)}, f32[72,768]{1,0:T(8,128)S(1)}, u32[]{:S(2)}, u32[]{:S(2)}) collective-permute-start(f32[72,768]{1,0:T(8,128)S(1)} %get-tuple-element.312), channel_id=1, source_target_pairs={{1,2},{2,1},{3,4},{4,3},{5,6},{6,5},{7,8},{8,7},{9,10},{10,9},{11,... | collective-permute-start | bytes 663560 | tf_op jit(solution)/shard_map/ppermute | solution.py:444
  12.4 5.8 %local_first.1 = (bf16[4,1024,256]{2,1,0:T(8,128)(2,1)S(1)}, bf16[4,1024,256]{2,1,0:T(8,128)(2,1)S(1)}, f32[64,1024]{1,0:T(8,128)S(1)}, f32[64,1024]{1,0:T(8,128)S(1)}, f32[3,1024,128]{2,1,0:T(8,128)S(1)}) custom-call(f32[3,1024]{1,0:T(4,128)} %coords.3, f32[1,1024]{1,0:T(1,128)} %bitcast.97, s32[3,4]{1,0:T(4,128)} %pair.7, f32[64,1024]{1,0:T(8,128)} %probes.3), custom_call_target="tpu_custom_call" | custom-call | tf_op jit(solution)/shard_map/local_first/pallas_call | solution.py:471
  18.3 0.0 collective-permute-done.3.received
  18.3 2.7 %mate_first.1 = (bf16[768,768]{1,0:T(8,128)(2,1)S(1)}, bf16[768,768]{1,0:T(8,128)(2,1)S(1)}, f32[64,1024]{1,0:T(8,128)S(1)}, f32[64,768]{1,0:T(8,128)S(1)}) custom-call(s32[3,4]{1,0:T(4,128)} %pair.7, f32[64,1024]{1,0:T(8,128)S(1)} %get-tuple-element.307.partial, f32[72,768]{1,0:T(8,128)S(1)} %collective-permute-done.3.received, ...), custom_call_target="tpu_custom_call" | custom-call | tf_op jit(solution)/shard_map/mate_first/pallas_call | solution.py:484
  21.0 0.0 copy-start.3
  21.0 3.6 %collective-permute-start.5 = (f32[64,768]{1,0:T(8,128)S(1)}, f32[64,768]{1,0:T(8,128)S(1)}, u32[]{:S(2)}, u32[]{:S(2)}) collective-permute-start(f32[64,768]{1,0:T(8,128)S(1)} %get-tuple-element.317), channel_id=1, source_target_pairs={{1,2},{2,1},{3,4},{4,3},{5,6},{6,5},{7,8},{8,7},{9,10},{10,9},{11,... | collective-permute-start | bytes 589832 | tf_op jit(solution)/shard_map/ppermute | solution.py:444
  24.6 0.0 collective-permute-done.4.received
  24.7 0.0 copy-done.5
  24.7 2.8 %next_first.1 = (bf16[768,768]{1,0:T(8,128)(2,1)S(1)}, bf16[768,768]{1,0:T(8,128)(2,1)S(1)}, f32[64,1024]{1,0:T(8,128)S(1)}, f32[64,768]{1,0:T(8,128)S(1)}, f32[64,768]{1,0:T(8,128)S(1)}) custom-call(s32[3,4]{1,0:T(4,128)S(1)} %copy-done.5, f32[64,1024]{1,0:T(8,128)S(1)} %get-tuple-element.310.partial, f32[64,1024]{1,0:T(8,128)S(1)} %get-tuple-element.311.first, ...), custom_call_target="tpu_custom_call" | custom-call | tf_op jit(solution)/shard_map/next_first/pallas_call | solution.py:488
  27.5 1.9 %collective-permute-start.6 = (f32[64,768]{1,0:T(8,128)S(1)}, f32[64,768]{1,0:T(8,128)S(1)}, u32[]{:S(2)}, u32[]{:S(2)}) collective-permute-start(f32[64,768]{1,0:T(8,128)S(1)} %get-tuple-element.319), channel_id=1, source_target_pairs={{0,1},{1,0},{2,3},{3,2},{4,5},{5,4},{6,7},{7,6},{8,9},{9,8},{10,11... | collective-permute-start | bytes 589832 | tf_op jit(solution)/shard_map/ppermute | solution.py:440
  29.4 0.0 copy-done.3
  29.4 0.8 local_second.1
  30.2 0.0 collective-permute-done.5.beyond
  30.2 0.6 collective-permute-done.6.mate
  30.8 1.1 %halo_second.1 = (f32[64,1024]{1,0:T(8,128)S(1)}, f32[64,768]{1,0:T(8,128)S(1)}, f32[64,768]{1,0:T(8,128)S(1)}) custom-call(f32[64,1024]{1,0:T(8,128)S(1)} %get-tuple-element.316.partial, f32[64,768]{1,0:T(8,128)S(1)} %collective-permute-done.5.beyond, f32[64,768]{1,0:T(8,128)S(1)} %get-tuple-element.318.given, f32[64,768]{1,0:T(8,128)S(1)} %collective-permute-done.6.mate, ...), custom_call_target="tpu_custom_call" | custom-call | tf_op jit(solution)/shard_map/halo_second/pallas_call | solution.py:500
  31.9 1.9 %collective-permute-start.7 = (f32[64,768]{1,0:T(8,128)S(1)}, f32[64,768]{1,0:T(8,128)S(1)}, u32[]{:S(2)}, u32[]{:S(2)}) collective-permute-start(f32[64,768]{1,0:T(8,128)S(1)} %get-tuple-element.327), channel_id=1, source_target_pairs={{1,2},{2,1},{3,4},{4,3},{5,6},{6,5},{7,8},{8,7},{9,10},{10,9},{11,... | collective-permute-start | bytes 589832 | tf_op jit(solution)/shard_map/ppermute | solution.py:444
  33.9 1.9 %collective-permute-start.8 = (f32[64,768]{1,0:T(8,128)S(1)}, f32[64,768]{1,0:T(8,128)S(1)}, u32[]{:S(2)}, u32[]{:S(2)}) collective-permute-start(f32[64,768]{1,0:T(8,128)S(1)} %get-tuple-element.328), channel_id=1, source_target_pairs={{0,1},{1,0},{2,3},{3,2},{4,5},{5,4},{6,7},{7,6},{8,9},{9,8},{10,11... | collective-permute-start | bytes 589832 | tf_op jit(solution)/shard_map/ppermute | solution.py:440
  35.8 0.8 local_third.1
  36.6 2.3 %collective-permute-done.7.beyond = f32[64,768]{1,0:T(8,128)S(1)} collective-permute-done((f32[64,768]{1,0:T(8,128)S(1)}, f32[64,768]{1,0:T(8,128)S(1)}, u32[]{:S(2)}, u32[]{:S(2)}) %collective-permute-start.7) | collective-permute-done | bytes 196640 | tf_op jit(solution)/shard_map/ppermute | solution.py:444
  38.9 0.0 collective-permute-done.8.mate
  38.9 1.3 %halo_third.1 = (f32[64,1024]{1,0:T(8,128)S(1)}, f32[32,4,128]{2,1,0:T(4,128)S(1)}) custom-call(f32[64,1024]{1,0:T(8,128)S(1)} %get-tuple-element.326.partial, f32[64,768]{1,0:T(8,128)S(1)} %collective-permute-done.7.beyond, f32[64,768]{1,0:T(8,128)S(1)} %collective-permute-done.8.mate, bf16[768,768]{1,0:T(8,128)(2,1)S(1)} %get-tuple-element.320.mate_high, ...), custom_call_target="tpu_custom_call" | custom-call | tf_op jit(solution)/shard_map/halo_third/pallas_call | solution.py:509
  40.3 0.0 copy-start.2
  40.3 0.0 copy-start.4
  40.3 22.0 %all_to_all.10 = f32[32,4,128]{2,1,0:T(4,128)S(1)} all-to-all(f32[32,4,128]{2,1,0:T(4,128)S(1)} %get-tuple-element.330), channel_id=1, replica_groups=mesh['region'=32,'sub'=16] {'region'}, dimensions={0} | all-to-all | bytes 131072 | tf_op jit(solution)/shard_map/all_to_all | solution.py:517
  62.3 16.0 %all_to_all.11.sums = f32[16,4,128]{2,1,0:T(4,128)S(1)} all-to-all(f32[16,4,128]{2,1,0:T(4,128)S(1)} %broadcast_in_dim.5), channel_id=1, replica_groups=mesh['region'=32,'sub'=16] {'sub'}, dimensions={0} | all-to-all | bytes 65536 | tf_op jit(solution)/shard_map/all_to_all | solution.py:518
  78.3 1.2 %finish.1 = (f32[64,1024]{1,0:T(8,128)}, f32[64,1024]{1,0:T(8,128)}, f32[1,1]{1,0:T(1,128)}) custom-call(f32[16,4,128]{2,1,0:T(4,128)S(1)} %all_to_all.11.sums, f32[64,1024]{1,0:T(8,128)S(1)} %get-tuple-element.311.first, f32[64,1024]{1,0:T(8,128)S(1)} %get-tuple-element.313.second, f32[64,1024]{1,0:T(8,128)S(1)} %get-tuple-element.324.third, ...), custom_call_target="tpu_custom_call" | custom-call | tf_op jit(solution)/shard_map/finish/pallas_call | solution.py:519
  79.5 0.0 copy-done.2
  79.5 0.0 copy-done.4
  79.6 0.8 %while.35 = (f32[1,1]{1,0:T(1,128)}, f32[64,1024]{1,0:T(8,128)}, f32[64,1024]{1,0:T(8,128)}, f32[64,1024]{1,0:T(8,128)S(1)}, f32[3,1024]{1,0:T(4,128)S(1)}, /*in...) while((f32[1,1]{1,0:T(1,128)}, f32[64,1024]{1,0:T(8,128)}, f32[64,1024]{1,0:T(8,128)}, ...), condition=%region_10.11_spmd, body=%region_1.10_spmd | while | flops 1439929600 | bytes 21131516 | solution.py:531
  (2 shorter events, 0.1 us)
Async XLA Ops:
  1.7 22.9 %copy-start.5 = (s32[3,4]{1,0:T(4,128)S(1)}, s32[3,4]{1,0:T(4,128)}, u32[]{:S(2)}) copy-start(s32[3,4]{1,0:T(4,128)} %pair.7) | copy-start | bytes 148
  1.7 16.6 %collective-permute-start.3 = (f32[72,768]{1,0:T(8,128)S(1)}, f32[72,768]{1,0:T(8,128)S(1)}, u32[]{:S(2)}, u32[]{:S(2)}) collective-permute-start(f32[72,768]{1,0:T(8,128)S(1)} %get-tuple-element.308), channel_id=1, source_target_pairs={{0,1},{1,0},{2,3},{3,2},{4,5},{5,4},{6,7},{7,6},{8,9},{9,8},{10,11... | collective-permute-start | bytes 663560 | tf_op jit(solution)/shard_map/ppermute | solution.py:440
  10.5 14.1 %collective-permute-start.4 = (f32[72,768]{1,0:T(8,128)S(1)}, f32[72,768]{1,0:T(8,128)S(1)}, u32[]{:S(2)}, u32[]{:S(2)}) collective-permute-start(f32[72,768]{1,0:T(8,128)S(1)} %get-tuple-element.312), channel_id=1, source_target_pairs={{1,2},{2,1},{3,4},{4,3},{5,6},{6,5},{7,8},{8,7},{9,10},{10,9},{11,... | collective-permute-start | bytes 663560 | tf_op jit(solution)/shard_map/ppermute | solution.py:444
  21.0 8.4 %copy-start.3 = (f32[1024]{0:T(1024)S(1)}, f32[1024]{0:T(1024)}, u32[]{:S(2)}) copy-start(f32[1024]{0:T(1024)} %param.17) | copy-start | bytes 12292
  21.0 9.2 %collective-permute-start.5 = (f32[64,768]{1,0:T(8,128)S(1)}, f32[64,768]{1,0:T(8,128)S(1)}, u32[]{:S(2)}, u32[]{:S(2)}) collective-permute-start(f32[64,768]{1,0:T(8,128)S(1)} %get-tuple-element.317), channel_id=1, source_target_pairs={{1,2},{2,1},{3,4},{4,3},{5,6},{6,5},{7,8},{8,7},{9,10},{10,9},{11,... | collective-permute-start | bytes 589832 | tf_op jit(solution)/shard_map/ppermute | solution.py:444
  27.5 3.3 %collective-permute-start.6 = (f32[64,768]{1,0:T(8,128)S(1)}, f32[64,768]{1,0:T(8,128)S(1)}, u32[]{:S(2)}, u32[]{:S(2)}) collective-permute-start(f32[64,768]{1,0:T(8,128)S(1)} %get-tuple-element.319), channel_id=1, source_target_pairs={{0,1},{1,0},{2,3},{3,2},{4,5},{5,4},{6,7},{7,6},{8,9},{9,8},{10,11... | collective-permute-start | bytes 589832 | tf_op jit(solution)/shard_map/ppermute | solution.py:440
  31.9 7.0 %collective-permute-start.7 = (f32[64,768]{1,0:T(8,128)S(1)}, f32[64,768]{1,0:T(8,128)S(1)}, u32[]{:S(2)}, u32[]{:S(2)}) collective-permute-start(f32[64,768]{1,0:T(8,128)S(1)} %get-tuple-element.327), channel_id=1, source_target_pairs={{1,2},{2,1},{3,4},{4,3},{5,6},{6,5},{7,8},{8,7},{9,10},{10,9},{11,... | collective-permute-start | bytes 589832 | tf_op jit(solution)/shard_map/ppermute | solution.py:444
  33.9 5.1 %collective-permute-start.8 = (f32[64,768]{1,0:T(8,128)S(1)}, f32[64,768]{1,0:T(8,128)S(1)}, u32[]{:S(2)}, u32[]{:S(2)}) collective-permute-start(f32[64,768]{1,0:T(8,128)S(1)} %get-tuple-element.328), channel_id=1, source_target_pairs={{0,1},{1,0},{2,3},{3,2},{4,5},{5,4},{6,7},{7,6},{8,9},{9,8},{10,11... | collective-permute-start | bytes 589832 | tf_op jit(solution)/shard_map/ppermute | solution.py:440
  40.3 39.3 %copy-start.2 = (f32[64,1024]{1,0:T(8,128)S(1)}, f32[64,1024]{1,0:T(8,128)}, u32[]{:S(2)}) copy-start(f32[64,1024]{1,0:T(8,128)} %probes.3) | copy-start | bytes 786436
  40.3 39.3 %copy-start.4 = (f32[3,1024]{1,0:T(4,128)S(1)}, f32[3,1024]{1,0:T(4,128)}, u32[]{:S(2)}) copy-start(f32[3,1024]{1,0:T(4,128)} %coords.3) | copy-start | bytes 36868

commit v4 on v3

--- a/solution.py
+++ b/solution.py
@@ -10,6 +10,8 @@
 ITERS = 3
 AXES = ("region", "sub")
 SHIFT = 6.0
+SCALE = 1.0 / 256.0
+FAR = 65536.0
 MAX_AMP = 100.0
 MAX_NORM = 30.0
 F32 = jnp.float32
@@ -107,7 +109,7 @@
     return copies
 
 
-def pack_kernel(coords, pair, probes, to_mate, to_next, points, flags, sem):
+def pack_kernel(coords, pair, probes, to_mate, to_next, own, points, flags, sem):
     links, blocks = pair.shape
     here = coords.shape[1]
     length = here // blocks
@@ -129,6 +131,7 @@
         flag = [flags[k, b].astype(F32) for b in range(blocks)]
         extra.append(jnp.concatenate([jnp.full((1, length), f, F32) for f in flag], axis=1))
     extra = jnp.concatenate(extra + [jnp.zeros((8 - 3 - links, here), F32)], axis=0)
+    own[...] = extra
     low, high = extra[:, 0:span], extra[:, here - span :]
     to_mate[rows : rows + 8, :] = jnp.where(right, high, low)
     to_next[rows : rows + 8, :] = jnp.where(right, low, high)
@@ -142,24 +145,34 @@
         columns[d, at : at + turned.shape[0], :] = jnp.broadcast_to(turned[:, d : d + 1], (turned.shape[0], 128))
 
 
-def fill_strip(columns, from_row, strip, rows, lanes, flag, stores):
-    column = [columns[d, pl.ds(from_row, strip), :].reshape(strip // 8, 8, 128) for d in range(3)]
-    for lane, one_flag, store in zip(lanes, flag, stores):
-        squared = None
-        for d in range(3):
-            away = column[d] - rows[d, :, lane : lane + 128][None]
-            squared = away * away if squared is None else squared + away * away
-        squared = jnp.maximum(squared, 1e-30)
-        distance = squared * lax.rsqrt(squared)
-        support = jnp.maximum(1.0 - distance, 0.0)
-        support = support * support
-        value = support * support * ((4.0 * one_flag)[None] * distance + one_flag[None])
-        store(*split(value.reshape(strip, 128)))
+def fill_tiles(k_high, k_low, to_row, columns, from_row, count, rows, at, first):
+    strip = 64 if at.stop - at.start <= 4 * 128 else 32
+
+    def body(s, _):
+        step = pl.multiple_of(s * strip, strip)
+        column = [columns[d, pl.ds(from_row + step, strip), :].reshape(strip // 8, 8, 128) for d in range(3)]
+        for lane in range(at.start, at.stop, 128):
+            squared = None
+            for d in range(3):
+                away = column[d] - rows[d, :, lane : lane + 128][None]
+                squared = away * away if squared is None else squared + away * away
+            squared = jnp.maximum(squared, 1e-30)
+            distance = squared * lax.rsqrt(squared)
+            support = jnp.maximum(4.0 - distance, 0.0)
+            support = support * support
+            value = support * support * (distance + 1.0)
+            top, rest = split(value.reshape(strip, 128))
+            to = slice(first + lane - at.start, first + lane - at.start + 128)
+            k_high[pl.ds(to_row + step, strip), to] = top
+            k_low[pl.ds(to_row + step, strip), to] = rest
+        return 0
+
+    lax.fori_loop(0, count // strip, body, 0)
 
 
 def store_halves(halves, at, vector):
     rows, size = vector.shape
-    top, rest = split(vector)
+    top, rest = split(vector * SCALE)
     halves[0:rows, at : at + size] = top
     halves[rows : 2 * rows, at : at + size] = rest
 
@@ -172,112 +185,75 @@
     return most[0:rows] + (most[rows : 2 * rows] + rest)
 
 
-def local_product(noise, vector, k_high, k_low, out, halves):
-    blocks, _, length = k_high.shape
+def local_product(noise, vector, k_high, k_low, out, halves, length):
+    here = vector.shape[1]
     store_halves(halves, 0, vector[...])
-    for i in range(blocks):
-        at = slice(i * length, (i + 1) * length)
-        value = multiply(halves[...], k_high[i], k_low[i])
+    for start in range(0, here, length):
+        stop = start + length
+        at, before, after = slice(start, stop), slice(0, stop), slice(stop, here)
+        value = multiply(halves[:, before], k_high[before, at], k_low[before, at])
+        if stop < here:
+            value = value + multiply(halves[:, after], k_high[at, after], k_low[at, after], turned=True)
         out[:, at] = value + (noise[:, at] - SHIFT) * vector[:, at]
 
 
-def local_first_kernel(coords, noise, pair, probes, k_high, k_low, out, first, columns, halves, rows, flags, sem):
-    links, blocks = pair.shape
-    here = probes.shape[1]
+def local_first_kernel(own, noise, probes, k_high, k_low, out, first, columns, halves, rows, sem, *, links):
+    here = own.shape[1]
+    blocks = links + 1
     length = here // blocks
     copy = pltpu.make_async_copy(probes, first, sem.at[0])
     copy.start()
     for j in range(blocks):
-        own = coords[:, j * length : (j + 1) * length]
-        fill_columns(columns, j * length, jnp.concatenate([own, jnp.zeros((5, length), F32)], axis=0))
-    for d in range(3):
-        rows[d] = jnp.broadcast_to(coords[d : d + 1, :], rows.shape[1:])
-    for j in range(blocks):
-        for i in range(blocks):
-            if i == j:
-                flag = 1.0
-            elif abs(i - j) <= links:
-                flag = pair[abs(i - j) - 1, min(i, j)].astype(F32)
-            else:
-                flag = 0.0
-            flags[j, :, i * length : (i + 1) * length] = jnp.full((8, length), flag, F32)
-    strip = 32
-
-    def store_to(i, row, lane):
-        def store(top, rest):
-            k_high[i, pl.ds(row, strip), lane : lane + 128] = top
-            k_low[i, pl.ds(row, strip), lane : lane + 128] = rest
-
-        return store
-
-    def body(s, _):
-        row = pl.multiple_of(s * strip, strip)
-        block = s // (length // strip)
-        lanes = list(range(0, here, 128))
-        fill_strip(
-            columns,
-            row,
-            strip,
-            rows,
-            lanes,
-            [flags[block, :, lane : lane + 128] for lane in lanes],
-            [store_to(lane // length, row, lane % length) for lane in lanes],
-        )
-        return 0
-
-    lax.fori_loop(0, here // strip, body, 0)
+        fill_columns(columns, j * length, 4.0 * own[:, j * length : (j + 1) * length])
+    for d in range(1, 3):
+        rows[d] = jnp.broadcast_to(4.0 * own[d : d + 1, :], rows.shape[1:])
+    for i in range(blocks):
+        for j in range(i, blocks):
+            at = slice(j * length, (j + 1) * length)
+            moved = 4.0 * own[0:1, at]
+            if j > i:
+                flag = own[2 + j - i : 3 + j - i, i * length : (i + 1) * length]
+                moved = jnp.where(flag == 1.0, moved, moved + FAR)
+            rows[0, :, at] = jnp.broadcast_to(moved, (8, length))
+        fill_tiles(k_high, k_low, i * length, columns, i * length, length, rows, slice(i * length, here), i * length)
     copy.wait()
-    local_product(noise, first, k_high, k_low, out, halves)
-
-
-def fill_halo(right, pair, received, columns, k_high, k_low, rows):
-    links, blocks = pair.shape
-    span = received.shape[1]
-    length = span // links
+    local_product(noise, first, k_high, k_low, out, halves, length)
+
+
+def fill_halo(right, own, received, columns, tables, rows, links):
+    length = received.shape[1] // links
+    blocks = own.shape[1] // length
     at = received.shape[0] - 8
     place = [pl.ds(halo_place(right, links, length, h), length) for h in range(links)]
-    for h in range(links):
-        for d in range(3):
-            coord = received[at + d : at + d + 1, place[h]]
+    for h in range(max(tables)):
+        for d in range(1, 3):
+            coord = 4.0 * received[at + d : at + d + 1, place[h]]
             rows[d, :, h * length : (h + 1) * length] = jnp.broadcast_to(coord, (8, length))
-    for n in range(1, links + 1):
-        own = own_place(right, blocks, links, length, n)
-        lower = jnp.where(right, blocks - 1 - links + n, 0)
-        flags = []
+    for n, (k_high, k_low) in tables.items():
+        mine = own_place(right, blocks, links, length, n)
         for h in range(n):
             k = links - n + h
-            ours = jnp.full((1, 128), pair[k, lower].astype(F32), F32)
-            theirs = received[at + 3 + k : at + 4 + k, place[h]][:, 0:128]
-            flags += [jnp.broadcast_to(jnp.where(right, ours, theirs), (8, 128))] * (length // 128)
-        lanes = list(range(0, n * length, 128))
-        strip = 32 if n > 2 else 64
-
-        def store_to(row, lane):
-            def store(top, rest):
-                k_high[pl.ds(row, strip), lane : lane + 128] = top
-                k_low[pl.ds(row, strip), lane : lane + 128] = rest
-
-            return store
-
-        def body(s, _):
-            step = pl.multiple_of(s * strip, strip)
-            stores = [store_to((n - 1) * length + step, lane) for lane in lanes]
-            fill_strip(columns, pl.multiple_of(own + step, strip), strip, rows, lanes, flags, stores)
-            return 0
-
-        lax.fori_loop(0, length // strip, body, 0)
-
-
-def halo_product(right, load, k_high, k_low, out, halves, blocks):
-    span = k_high.shape[0]
-    length = out.shape[1] // blocks
-    links = span // length
-    for h in range(links):
+            ours = own[3 + k : 4 + k, pl.ds(mine, length)]
+            theirs = received[at + 3 + k : at + 4 + k, place[h]]
+            coord = 4.0 * received[at : at + 1, place[h]]
+            coord = jnp.where(jnp.where(right, ours, theirs) == 1.0, coord, coord + FAR)
+            rows[0, :, h * length : (h + 1) * length] = jnp.broadcast_to(coord, (8, length))
+        fill_tiles(k_high, k_low, 0, columns, mine, length, rows, slice(0, n * length), 0)
+
+
+def table_rows(k_high, k_low, ns, length):
+    parts = {n: (pl.ds((n - ns[0]) * length, length), slice(0, n * length)) for n in ns}
+    return {n: (k_high.at[part], k_low.at[part]) for n, part in parts.items()}
+
+
+def halo_product(right, load, tables, out, halves, links):
+    length = halves.shape[1] // links
+    blocks = out.shape[1] // length
+    for h in range(max(tables)):
         store_halves(halves, h * length, load(pl.ds(halo_place(right, links, length, h), length)))
-    for n in range(1, links + 1):
-        deep, at = slice(0, n * length), slice((n - 1) * length, n * length)
+    for n, (k_high, k_low) in tables.items():
         own = pl.ds(own_place(right, blocks, links, length, n), length)
-        out[:, own] = out[:, own] + multiply(halves[:, deep], k_high[at, deep], k_low[at, deep], turned=True)
+        out[:, own] = out[:, own] + multiply(halves[:, 0 : n * length], k_high[...], k_low[...], turned=True)
 
 
 def own_product(right, vector, k_high, k_low, out, halves, blocks):
@@ -298,25 +274,33 @@
     send[...] = vector[:, pl.ds(send_place(right, here, span), span)]
 
 
-def mate_first_kernel(pair, partial, received, columns, k_high, k_low, out, to_next, halves, rows):
+def mate_first_kernel(own, partial, received, columns, k_high, k_low, out, to_next, halves, rows, *, links):
     probe_count = out.shape[0]
     right = is_right(True)
-    fill_halo(right, pair, received, columns, k_high, k_low, rows)
+    length = halves.shape[1] // links
+    tables = table_rows(k_high, k_low, range(1, links), length)
+    fill_halo(right, own, received, columns, tables, rows, links)
     out[...] = partial[...]
-    halo_product(right, lambda at: received[0:probe_count, at], k_high, k_low, out, halves, pair.shape[1])
+    halo_product(right, lambda at: received[0:probe_count, at], tables, out, halves, links)
     store_send(is_right(False), out, to_next)
 
 
 def next_first_kernel(
-    pair, partial, first, received, columns, k_high, k_low, out, given, to_mate, halves, rows
+    own, partial, first, mate, received, columns, mate_high, mate_low, k_high, k_low, out, given, to_mate, halves, rows, *, links
 ):
     probe_count = out.shape[0]
+    length = halves.shape[1] // links
+    out[...] = partial[...]
+    right = is_right(True)
+    tables = table_rows(mate_high, mate_low, range(links, links + 1), length)
+    fill_halo(right, own, mate, columns, tables, rows, links)
+    halo_product(right, lambda at: mate[0:probe_count, at], tables, out, halves, links)
     right = is_right(False)
-    fill_halo(right, pair, received, columns, k_high, k_low, rows)
-    out[...] = partial[...]
-    halo_product(right, lambda at: received[0:probe_count, at], k_high, k_low, out, halves, pair.shape[1])
+    tables = table_rows(k_high, k_low, range(1, links + 1), length)
+    fill_halo(right, own, received, columns, tables, rows, links)
+    halo_product(right, lambda at: received[0:probe_count, at], tables, out, halves, links)
     store_send(is_right(True), out, to_mate)
-    own_product(right, first, k_high, k_low, given, halves, pair.shape[1])
+    own_product(right, first, k_high, k_low, given, halves, links + 1)
 
 
 def add_sums(table, terms):
@@ -330,32 +314,35 @@
     return table
 
 
-def local_second_kernel(noise, first, second, k_high, k_low, out, table, halves):
-    local_product(noise, second, k_high, k_low, out, halves)
+def local_second_kernel(noise, first, second, k_high, k_low, out, table, halves, *, length):
+    local_product(noise, second, k_high, k_low, out, halves, length)
     table[...] = add_sums(jnp.zeros(table.shape, F32), ((0, first, first), (1, first, second), (2, second, second)))
 
 
-def local_third_kernel(noise, second, third, table_in, k_high, k_low, out, table, halves):
-    local_product(noise, third, k_high, k_low, out, halves)
+def local_third_kernel(noise, second, third, table_in, k_high, k_low, out, table, halves, *, length):
+    local_product(noise, third, k_high, k_low, out, halves, length)
     table[...] = add_sums(table_in[...], ((3, second, third), (4, third, third)))
 
 
-def halo_second_kernel(
-    partial, beyond, given, mate, mate_high, mate_low, next_high, next_low, out, to_next, to_mate, halves, *, blocks
-):
+def both_products(partial, beyond, mate, tables, out, halves, links):
+    length = halves.shape[1] // links
     out[...] = partial[...]
-    halo_product(is_right(True), lambda at: mate[:, at], mate_high, mate_low, out, halves, blocks)
-    halo_product(is_right(False), lambda at: beyond[:, at] + given[:, at], next_high, next_low, out, halves, blocks)
+    mate_tables = table_rows(*tables[0:2], range(1, links), length)
+    mate_tables.update(table_rows(*tables[2:4], range(links, links + 1), length))
+    halo_product(is_right(True), lambda at: mate[:, at], mate_tables, out, halves, links)
+    halo_product(is_right(False), beyond, table_rows(*tables[4:6], range(1, links + 1), length), out, halves, links)
+
+
+def halo_second_kernel(partial, beyond, given, mate, *rest, links):
+    tables, (out, to_next, to_mate, halves) = rest[0:6], rest[6:]
+    both_products(partial, lambda at: beyond[:, at] + given[:, at], mate, tables, out, halves, links)
     store_send(is_right(False), out, to_next)
     store_send(is_right(True), out, to_mate)
 
 
-def halo_third_kernel(
-    partial, beyond, mate, mate_high, mate_low, next_high, next_low, third, table, out, sums, halves, *, blocks
-):
-    out[...] = partial[...]
-    halo_product(is_right(True), lambda at: mate[:, at], mate_high, mate_low, out, halves, blocks)
-    halo_product(is_right(False), lambda at: beyond[:, at], next_high, next_low, out, halves, blocks)
+def halo_third_kernel(partial, beyond, mate, *rest, links):
+    tables, (third, table, out, sums, halves) = rest[0:6], rest[6:]
+    both_products(partial, lambda at: beyond[:, at], mate, tables, out, halves, links)
     full = add_sums(table[...], ((5, third, out), (6, out, out)))
     turned = jnp.transpose(full)[0:8, :]
     compact = jnp.concatenate([turned[0:4], turned[4:8]], axis=1)
@@ -455,64 +442,70 @@
     part = jax.ShapeDtypeStruct((rows, span), F32)
     packed = jax.ShapeDtypeStruct((rows + 8, span), F32)
     sums_table = jax.ShapeDtypeStruct((rows, 128), F32)
-    local_table = jax.ShapeDtypeStruct((blocks, here, length), BF16)
+    local_table = jax.ShapeDtypeStruct((here, here), BF16)
     halo_table = jax.ShapeDtypeStruct((span, span), BF16)
     local_halves = pltpu.VMEM((2 * rows, here), BF16)
     halo_halves = pltpu.VMEM((2 * rows, span), BF16)
 
-    to_mate, to_next = call(
+    to_mate, to_next, own = call(
         pack_kernel,
         "pack",
-        (packed, packed),
+        (packed, packed, jax.ShapeDtypeStruct((8, here), F32)),
         [ANY, ANY, ANY],
         [pltpu.VMEM((3, here), F32), pltpu.SMEM((links, blocks), jnp.int32), pltpu.SemaphoreType.DMA((4,))],
     )(coords, pair_list, probes)
     mate, beyond = swap_mate(to_mate), swap_next(to_next)
     k_high, k_low, partial, first, columns = call(
-        local_first_kernel,
+        functools.partial(local_first_kernel, links=links),
         "local_first",
         (local_table, local_table, whole, whole, jax.ShapeDtypeStruct((3, here, 128), F32)),
-        [VMEM, VMEM, SMEM, ANY],
+        [VMEM, VMEM, ANY],
         [
             local_halves,
             pltpu.VMEM((3, 8, here), F32),
-            pltpu.VMEM((blocks, 8, here), F32),
             pltpu.SemaphoreType.DMA((1,)),
         ],
-    )(coords, noise, pair_list, probes)
+    )(own, noise, probes)
     halo_scratch = [halo_halves, pltpu.VMEM((3, 8, span), F32)]
-    mate_high, mate_low, partial, to_next = call(
-        mate_first_kernel, "mate_first", (halo_table, halo_table, whole, part), [SMEM, VMEM, VMEM, VMEM], halo_scratch
-    )(pair_list, partial, mate, columns)
+    early_table = jax.ShapeDtypeStruct((span - length, span - length), BF16)
+    late_table = jax.ShapeDtypeStruct((length, span), BF16)
+    early_high, early_low, partial, to_next = call(
+        functools.partial(mate_first_kernel, links=links),
+        "mate_first",
+        (early_table, early_table, whole, part),
+        [VMEM] * 4,
+        halo_scratch,
+    )(own, partial, mate, columns)
     ahead = swap_next(to_next)
-    next_high, next_low, second, given, to_mate = call(
-        next_first_kernel,
+    late_high, late_low, next_high, next_low, second, given, to_mate = call(
+        functools.partial(next_first_kernel, links=links),
         "next_first",
-        (halo_table, halo_table, whole, part, part),
-        [SMEM, VMEM, VMEM, VMEM, VMEM],
+        (late_table, late_table, halo_table, halo_table, whole, part, part),
+        [VMEM] * 6,
         halo_scratch,
-    )(pair_list, partial, first, beyond, columns)
+    )(own, partial, first, mate, beyond, columns)
+    tables = (early_high, early_low, late_high, late_low, next_high, next_low)
 
     mate = swap_mate(to_mate)
-    partial, table = call(local_second_kernel, "local_second", (whole, sums_table), [VMEM] * 5, [local_halves])(
-        noise, first, second, k_high, k_low
-    )
+    partial, table = call(
+        functools.partial(local_second_kernel, length=length), "local_second", (whole, sums_table), [VMEM] * 5, [local_halves]
+    )(noise, first, second, k_high, k_low)
     third, to_next, to_mate = call(
-        functools.partial(halo_second_kernel, blocks=blocks), "halo_second", (whole, part, part), [VMEM] * 8, [halo_halves]
-    )(partial, ahead, given, mate, mate_high, mate_low, next_high, next_low)
+        functools.partial(halo_second_kernel, links=links), "halo_second", (whole, part, part), [VMEM] * 10, [halo_halves]
+    )(partial, ahead, given, mate, *tables)
 
     beyond, mate = swap_next(to_next), swap_mate(to_mate)
-    partial, table = call(local_third_kernel, "local_third", (whole, sums_table), [VMEM] * 6, [local_halves])(
-        noise, second, third, table, k_high, k_low
-    )
+    partial, table = call(
+        functools.partial(local_third_kernel, length=length), "local_third", (whole, sums_table), [VMEM] * 6, [local_halves]
+    )(noise, second, third, table, k_high, k_low)
     regions, subs = lax.axis_size("region"), lax.axis_size("sub")
     fourth, sums = call(
-        functools.partial(halo_third_kernel, blocks=blocks),
+        functools.partial(halo_third_kernel, links=links),
         "halo_third",
         (whole, jax.ShapeDtypeStruct((regions, 4, 128), F32)),
-        [VMEM] * 9,
+        [VMEM] * 11,
         [halo_halves],
-    )(partial, beyond, mate, mate_high, mate_low, next_high, next_low, third, table)
+    )(partial, beyond, mate, *tables, third, table)
 
     sums = jnp.sum(lax.all_to_all(sums, "region", 0, 0), axis=0)
     sums = lax.all_to_all(jnp.broadcast_to(sums[None], (subs, 4, 128)), "sub", 0, 0)

time: 81 us -> 77.9 us (0.962)
  Pallas kernels: 17.6 us -> 16.1 us
  blocking collectives: 38 us -> 37 us
    pallas_call x8, Pallas kernels: 16.4 us -> 14.9 us  [the longest x1 4.59 us: per_device(): call(functools.partial(local_first_kernel, links=links), 'local_first', (...]
    all_to_all x1, blocking collectives: 16 us -> 15.2 us  [per_device(): lax.all_to_all(jnp.broadcast_to(sums[None], (subs, 4, 128)), 'sub', 0, 0)]
  transfers between devices with their start and end apart: 6 -> 6, of which waited for: 2 -> 2; matrix products, arithmetic and copies ran while one was open for 0% -> 0% of each run, Pallas kernels for 16% -> 15%
where the time goes in v4:
time: 77.9 us; the launch traced here: 77.5 us
  blocking collectives  37 us (47%)
  starting transfers between devices  20.1 us (26%)
  Pallas kernels  16.1 us (21%)
  waiting for transfers between devices  2.47 us (3%)
  between operations  0.97 us (1%)
  loops' own time  0.81 us (1%)
    all_to_all x1, blocking collectives, per_device(): sums = jnp.sum(lax.all_to_all(sums, 'region', 0, 0), axis=0)  21.8 us
    all_to_all x1, blocking collectives, per_device(): lax.all_to_all(jnp.broadcast_to(sums[None], (subs, 4, 128)), 'sub', 0, 0)  15.2 us
    ppermute x3, starting transfers between devices, swap_mate(): lax.ppermute(array, AXES, [(i, i ^ 1) for i in range(lax.axis_size(AXES))])  12.6 us
    ppermute x3, starting transfers between devices, swap_next(): lax.ppermute(array, AXES, [(i, i + 1 if i % 2 else i - 1) for i in range(...  7.48 us
    pallas_call x1, Pallas kernels, per_device(): call(functools.partial(local_first_kernel, links=links), 'local_first', (...  4.59 us
    pallas_call x1, Pallas kernels, per_device(): call(functools.partial(next_first_kernel, links=links), 'next_first', (la...  3.61 us
    ppermute x3, waiting for transfers between devices, swap_next(): lax.ppermute(array, AXES, [(i, i + 1 if i % 2 else i - 1) for i in range(...  2.11 us
  transfers between devices with their start and end apart: 6, of which 2 were waited for; matrix products, arithmetic and copies ran while one was open for 0% of the time, Pallas kernels for 15%

profile of v4, /device:TPU:1, one launch (start us, length us, event | category | flops | bytes accessed | tf_op | source)
XLA Modules:
  0.0 77.5 jit_solution(3570292198621036046)
XLA Ops:
  0.6 1.1 %pack.1 = (f32[72,768]{1,0:T(8,128)S(1)}, f32[72,768]{1,0:T(8,128)S(1)}, f32[8,1024]{1,0:T(8,128)S(1)}) custom-call(f32[3,1024]{1,0:T(4,128)} %coords.1, s32[3,4]{1,0:T(4,128)} %pair.1, f32[64,1024]{1,0:T(8,128)} %probes.3), custom_call_target="tpu_custom_call" | custom-call | tf_op jit(solution)/shard_map/pack/pallas_call | solution.py:450
  1.7 8.8 %collective-permute-start.3 = (f32[72,768]{1,0:T(8,128)S(1)}, f32[72,768]{1,0:T(8,128)S(1)}, u32[]{:S(2)}, u32[]{:S(2)}) collective-permute-start(f32[72,768]{1,0:T(8,128)S(1)} %get-tuple-element.312), channel_id=1, source_target_pairs={{0,1},{1,0},{2,3},{3,2},{4,5},{5,4},{6,7},{7,6},{8,9},{9,8},{10,11... | collective-permute-start | bytes 663560 | tf_op jit(solution)/shard_map/ppermute | solution.py:427
  10.5 1.9 %collective-permute-start.4 = (f32[72,768]{1,0:T(8,128)S(1)}, f32[72,768]{1,0:T(8,128)S(1)}, u32[]{:S(2)}, u32[]{:S(2)}) collective-permute-start(f32[72,768]{1,0:T(8,128)S(1)} %get-tuple-element.316), channel_id=1, source_target_pairs={{1,2},{2,1},{3,4},{4,3},{5,6},{6,5},{7,8},{8,7},{9,10},{10,9},{11,... | collective-permute-start | bytes 663560 | tf_op jit(solution)/shard_map/ppermute | solution.py:431
  12.4 4.6 %local_first.1 = (bf16[1024,1024]{1,0:T(8,128)(2,1)S(1)}, bf16[1024,1024]{1,0:T(8,128)(2,1)S(1)}, f32[64,1024]{1,0:T(8,128)S(1)}, f32[64,1024]{1,0:T(8,128)S(1)}, f32[3,1024,128]{2,1,0:T(8,128)S(1)}) custom-call(f32[8,1024]{1,0:T(8,128)S(1)} %get-tuple-element.310.own, f32[1,1024]{1,0:T(1,128)} %bitcast.97, f32[64,1024]{1,0:T(8,128)} %probes.3), custom_call_target="tpu_custom_call" | custom-call | tf_op jit(solution)/shard_map/local_first/pallas_call | solution.py:458
  17.0 0.0 collective-permute-done.3.received.mate
  17.0 1.1 %mate_first.1 = (bf16[512,512]{1,0:T(8,128)(2,1)S(1)}, bf16[512,512]{1,0:T(8,128)(2,1)S(1)}, f32[64,1024]{1,0:T(8,128)S(1)}, f32[64,768]{1,0:T(8,128)S(1)}) custom-call(f32[8,1024]{1,0:T(8,128)S(1)} %get-tuple-element.310.own, f32[64,1024]{1,0:T(8,128)S(1)} %get-tuple-element.311.partial, f32[72,768]{1,0:T(8,128)S(1)} %collective-permute-done.3.received.mate, ...), custom_call_target="tpu_custom_call" | custom-call | tf_op jit(solution)/shard_map/mate_first/pallas_call | solution.py:472
  18.1 0.0 copy-start.3
  18.1 3.6 %collective-permute-start.5 = (f32[64,768]{1,0:T(8,128)S(1)}, f32[64,768]{1,0:T(8,128)S(1)}, u32[]{:S(2)}, u32[]{:S(2)}) collective-permute-start(f32[64,768]{1,0:T(8,128)S(1)} %get-tuple-element.321), channel_id=1, source_target_pairs={{1,2},{2,1},{3,4},{4,3},{5,6},{6,5},{7,8},{8,7},{9,10},{10,9},{11,... | collective-permute-start | bytes 589832 | tf_op jit(solution)/shard_map/ppermute | solution.py:431
  21.8 0.0 collective-permute-done.4.received
  21.8 3.6 %next_first.1 = (bf16[256,768]{1,0:T(8,128)(2,1)S(1)}, bf16[256,768]{1,0:T(8,128)(2,1)S(1)}, bf16[768,768]{1,0:T(8,128)(2,1)S(1)}, bf16[768,768]{1,0:T(8,128)(2,...) custom-call(f32[8,1024]{1,0:T(8,128)S(1)} %get-tuple-element.310.own, ...), custom_call_target="tpu_custom_call" | custom-call | tf_op jit(solution)/shard_map/next_first/pallas_call | solution.py:480
  25.4 1.9 %collective-permute-start.6 = (f32[64,768]{1,0:T(8,128)S(1)}, f32[64,768]{1,0:T(8,128)S(1)}, u32[]{:S(2)}, u32[]{:S(2)}) collective-permute-start(f32[64,768]{1,0:T(8,128)S(1)} %get-tuple-element.323), channel_id=1, source_target_pairs={{0,1},{1,0},{2,3},{3,2},{4,5},{5,4},{6,7},{7,6},{8,9},{9,8},{10,11... | collective-permute-start | bytes 589832 | tf_op jit(solution)/shard_map/ppermute | solution.py:427
  27.3 0.0 copy-done.3
  27.4 1.0 %local_second.1 = (f32[64,1024]{1,0:T(8,128)S(1)}, f32[64,128]{1,0:T(8,128)S(1)}) custom-call(f32[1,1024]{1,0:T(1,128)S(1)} %bitcast.98, f32[64,1024]{1,0:T(8,128)S(1)} %get-tuple-element.315.first, f32[64,1024]{1,0:T(8,128)S(1)} %get-tuple-element.317.second, bf16[1024,1024]{1,0:T(8,128)(2,1)S(1)} %get-tuple-element.318.k_high, ...), custom_call_target="tpu_custom_call" | custom-call | tf_op jit(solution)/shard_map/local_second/pallas_call | solution.py:490
  28.4 0.0 collective-permute-done.5.beyond
  28.4 0.4 collective-permute-done.6.mate
  28.8 1.1 %halo_second.1 = (f32[64,1024]{1,0:T(8,128)S(1)}, f32[64,768]{1,0:T(8,128)S(1)}, f32[64,768]{1,0:T(8,128)S(1)}) custom-call(f32[64,1024]{1,0:T(8,128)S(1)} %get-tuple-element.320.partial, f32[64,768]{1,0:T(8,128)S(1)} %collective-permute-done.5.beyond, f32[64,768]{1,0:T(8,128)S(1)} %get-tuple-element.322.given, f32[64,768]{1,0:T(8,128)S(1)} %collective-permute-done.6.mate, ...), custom_call_target="tpu_custom_call" | custom-call | tf_op jit(solution)/shard_map/halo_second/pallas_call | solution.py:493
  29.9 1.9 %collective-permute-start.7 = (f32[64,768]{1,0:T(8,128)S(1)}, f32[64,768]{1,0:T(8,128)S(1)}, u32[]{:S(2)}, u32[]{:S(2)}) collective-permute-start(f32[64,768]{1,0:T(8,128)S(1)} %get-tuple-element.333), channel_id=1, source_target_pairs={{1,2},{2,1},{3,4},{4,3},{5,6},{6,5},{7,8},{8,7},{9,10},{10,9},{11,... | collective-permute-start | bytes 589832 | tf_op jit(solution)/shard_map/ppermute | solution.py:431
  31.8 1.9 %collective-permute-start.8 = (f32[64,768]{1,0:T(8,128)S(1)}, f32[64,768]{1,0:T(8,128)S(1)}, u32[]{:S(2)}, u32[]{:S(2)}) collective-permute-start(f32[64,768]{1,0:T(8,128)S(1)} %get-tuple-element.334), channel_id=1, source_target_pairs={{0,1},{1,0},{2,3},{3,2},{4,5},{5,4},{6,7},{7,6},{8,9},{9,8},{10,11... | collective-permute-start | bytes 589832 | tf_op jit(solution)/shard_map/ppermute | solution.py:427
  33.8 1.0 %local_third.1 = (f32[64,1024]{1,0:T(8,128)S(1)}, f32[64,128]{1,0:T(8,128)S(1)}) custom-call(f32[1,1024]{1,0:T(1,128)S(1)} %bitcast.99, f32[64,1024]{1,0:T(8,128)S(1)} %get-tuple-element.317.second, f32[64,1024]{1,0:T(8,128)S(1)} %get-tuple-element.330.third.rest_6_, f32[64,128]{1,0:T(8,128)S(1)} %get-tuple-element.331.table_in, ...), custom_call_target="tpu_custom_call" | custom-call | tf_op jit(solution)/shard_map/local_third/pallas_call | solution.py:498
  34.8 2.1 %collective-permute-done.7.beyond = f32[64,768]{1,0:T(8,128)S(1)} collective-permute-done((f32[64,768]{1,0:T(8,128)S(1)}, f32[64,768]{1,0:T(8,128)S(1)}, u32[]{:S(2)}, u32[]{:S(2)}) %collective-permute-start.7) | collective-permute-done | bytes 196640 | tf_op jit(solution)/shard_map/ppermute | solution.py:431
  36.9 0.0 collective-permute-done.8.mate
  36.9 0.0 copy-start.2
  36.9 0.0 copy-start.4
  36.9 0.0 copy-start.5
  36.9 1.4 %halo_third.1 = (f32[64,1024]{1,0:T(8,128)S(1)}, f32[32,4,128]{2,1,0:T(4,128)S(1)}) custom-call(f32[64,1024]{1,0:T(8,128)S(1)} %get-tuple-element.332.partial, f32[64,768]{1,0:T(8,128)S(1)} %collective-permute-done.7.beyond, f32[64,768]{1,0:T(8,128)S(1)} %collective-permute-done.8.mate, bf16[512,512]{1,0:T(8,128)(2,1)S(1)} %get-tuple-element.324.rest_0_, ...), custom_call_target="tpu_custom_call" | custom-call | tf_op jit(solution)/shard_map/halo_third/pallas_call | solution.py:502
  38.3 21.8 %all_to_all.10 = f32[32,4,128]{2,1,0:T(4,128)S(1)} all-to-all(f32[32,4,128]{2,1,0:T(4,128)S(1)} %get-tuple-element.336), channel_id=1, replica_groups=mesh['region'=32,'sub'=16] {'region'}, dimensions={0} | all-to-all | bytes 131072 | tf_op jit(solution)/shard_map/all_to_all | solution.py:510
  60.2 15.2 %all_to_all.11.sums = f32[16,4,128]{2,1,0:T(4,128)S(1)} all-to-all(f32[16,4,128]{2,1,0:T(4,128)S(1)} %broadcast_in_dim.5), channel_id=1, replica_groups=mesh['region'=32,'sub'=16] {'sub'}, dimensions={0} | all-to-all | bytes 65536 | tf_op jit(solution)/shard_map/all_to_all | solution.py:511
  75.3 1.2 %finish.1 = (f32[64,1024]{1,0:T(8,128)}, f32[64,1024]{1,0:T(8,128)}, f32[1,1]{1,0:T(1,128)}) custom-call(f32[16,4,128]{2,1,0:T(4,128)S(1)} %all_to_all.11.sums, f32[64,1024]{1,0:T(8,128)S(1)} %get-tuple-element.315.first, f32[64,1024]{1,0:T(8,128)S(1)} %get-tuple-element.317.second, f32[64,1024]{1,0:T(8,128)S(1)} %get-tuple-element.330.third.rest_6_, ...), custom_call_target="tpu_custom_call" | custom-call | tf_op jit(solution)/shard_map/finish/pallas_call | solution.py:512
  76.5 0.0 copy-done.2
  76.5 0.0 copy-done.4
  76.5 0.0 copy-done.5
  76.6 0.8 %while.35 = (f32[1,1]{1,0:T(1,128)}, f32[64,1024]{1,0:T(8,128)}, f32[64,1024]{1,0:T(8,128)}, f32[64,1024]{1,0:T(8,128)S(1)}, f32[3,1024]{1,0:T(4,128)S(1)}, /*in...) while((f32[1,1]{1,0:T(1,128)}, f32[64,1024]{1,0:T(8,128)}, f32[64,1024]{1,0:T(8,128)}, ...), condition=%region_10.11_spmd, body=%region_1.10_spmd | while | flops 1439929600 | bytes 21131516 | solution.py:524
  (2 shorter events, 0.1 us)
Async XLA Ops:
  1.7 15.3 %collective-permute-start.3 = (f32[72,768]{1,0:T(8,128)S(1)}, f32[72,768]{1,0:T(8,128)S(1)}, u32[]{:S(2)}, u32[]{:S(2)}) collective-permute-start(f32[72,768]{1,0:T(8,128)S(1)} %get-tuple-element.312), channel_id=1, source_target_pairs={{0,1},{1,0},{2,3},{3,2},{4,5},{5,4},{6,7},{7,6},{8,9},{9,8},{10,11... | collective-permute-start | bytes 663560 | tf_op jit(solution)/shard_map/ppermute | solution.py:427
  10.5 11.3 %collective-permute-start.4 = (f32[72,768]{1,0:T(8,128)S(1)}, f32[72,768]{1,0:T(8,128)S(1)}, u32[]{:S(2)}, u32[]{:S(2)}) collective-permute-start(f32[72,768]{1,0:T(8,128)S(1)} %get-tuple-element.316), channel_id=1, source_target_pairs={{1,2},{2,1},{3,4},{4,3},{5,6},{6,5},{7,8},{8,7},{9,10},{10,9},{11,... | collective-permute-start | bytes 663560 | tf_op jit(solution)/shard_map/ppermute | solution.py:431
  18.1 9.2 %copy-start.3 = (f32[1024]{0:T(1024)S(1)}, f32[1024]{0:T(1024)}, u32[]{:S(2)}) copy-start(f32[1024]{0:T(1024)} %param.17) | copy-start | bytes 12292
  18.1 10.3 %collective-permute-start.5 = (f32[64,768]{1,0:T(8,128)S(1)}, f32[64,768]{1,0:T(8,128)S(1)}, u32[]{:S(2)}, u32[]{:S(2)}) collective-permute-start(f32[64,768]{1,0:T(8,128)S(1)} %get-tuple-element.321), channel_id=1, source_target_pairs={{1,2},{2,1},{3,4},{4,3},{5,6},{6,5},{7,8},{8,7},{9,10},{10,9},{11,... | collective-permute-start | bytes 589832 | tf_op jit(solution)/shard_map/ppermute | solution.py:431
  25.4 3.3 %collective-permute-start.6 = (f32[64,768]{1,0:T(8,128)S(1)}, f32[64,768]{1,0:T(8,128)S(1)}, u32[]{:S(2)}, u32[]{:S(2)}) collective-permute-start(f32[64,768]{1,0:T(8,128)S(1)} %get-tuple-element.323), channel_id=1, source_target_pairs={{0,1},{1,0},{2,3},{3,2},{4,5},{5,4},{6,7},{7,6},{8,9},{9,8},{10,11... | collective-permute-start | bytes 589832 | tf_op jit(solution)/shard_map/ppermute | solution.py:427
  29.9 7.0 %collective-permute-start.7 = (f32[64,768]{1,0:T(8,128)S(1)}, f32[64,768]{1,0:T(8,128)S(1)}, u32[]{:S(2)}, u32[]{:S(2)}) collective-permute-start(f32[64,768]{1,0:T(8,128)S(1)} %get-tuple-element.333), channel_id=1, source_target_pairs={{1,2},{2,1},{3,4},{4,3},{5,6},{6,5},{7,8},{8,7},{9,10},{10,9},{11,... | collective-permute-start | bytes 589832 | tf_op jit(solution)/shard_map/ppermute | solution.py:431
  31.8 5.1 %collective-permute-start.8 = (f32[64,768]{1,0:T(8,128)S(1)}, f32[64,768]{1,0:T(8,128)S(1)}, u32[]{:S(2)}, u32[]{:S(2)}) collective-permute-start(f32[64,768]{1,0:T(8,128)S(1)} %get-tuple-element.334), channel_id=1, source_target_pairs={{0,1},{1,0},{2,3},{3,2},{4,5},{5,4},{6,7},{7,6},{8,9},{9,8},{10,11... | collective-permute-start | bytes 589832 | tf_op jit(solution)/shard_map/ppermute | solution.py:427
  36.9 39.6 %copy-start.2 = (f32[64,1024]{1,0:T(8,128)S(1)}, f32[64,1024]{1,0:T(8,128)}, u32[]{:S(2)}) copy-start(f32[64,1024]{1,0:T(8,128)} %probes.3) | copy-start | bytes 786436
  36.9 39.6 %copy-start.4 = (f32[3,1024]{1,0:T(4,128)S(1)}, f32[3,1024]{1,0:T(4,128)}, u32[]{:S(2)}) copy-start(f32[3,1024]{1,0:T(4,128)} %coords.1) | copy-start | bytes 36868
  36.9 39.6 %copy-start.5 = (s32[3,4]{1,0:T(4,128)S(1)}, s32[3,4]{1,0:T(4,128)}, u32[]{:S(2)}) copy-start(s32[3,4]{1,0:T(4,128)} %pair.1) | copy-start | bytes 148

commit v5 on v4

--- a/solution.py
+++ b/solution.py
@@ -271,7 +271,10 @@
 
 def store_send(right, vector, send):
     here, span = vector.shape[1], send.shape[1]
-    send[...] = vector[:, pl.ds(send_place(right, here, span), span)]
+    rows = vector.shape[0]
+    send[0:rows, :] = vector[:, pl.ds(send_place(right, here, span), span)]
+    if send.shape[0] > rows:
+        send[rows:, :] = jnp.zeros((send.shape[0] - rows, span), F32)
 
 
 def mate_first_kernel(own, partial, received, columns, k_high, k_low, out, to_next, halves, rows, *, links):
@@ -286,7 +289,7 @@
 
 
 def next_first_kernel(
-    own, partial, first, mate, received, columns, mate_high, mate_low, k_high, k_low, out, given, to_mate, halves, rows, *, links
+    own, partial, mate, received, columns, mate_high, mate_low, k_high, k_low, out, to_mate, halves, rows, *, links
 ):
     probe_count = out.shape[0]
     length = halves.shape[1] // links
@@ -300,7 +303,6 @@
     fill_halo(right, own, received, columns, tables, rows, links)
     halo_product(right, lambda at: received[0:probe_count, at], tables, out, halves, links)
     store_send(is_right(True), out, to_mate)
-    own_product(right, first, k_high, k_low, given, halves, links + 1)
 
 
 def add_sums(table, terms):
@@ -314,35 +316,56 @@
     return table
 
 
-def local_second_kernel(noise, first, second, k_high, k_low, out, table, halves, *, length):
+def local_second_kernel(noise, second, k_high, k_low, out, halves, *, length):
     local_product(noise, second, k_high, k_low, out, halves, length)
-    table[...] = add_sums(jnp.zeros(table.shape, F32), ((0, first, first), (1, first, second), (2, second, second)))
-
-
-def local_third_kernel(noise, second, third, table_in, k_high, k_low, out, table, halves, *, length):
+
+
+def local_third_kernel(noise, first, second, third, k_high, k_low, out, table, halves, *, length):
     local_product(noise, third, k_high, k_low, out, halves, length)
-    table[...] = add_sums(table_in[...], ((3, second, third), (4, third, third)))
-
-
-def both_products(partial, beyond, mate, tables, out, halves, links):
+    terms = ((0, first, first), (1, first, second), (2, second, second), (3, second, third), (4, third, third))
+    table[...] = add_sums(jnp.zeros(table.shape, F32), terms)
+
+
+def mate_second_kernel(partial, mate, k_high, k_low, out, to_next, halves, *, links):
     length = halves.shape[1] // links
     out[...] = partial[...]
-    mate_tables = table_rows(*tables[0:2], range(1, links), length)
-    mate_tables.update(table_rows(*tables[2:4], range(links, links + 1), length))
-    halo_product(is_right(True), lambda at: mate[:, at], mate_tables, out, halves, links)
-    halo_product(is_right(False), beyond, table_rows(*tables[4:6], range(1, links + 1), length), out, halves, links)
-
-
-def halo_second_kernel(partial, beyond, given, mate, *rest, links):
-    tables, (out, to_next, to_mate, halves) = rest[0:6], rest[6:]
-    both_products(partial, lambda at: beyond[:, at] + given[:, at], mate, tables, out, halves, links)
+    tables = table_rows(k_high, k_low, range(1, links), length)
+    halo_product(is_right(True), lambda at: mate[:, at], tables, out, halves, links)
     store_send(is_right(False), out, to_next)
+
+
+def next_second_kernel(
+    partial, first, second, mate, ahead, mate_high, mate_low, k_high, k_low, out, given, to_mate, halves, *, links
+):
+    length = halves.shape[1] // links
+    right = is_right(False)
+    out[...] = partial[...]
+    tables = table_rows(mate_high, mate_low, range(links, links + 1), length)
+    halo_product(is_right(True), lambda at: mate[:, at], tables, out, halves, links)
+    own_product(right, first, k_high, k_low, given, halves, links + 1)
+    tables = table_rows(k_high, k_low, range(1, links + 1), length)
+    halo_product(right, received_share(ahead, given), tables, out, halves, links)
     store_send(is_right(True), out, to_mate)
-
-
-def halo_third_kernel(partial, beyond, mate, *rest, links):
-    tables, (third, table, out, sums, halves) = rest[0:6], rest[6:]
-    both_products(partial, lambda at: beyond[:, at], mate, tables, out, halves, links)
+    own_product(right, second, k_high, k_low, given, halves, links + 1)
+
+
+def received_share(received, given):
+    return lambda at: received[0 : given.shape[0], at] + given[:, at]
+
+
+def mate_third_kernel(partial, mate, early_high, early_low, late_high, late_low, out, halves, *, links):
+    length = halves.shape[1] // links
+    out[...] = partial[...]
+    tables = table_rows(early_high, early_low, range(1, links), length)
+    tables.update(table_rows(late_high, late_low, range(links, links + 1), length))
+    halo_product(is_right(True), lambda at: mate[:, at], tables, out, halves, links)
+
+
+def next_third_kernel(partial, after, given, k_high, k_low, third, table, out, sums, halves, *, links):
+    length = halves.shape[1] // links
+    out[...] = partial[...]
+    tables = table_rows(k_high, k_low, range(1, links + 1), length)
+    halo_product(is_right(False), received_share(after, given), tables, out, halves, links)
     full = add_sums(table[...], ((5, third, out), (6, out, out)))
     turned = jnp.transpose(full)[0:8, :]
     compact = jnp.concatenate([turned[0:4], turned[4:8]], axis=1)
@@ -441,6 +464,7 @@
     whole = jax.ShapeDtypeStruct((rows, here), F32)
     part = jax.ShapeDtypeStruct((rows, span), F32)
     packed = jax.ShapeDtypeStruct((rows + 8, span), F32)
+    wide_part = jax.ShapeDtypeStruct((rows + 8, span), F32)
     sums_table = jax.ShapeDtypeStruct((rows, 128), F32)
     local_table = jax.ShapeDtypeStruct((here, here), BF16)
     halo_table = jax.ShapeDtypeStruct((span, span), BF16)
@@ -472,40 +496,50 @@
     early_high, early_low, partial, to_next = call(
         functools.partial(mate_first_kernel, links=links),
         "mate_first",
-        (early_table, early_table, whole, part),
+        (early_table, early_table, whole, wide_part),
         [VMEM] * 4,
         halo_scratch,
     )(own, partial, mate, columns)
     ahead = swap_next(to_next)
-    late_high, late_low, next_high, next_low, second, given, to_mate = call(
+    late_high, late_low, next_high, next_low, second, to_mate = call(
         functools.partial(next_first_kernel, links=links),
         "next_first",
-        (late_table, late_table, halo_table, halo_table, whole, part, part),
-        [VMEM] * 6,
+        (late_table, late_table, halo_table, halo_table, whole, part),
+        [VMEM] * 5,
         halo_scratch,
-    )(own, partial, first, mate, beyond, columns)
-    tables = (early_high, early_low, late_high, late_low, next_high, next_low)
+    )(own, partial, mate, beyond, columns)
+
+    mate = swap_mate(to_mate)
+    partial = call(
+        functools.partial(local_second_kernel, length=length), "local_second", whole, [VMEM] * 4, [local_halves]
+    )(noise, second, k_high, k_low)
+    partial, to_next = call(
+        functools.partial(mate_second_kernel, links=links), "mate_second", (whole, wide_part), [VMEM] * 4, [halo_halves]
+    )(partial, mate, early_high, early_low)
+    after = swap_next(to_next)
+    third, given, to_mate = call(
+        functools.partial(next_second_kernel, links=links),
+        "next_second",
+        (whole, part, part),
+        [VMEM] * 9,
+        [halo_halves],
+    )(partial, first, second, mate, ahead, late_high, late_low, next_high, next_low)
 
     mate = swap_mate(to_mate)
     partial, table = call(
-        functools.partial(local_second_kernel, length=length), "local_second", (whole, sums_table), [VMEM] * 5, [local_halves]
-    )(noise, first, second, k_high, k_low)
-    third, to_next, to_mate = call(
-        functools.partial(halo_second_kernel, links=links), "halo_second", (whole, part, part), [VMEM] * 10, [halo_halves]
-    )(partial, ahead, given, mate, *tables)
-
-    beyond, mate = swap_next(to_next), swap_mate(to_mate)
-    partial, table = call(
         functools.partial(local_third_kernel, length=length), "local_third", (whole, sums_table), [VMEM] * 6, [local_halves]
-    )(noise, second, third, table, k_high, k_low)
+    )(noise, first, second, third, k_high, k_low)
     regions, subs = lax.axis_size("region"), lax.axis_size("sub")
+    partial = call(
+        functools.partial(mate_third_kernel, links=links), "mate_third", whole, [VMEM] * 6, [halo_halves]
+    )(partial, mate, early_high, early_low, late_high, late_low)
     fourth, sums = call(
-        functools.partial(halo_third_kernel, links=links),
-        "halo_third",
+        functools.partial(next_third_kernel, links=links),
+        "next_third",
         (whole, jax.ShapeDtypeStruct((regions, 4, 128), F32)),
-        [VMEM] * 11,
+        [VMEM] * 7,
         [halo_halves],
-    )(partial, beyond, mate, *tables, third, table)
+    )(partial, after, given, next_high, next_low, third, table)
 
     sums = jnp.sum(lax.all_to_all(sums, "region", 0, 0), axis=0)
     sums = lax.all_to_all(jnp.broadcast_to(sums[None], (subs, 4, 128)), "sub", 0, 0)

time: 77.9 us -> 75.7 us (0.972)
  waiting for transfers between devices: 2.47 us -> 0.75 us
  blocking collectives: 37 us -> 36.2 us
    all_to_all x1, blocking collectives: 15.2 us -> 12.7 us  [per_device(): lax.all_to_all(jnp.broadcast_to(sums[None], (subs, 4, 128)), 'sub', 0, 0)]
    ppermute x3, waiting for transfers between devices: 2.11 us -> 0.01 us  [swap_next(): lax.ppermute(array, AXES, [(i, i + 1 if i % 2 else i - 1) for i in range(...]
    all_to_all x1, blocking collectives: 21.8 us -> 23.6 us  [per_device(): sums = jnp.sum(lax.all_to_all(sums, 'region', 0, 0), axis=0)]
    pallas_call x2 -> x4, Pallas kernels: 2.5 us -> 3.25 us  [the longest x1 1.38 us: per_device(): call(functools.partial(next_second_kernel, links=links), 'next_second', (...]
  transfers between devices with their start and end apart: 6 -> 6, of which waited for: 2 -> 2; matrix products, arithmetic and copies ran while one was open for 0% -> 0% of each run, Pallas kernels for 15% -> 17%
where the time goes in v5:
time: 75.7 us; the launch traced here: 75.3 us
  blocking collectives  36.2 us (48%)
  starting transfers between devices  20.1 us (27%)
  Pallas kernels  16.3 us (22%)
  between operations  1 us (1%)
  loops' own time  0.81 us (1%)
    all_to_all x1, blocking collectives, per_device(): sums = jnp.sum(lax.all_to_all(sums, 'region', 0, 0), axis=0)  23.6 us
    all_to_all x1, blocking collectives, per_device(): lax.all_to_all(jnp.broadcast_to(sums[None], (subs, 4, 128)), 'sub', 0, 0)  12.7 us
    ppermute x3, starting transfers between devices, swap_mate(): lax.ppermute(array, AXES, [(i, i ^ 1) for i in range(lax.axis_size(AXES))])  12.6 us
    ppermute x3, starting transfers between devices, swap_next(): lax.ppermute(array, AXES, [(i, i + 1 if i % 2 else i - 1) for i in range(...  7.48 us
    pallas_call x1, Pallas kernels, per_device(): call(functools.partial(local_first_kernel, links=links), 'local_first', (...  4.59 us
    pallas_call x1, Pallas kernels, per_device(): call(functools.partial(next_first_kernel, links=links), 'next_first', (la...  3.04 us
  transfers between devices with their start and end apart: 6, of which 2 were waited for; matrix products, arithmetic and copies ran while one was open for 0% of the time, Pallas kernels for 17%

profile of v5, /device:TPU:1, one launch (start us, length us, event | category | flops | bytes accessed | tf_op | source)
XLA Modules:
  0.0 75.3 jit_solution(12213158341498315316)
XLA Ops:
  0.6 1.1 %pack.1 = (f32[72,768]{1,0:T(8,128)S(1)}, f32[72,768]{1,0:T(8,128)S(1)}, f32[8,1024]{1,0:T(8,128)S(1)}) custom-call(f32[3,1024]{1,0:T(4,128)} %coords.1, s32[3,4]{1,0:T(4,128)} %pair.1, f32[64,1024]{1,0:T(8,128)} %probes.3), custom_call_target="tpu_custom_call" | custom-call | tf_op jit(solution)/shard_map/pack/pallas_call | solution.py:474
  1.7 8.8 %collective-permute-start.3 = (f32[72,768]{1,0:T(8,128)S(1)}, f32[72,768]{1,0:T(8,128)S(1)}, u32[]{:S(2)}, u32[]{:S(2)}) collective-permute-start(f32[72,768]{1,0:T(8,128)S(1)} %get-tuple-element.312), channel_id=1, source_target_pairs={{0,1},{1,0},{2,3},{3,2},{4,5},{5,4},{6,7},{7,6},{8,9},{9,8},{10,11... | collective-permute-start | bytes 663560 | tf_op jit(solution)/shard_map/ppermute | solution.py:450
  10.5 1.9 %collective-permute-start.4 = (f32[72,768]{1,0:T(8,128)S(1)}, f32[72,768]{1,0:T(8,128)S(1)}, u32[]{:S(2)}, u32[]{:S(2)}) collective-permute-start(f32[72,768]{1,0:T(8,128)S(1)} %get-tuple-element.315), channel_id=1, source_target_pairs={{1,2},{2,1},{3,4},{4,3},{5,6},{6,5},{7,8},{8,7},{9,10},{10,9},{11,... | collective-permute-start | bytes 663560 | tf_op jit(solution)/shard_map/ppermute | solution.py:454
  12.4 4.6 %local_first.1 = (bf16[1024,1024]{1,0:T(8,128)(2,1)S(1)}, bf16[1024,1024]{1,0:T(8,128)(2,1)S(1)}, f32[64,1024]{1,0:T(8,128)S(1)}, f32[64,1024]{1,0:T(8,128)S(1)}, f32[3,1024,128]{2,1,0:T(8,128)S(1)}) custom-call(f32[8,1024]{1,0:T(8,128)S(1)} %get-tuple-element.309.own, f32[1,1024]{1,0:T(1,128)} %bitcast.97, f32[64,1024]{1,0:T(8,128)} %probes.3), custom_call_target="tpu_custom_call" | custom-call | tf_op jit(solution)/shard_map/local_first/pallas_call | solution.py:482
  17.0 0.0 collective-permute-done.3.received.mate
  17.0 1.1 %mate_first.1 = (bf16[512,512]{1,0:T(8,128)(2,1)S(1)}, bf16[512,512]{1,0:T(8,128)(2,1)S(1)}, f32[64,1024]{1,0:T(8,128)S(1)}, f32[72,768]{1,0:T(8,128)S(1)}) custom-call(f32[8,1024]{1,0:T(8,128)S(1)} %get-tuple-element.309.own, f32[64,1024]{1,0:T(8,128)S(1)} %get-tuple-element.311.partial, f32[72,768]{1,0:T(8,128)S(1)} %collective-permute-done.3.received.mate, ...), custom_call_target="tpu_custom_call" | custom-call | tf_op jit(solution)/shard_map/mate_first/pallas_call | solution.py:496
  18.1 0.0 copy-start.3
  18.1 3.6 %collective-permute-start.6 = (f32[72,768]{1,0:T(8,128)S(1)}, f32[72,768]{1,0:T(8,128)S(1)}, u32[]{:S(2)}, u32[]{:S(2)}) collective-permute-start(f32[72,768]{1,0:T(8,128)S(1)} %get-tuple-element.323), channel_id=1, source_target_pairs={{1,2},{2,1},{3,4},{4,3},{5,6},{6,5},{7,8},{8,7},{9,10},{10,9},{11,... | collective-permute-start | bytes 663560 | tf_op jit(solution)/shard_map/ppermute | solution.py:454
  21.8 0.0 collective-permute-done.4.received
  21.8 3.0 %next_first.1 = (bf16[256,768]{1,0:T(8,128)(2,1)S(1)}, bf16[256,768]{1,0:T(8,128)(2,1)S(1)}, bf16[768,768]{1,0:T(8,128)(2,1)S(1)}, bf16[768,768]{1,0:T(8,128)(2,...) custom-call(f32[8,1024]{1,0:T(8,128)S(1)} %get-tuple-element.309.own, f32[64,1024]{1,0:T(8,128)S(1)} %get-tuple-element.314.partial, ...), custom_call_target="tpu_custom_call" | custom-call | tf_op jit(solution)/shard_map/next_first/pallas_call | solution.py:504
  24.8 1.9 %collective-permute-start.5 = (f32[64,768]{1,0:T(8,128)S(1)}, f32[64,768]{1,0:T(8,128)S(1)}, u32[]{:S(2)}, u32[]{:S(2)}) collective-permute-start(f32[64,768]{1,0:T(8,128)S(1)} %get-tuple-element.319), channel_id=1, source_target_pairs={{0,1},{1,0},{2,3},{3,2},{4,5},{5,4},{6,7},{7,6},{8,9},{9,8},{10,11... | collective-permute-start | bytes 589832 | tf_op jit(solution)/shard_map/ppermute | solution.py:450
  26.8 0.0 copy-done.3
  26.8 1.0 %local_second.1.partial = f32[64,1024]{1,0:T(8,128)S(1)} custom-call(f32[1,1024]{1,0:T(1,128)S(1)} %bitcast.98, f32[64,1024]{1,0:T(8,128)S(1)} %get-tuple-element.316.second, bf16[1024,1024]{1,0:T(8,128)(2,1)S(1)} %get-tuple-element.317.k_high, bf16[1024,1024]{1,0:T(8,128)(2,1)S(1)} %get-tuple-element.318.k_low), custom_call_target="tpu_custom_call" | custom-call | tf_op jit(solution)/shard_map/local_second/pallas_call | solution.py:513
  27.8 0.4 collective-permute-done.5.mate
  28.2 0.4 mate_second.1
  28.6 1.9 %collective-permute-start.8 = (f32[72,768]{1,0:T(8,128)S(1)}, f32[72,768]{1,0:T(8,128)S(1)}, u32[]{:S(2)}, u32[]{:S(2)}) collective-permute-start(f32[72,768]{1,0:T(8,128)S(1)} %get-tuple-element.331), channel_id=1, source_target_pairs={{1,2},{2,1},{3,4},{4,3},{5,6},{6,5},{7,8},{8,7},{9,10},{10,9},{11,... | collective-permute-start | bytes 663560 | tf_op jit(solution)/shard_map/ppermute | solution.py:454
  30.5 0.0 collective-permute-done.6.ahead
  30.5 1.4 %next_second.1 = (f32[64,1024]{1,0:T(8,128)S(1)}, f32[64,768]{1,0:T(8,128)S(1)}, f32[64,768]{1,0:T(8,128)S(1)}) custom-call(f32[64,1024]{1,0:T(8,128)S(1)} %get-tuple-element.322.partial, f32[64,1024]{1,0:T(8,128)S(1)} %get-tuple-element.310.first, f32[64,1024]{1,0:T(8,128)S(1)} %get-tuple-element.316.second, f32[64,768]{1,0:T(8,128)S(1)} %collective-permute-done.5.mate, ...), custom_call_target="tpu_custom_call" | custom-call | tf_op jit(solution)/shard_map/next_second/pallas_call | solution.py:520
  31.9 1.9 %collective-permute-start.7 = (f32[64,768]{1,0:T(8,128)S(1)}, f32[64,768]{1,0:T(8,128)S(1)}, u32[]{:S(2)}, u32[]{:S(2)}) collective-permute-start(f32[64,768]{1,0:T(8,128)S(1)} %get-tuple-element.330), channel_id=1, source_target_pairs={{0,1},{1,0},{2,3},{3,2},{4,5},{5,4},{6,7},{7,6},{8,9},{9,8},{10,11... | collective-permute-start | bytes 589832 | tf_op jit(solution)/shard_map/ppermute | solution.py:450
  33.8 1.0 %local_third.1 = (f32[64,1024]{1,0:T(8,128)S(1)}, f32[64,128]{1,0:T(8,128)S(1)}) custom-call(f32[1,1024]{1,0:T(1,128)S(1)} %bitcast.99, f32[64,1024]{1,0:T(8,128)S(1)} %get-tuple-element.310.first, f32[64,1024]{1,0:T(8,128)S(1)} %get-tuple-element.316.second, f32[64,1024]{1,0:T(8,128)S(1)} %get-tuple-element.328.third, ...), custom_call_target="tpu_custom_call" | custom-call | tf_op jit(solution)/shard_map/local_third/pallas_call | solution.py:529
  34.9 0.4 collective-permute-done.7.mate
  35.2 0.6 mate_third.1.partial
  35.9 0.0 collective-permute-done.8.after
  35.9 0.0 copy-start.2
  35.9 0.0 copy-start.4
  35.9 0.0 copy-start.5
  35.9 0.9 %next_third.1 = (f32[64,1024]{1,0:T(8,128)S(1)}, f32[32,4,128]{2,1,0:T(4,128)S(1)}) custom-call(f32[64,1024]{1,0:T(8,128)S(1)} %mate_third.1.partial, f32[72,768]{1,0:T(8,128)S(1)} %collective-permute-done.8.after, f32[64,768]{1,0:T(8,128)S(1)} %get-tuple-element.332.given, bf16[768,768]{1,0:T(8,128)(2,1)S(1)} %get-tuple-element.326.k_high, ...), custom_call_target="tpu_custom_call" | custom-call | tf_op jit(solution)/shard_map/next_third/pallas_call | solution.py:536
  36.8 23.6 %all_to_all.10 = f32[32,4,128]{2,1,0:T(4,128)S(1)} all-to-all(f32[32,4,128]{2,1,0:T(4,128)S(1)} %get-tuple-element.334), channel_id=1, replica_groups=mesh['region'=32,'sub'=16] {'region'}, dimensions={0} | all-to-all | bytes 131072 | tf_op jit(solution)/shard_map/all_to_all | solution.py:544
  60.4 12.7 %all_to_all.11.sums = f32[16,4,128]{2,1,0:T(4,128)S(1)} all-to-all(f32[16,4,128]{2,1,0:T(4,128)S(1)} %broadcast_in_dim.5), channel_id=1, replica_groups=mesh['region'=32,'sub'=16] {'sub'}, dimensions={0} | all-to-all | bytes 65536 | tf_op jit(solution)/shard_map/all_to_all | solution.py:545
  73.1 1.2 %finish.1 = (f32[64,1024]{1,0:T(8,128)}, f32[64,1024]{1,0:T(8,128)}, f32[1,1]{1,0:T(1,128)}) custom-call(f32[16,4,128]{2,1,0:T(4,128)S(1)} %all_to_all.11.sums, f32[64,1024]{1,0:T(8,128)S(1)} %get-tuple-element.310.first, f32[64,1024]{1,0:T(8,128)S(1)} %get-tuple-element.316.second, f32[64,1024]{1,0:T(8,128)S(1)} %get-tuple-element.328.third, ...), custom_call_target="tpu_custom_call" | custom-call | tf_op jit(solution)/shard_map/finish/pallas_call | solution.py:546
  74.3 0.0 copy-done.2
  74.3 0.0 copy-done.4
  74.3 0.0 copy-done.5
  74.3 0.8 %while.35 = (f32[1,1]{1,0:T(1,128)}, f32[64,1024]{1,0:T(8,128)}, f32[64,1024]{1,0:T(8,128)}, f32[64,1024]{1,0:T(8,128)S(1)}, f32[3,1024]{1,0:T(4,128)S(1)}, /*in...) while((f32[1,1]{1,0:T(1,128)}, f32[64,1024]{1,0:T(8,128)}, f32[64,1024]{1,0:T(8,128)}, ...), condition=%region_10.11_spmd, body=%region_1.10_spmd | while | flops 1439929600 | bytes 21131516 | solution.py:558
  (2 shorter events, 0.1 us)
Async XLA Ops:
  1.7 15.3 %collective-permute-start.3 = (f32[72,768]{1,0:T(8,128)S(1)}, f32[72,768]{1,0:T(8,128)S(1)}, u32[]{:S(2)}, u32[]{:S(2)}) collective-permute-start(f32[72,768]{1,0:T(8,128)S(1)} %get-tuple-element.312), channel_id=1, source_target_pairs={{0,1},{1,0},{2,3},{3,2},{4,5},{5,4},{6,7},{7,6},{8,9},{9,8},{10,11... | collective-permute-start | bytes 663560 | tf_op jit(solution)/shard_map/ppermute | solution.py:450
  10.5 11.3 %collective-permute-start.4 = (f32[72,768]{1,0:T(8,128)S(1)}, f32[72,768]{1,0:T(8,128)S(1)}, u32[]{:S(2)}, u32[]{:S(2)}) collective-permute-start(f32[72,768]{1,0:T(8,128)S(1)} %get-tuple-element.315), channel_id=1, source_target_pairs={{1,2},{2,1},{3,4},{4,3},{5,6},{6,5},{7,8},{8,7},{9,10},{10,9},{11,... | collective-permute-start | bytes 663560 | tf_op jit(solution)/shard_map/ppermute | solution.py:454
  18.1 8.6 %copy-start.3 = (f32[1024]{0:T(1024)S(1)}, f32[1024]{0:T(1024)}, u32[]{:S(2)}) copy-start(f32[1024]{0:T(1024)} %param.17) | copy-start | bytes 12292
  18.1 12.4 %collective-permute-start.6 = (f32[72,768]{1,0:T(8,128)S(1)}, f32[72,768]{1,0:T(8,128)S(1)}, u32[]{:S(2)}, u32[]{:S(2)}) collective-permute-start(f32[72,768]{1,0:T(8,128)S(1)} %get-tuple-element.323), channel_id=1, source_target_pairs={{1,2},{2,1},{3,4},{4,3},{5,6},{6,5},{7,8},{8,7},{9,10},{10,9},{11,... | collective-permute-start | bytes 663560 | tf_op jit(solution)/shard_map/ppermute | solution.py:454
  24.8 3.3 %collective-permute-start.5 = (f32[64,768]{1,0:T(8,128)S(1)}, f32[64,768]{1,0:T(8,128)S(1)}, u32[]{:S(2)}, u32[]{:S(2)}) collective-permute-start(f32[64,768]{1,0:T(8,128)S(1)} %get-tuple-element.319), channel_id=1, source_target_pairs={{0,1},{1,0},{2,3},{3,2},{4,5},{5,4},{6,7},{7,6},{8,9},{9,8},{10,11... | collective-permute-start | bytes 589832 | tf_op jit(solution)/shard_map/ppermute | solution.py:450
  28.6 7.3 %collective-permute-start.8 = (f32[72,768]{1,0:T(8,128)S(1)}, f32[72,768]{1,0:T(8,128)S(1)}, u32[]{:S(2)}, u32[]{:S(2)}) collective-permute-start(f32[72,768]{1,0:T(8,128)S(1)} %get-tuple-element.331), channel_id=1, source_target_pairs={{1,2},{2,1},{3,4},{4,3},{5,6},{6,5},{7,8},{8,7},{9,10},{10,9},{11,... | collective-permute-start | bytes 663560 | tf_op jit(solution)/shard_map/ppermute | solution.py:454
  31.9 3.3 %collective-permute-start.7 = (f32[64,768]{1,0:T(8,128)S(1)}, f32[64,768]{1,0:T(8,128)S(1)}, u32[]{:S(2)}, u32[]{:S(2)}) collective-permute-start(f32[64,768]{1,0:T(8,128)S(1)} %get-tuple-element.330), channel_id=1, source_target_pairs={{0,1},{1,0},{2,3},{3,2},{4,5},{5,4},{6,7},{7,6},{8,9},{9,8},{10,11... | collective-permute-start | bytes 589832 | tf_op jit(solution)/shard_map/ppermute | solution.py:450
  35.9 38.4 %copy-start.2 = (f32[64,1024]{1,0:T(8,128)S(1)}, f32[64,1024]{1,0:T(8,128)}, u32[]{:S(2)}) copy-start(f32[64,1024]{1,0:T(8,128)} %probes.3) | copy-start | bytes 786436
  35.9 38.4 %copy-start.4 = (f32[3,1024]{1,0:T(4,128)S(1)}, f32[3,1024]{1,0:T(4,128)}, u32[]{:S(2)}) copy-start(f32[3,1024]{1,0:T(4,128)} %coords.1) | copy-start | bytes 36868
  35.9 38.4 %copy-start.5 = (s32[3,4]{1,0:T(4,128)S(1)}, s32[3,4]{1,0:T(4,128)}, u32[]{:S(2)}) copy-start(s32[3,4]{1,0:T(4,128)} %pair.1) | copy-start | bytes 148

commit v6 on v5

--- a/solution.py
+++ b/solution.py
@@ -139,35 +139,55 @@
     copies[3].wait()
 
 
-def fill_columns(columns, at, block):
-    turned = jnp.transpose(block)
-    for d in range(3):
-        columns[d, at : at + turned.shape[0], :] = jnp.broadcast_to(turned[:, d : d + 1], (turned.shape[0], 128))
-
-
-def fill_tiles(k_high, k_low, to_row, columns, from_row, count, rows, at, first):
+def column_steps(columns, at, block):
+    def fill(d, turned):
+        size = turned.shape[0]
+        columns[d, at : at + size, :] = jnp.broadcast_to(turned[:, d : d + 1], (size, 128))
+
+    def step():
+        turned = jnp.transpose(block)
+        for d in range(3):
+            fill(d, turned)
+
+    return [step]
+
+
+def fill_strip(k_high, k_low, to_row, columns, from_row, strip, rows, x, at, first):
+    column = [columns[d, pl.ds(from_row, strip), :].reshape(strip // 8, 8, 128) for d in range(3)]
+    for lane in range(at.start, at.stop, 128):
+        squared = None
+        for d in range(3):
+            away = column[d] - rows[d if d else x, :, lane : lane + 128][None]
+            squared = away * away if squared is None else squared + away * away
+        squared = jnp.maximum(squared, 1e-30)
+        distance = squared * lax.rsqrt(squared)
+        support = jnp.maximum(4.0 - distance, 0.0)
+        support = support * support
+        value = support * support * (distance + 1.0)
+        top, rest = split(value.reshape(strip, 128))
+        to = slice(first + lane - at.start, first + lane - at.start + 128)
+        k_high[pl.ds(to_row, strip), to] = top
+        k_low[pl.ds(to_row, strip), to] = rest
+
+
+def fill_tiles(k_high, k_low, to_row, columns, from_row, count, rows, x, at, first, beside=()):
     strip = 64 if at.stop - at.start <= 4 * 128 else 32
-
-    def body(s, _):
-        step = pl.multiple_of(s * strip, strip)
-        column = [columns[d, pl.ds(from_row + step, strip), :].reshape(strip // 8, 8, 128) for d in range(3)]
-        for lane in range(at.start, at.stop, 128):
-            squared = None
-            for d in range(3):
-                away = column[d] - rows[d, :, lane : lane + 128][None]
-                squared = away * away if squared is None else squared + away * away
-            squared = jnp.maximum(squared, 1e-30)
-            distance = squared * lax.rsqrt(squared)
-            support = jnp.maximum(4.0 - distance, 0.0)
-            support = support * support
-            value = support * support * (distance + 1.0)
-            top, rest = split(value.reshape(strip, 128))
-            to = slice(first + lane - at.start, first + lane - at.start + 128)
-            k_high[pl.ds(to_row + step, strip), to] = top
-            k_low[pl.ds(to_row + step, strip), to] = rest
-        return 0
-
-    lax.fori_loop(0, count // strip, body, 0)
+    if not beside:
+
+        def body(s, _):
+            step = pl.multiple_of(s * strip, strip)
+            fill_strip(k_high, k_low, to_row + step, columns, from_row + step, strip, rows, x, at, first)
+            return 0
+
+        lax.fori_loop(0, count // strip, body, 0)
+        return
+    done = 0
+    for s in range(count // strip):
+        step = s * strip
+        fill_strip(k_high, k_low, to_row + step, columns, from_row + step, strip, rows, x, at, first)
+        while done < len(beside) * (s + 1) * strip // count:
+            beside[done]()
+            done += 1
 
 
 def store_halves(halves, at, vector):
@@ -197,16 +217,46 @@
         out[:, at] = value + (noise[:, at] - SHIFT) * vector[:, at]
 
 
+def row_steps(halves, k_high, k_low, out, start, length):
+    stop, here = start + length, out.shape[1]
+    steps = []
+
+    def natural(at):
+        def step():
+            out[:, at] = out[:, at] + multiply(halves[:, start:stop], k_high[start:stop, at], k_low[start:stop, at])
+
+        return step
+
+    def mirrored(at):
+        def step():
+            value = multiply(halves[:, at], k_high[start:stop, at], k_low[start:stop, at], turned=True)
+            out[:, start:stop] = out[:, start:stop] + value
+
+        return step
+
+    for at in range(start, here, length):
+        steps.append(natural(slice(at, at + length)))
+    for at in range(stop, here, length):
+        steps.append(mirrored(slice(at, at + length)))
+    return steps
+
+
 def local_first_kernel(own, noise, probes, k_high, k_low, out, first, columns, halves, rows, sem, *, links):
     here = own.shape[1]
     blocks = links + 1
     length = here // blocks
     copy = pltpu.make_async_copy(probes, first, sem.at[0])
     copy.start()
-    for j in range(blocks):
-        fill_columns(columns, j * length, 4.0 * own[:, j * length : (j + 1) * length])
     for d in range(1, 3):
         rows[d] = jnp.broadcast_to(4.0 * own[d : d + 1, :], rows.shape[1:])
+    steps = []
+    for j in range(blocks):
+        half = length // 2
+        for at in (j * length, j * length + half):
+            steps += column_steps(columns, at, 4.0 * own[:, at : at + half])
+    for step in steps[0:2]:
+        step()
+    steps = steps[2:]
     for i in range(blocks):
         for j in range(i, blocks):
             at = slice(j * length, (j + 1) * length)
@@ -214,22 +264,28 @@
             if j > i:
                 flag = own[2 + j - i : 3 + j - i, i * length : (i + 1) * length]
                 moved = jnp.where(flag == 1.0, moved, moved + FAR)
-            rows[0, :, at] = jnp.broadcast_to(moved, (8, length))
-        fill_tiles(k_high, k_low, i * length, columns, i * length, length, rows, slice(i * length, here), i * length)
-    copy.wait()
-    local_product(noise, first, k_high, k_low, out, halves, length)
-
-
-def fill_halo(right, own, received, columns, tables, rows, links):
+            rows[3 + i, :, at] = jnp.broadcast_to(moved, (8, length))
+        start = i * length
+        fill_tiles(k_high, k_low, start, columns, start, length, rows, 3 + i, slice(start, here), start, steps)
+        if i == 0:
+            copy.wait()
+            store_halves(halves, 0, first[...])
+            out[...] = (noise[...] - SHIFT) * first[...]
+        steps = row_steps(halves, k_high, k_low, out, start, length)
+    for step in steps:
+        step()
+
+
+def halo_rows(right, own, received, rows, links, ns):
     length = received.shape[1] // links
     blocks = own.shape[1] // length
     at = received.shape[0] - 8
     place = [pl.ds(halo_place(right, links, length, h), length) for h in range(links)]
-    for h in range(max(tables)):
+    for h in range(max(ns)):
         for d in range(1, 3):
             coord = 4.0 * received[at + d : at + d + 1, place[h]]
             rows[d, :, h * length : (h + 1) * length] = jnp.broadcast_to(coord, (8, length))
-    for n, (k_high, k_low) in tables.items():
+    for n in ns:
         mine = own_place(right, blocks, links, length, n)
         for h in range(n):
             k = links - n + h
@@ -237,8 +293,33 @@
             theirs = received[at + 3 + k : at + 4 + k, place[h]]
             coord = 4.0 * received[at : at + 1, place[h]]
             coord = jnp.where(jnp.where(right, ours, theirs) == 1.0, coord, coord + FAR)
-            rows[0, :, h * length : (h + 1) * length] = jnp.broadcast_to(coord, (8, length))
-        fill_tiles(k_high, k_low, 0, columns, mine, length, rows, slice(0, n * length), 0)
+            rows[2 + n, :, h * length : (h + 1) * length] = jnp.broadcast_to(coord, (8, length))
+
+
+def fill_halo(right, received, columns, tables, out, halves, rows, links, beside):
+    probe_count = out.shape[0]
+    length = received.shape[1] // links
+    blocks = out.shape[1] // length
+    for h in range(max(tables)):
+        place = pl.ds(halo_place(right, links, length, h), length)
+        store_halves(halves, h * length, received[0:probe_count, place])
+
+    def product(n, h):
+        own = pl.ds(own_place(right, blocks, links, length, n), length)
+        at = slice(h * length, (h + 1) * length)
+        k_high, k_low = tables[n]
+
+        def step():
+            out[:, own] = out[:, own] + multiply(halves[:, at], k_high[:, at], k_low[:, at], turned=True)
+
+        return step
+
+    for n in sorted(tables, reverse=True):
+        mine = own_place(right, blocks, links, length, n)
+        k_high, k_low = tables[n]
+        fill_tiles(k_high, k_low, 0, columns, mine, length, rows, 2 + n, slice(0, n * length), 0, beside)
+        beside = [product(n, h) for h in range(n)]
+    return beside
 
 
 def table_rows(k_high, k_low, ns, length):
@@ -278,30 +359,47 @@
 
 
 def mate_first_kernel(own, partial, received, columns, k_high, k_low, out, to_next, halves, rows, *, links):
-    probe_count = out.shape[0]
     right = is_right(True)
     length = halves.shape[1] // links
-    tables = table_rows(k_high, k_low, range(1, links), length)
-    fill_halo(right, own, received, columns, tables, rows, links)
+    ns = range(1, links)
+    halo_rows(right, own, received, rows, links, ns)
     out[...] = partial[...]
-    halo_product(right, lambda at: received[0:probe_count, at], tables, out, halves, links)
+    tables = table_rows(k_high, k_low, ns, length)
+    for step in fill_halo(right, received, columns, tables, out, halves, rows, links, []):
+        step()
     store_send(is_right(False), out, to_next)
 
 
 def next_first_kernel(
-    own, partial, mate, received, columns, mate_high, mate_low, k_high, k_low, out, to_mate, halves, rows, *, links
+    own,
+    partial,
+    mate,
+    received,
+    columns,
+    mate_high,
+    mate_low,
+    k_high,
+    k_low,
+    out,
+    to_mate,
+    mate_halves,
+    mate_rows,
+    halves,
+    rows,
+    *,
+    links,
 ):
-    probe_count = out.shape[0]
     length = halves.shape[1] // links
     out[...] = partial[...]
-    right = is_right(True)
-    tables = table_rows(mate_high, mate_low, range(links, links + 1), length)
-    fill_halo(right, own, mate, columns, tables, rows, links)
-    halo_product(right, lambda at: mate[0:probe_count, at], tables, out, halves, links)
-    right = is_right(False)
-    tables = table_rows(k_high, k_low, range(1, links + 1), length)
-    fill_halo(right, own, received, columns, tables, rows, links)
-    halo_product(right, lambda at: received[0:probe_count, at], tables, out, halves, links)
+    left, right = is_right(True), is_right(False)
+    late, ns = range(links, links + 1), range(1, links + 1)
+    halo_rows(left, own, mate, mate_rows, links, late)
+    halo_rows(right, own, received, rows, links, ns)
+    tables = table_rows(mate_high, mate_low, late, length)
+    steps = fill_halo(left, mate, columns, tables, out, mate_halves, mate_rows, links, [])
+    tables = table_rows(k_high, k_low, ns, length)
+    for step in fill_halo(right, received, columns, tables, out, halves, rows, links, steps):
+        step()
     store_send(is_right(True), out, to_mate)
 
 
@@ -486,11 +584,11 @@
         [VMEM, VMEM, ANY],
         [
             local_halves,
-            pltpu.VMEM((3, 8, here), F32),
+            pltpu.VMEM((3 + blocks, 8, here), F32),
             pltpu.SemaphoreType.DMA((1,)),
         ],
     )(own, noise, probes)
-    halo_scratch = [halo_halves, pltpu.VMEM((3, 8, span), F32)]
+    halo_scratch = [halo_halves, pltpu.VMEM((3 + links, 8, span), F32)]
     early_table = jax.ShapeDtypeStruct((span - length, span - length), BF16)
     late_table = jax.ShapeDtypeStruct((length, span), BF16)
     early_high, early_low, partial, to_next = call(
@@ -506,7 +604,7 @@
         "next_first",
         (late_table, late_table, halo_table, halo_table, whole, part),
         [VMEM] * 5,
-        halo_scratch,
+        halo_scratch + halo_scratch,
     )(own, partial, mate, beyond, columns)
 
     mate = swap_mate(to_mate)

time: 75.7 us -> 73.9 us (0.976)
  Pallas kernels: 16.3 us -> 14.6 us
    pallas_call x1, Pallas kernels: 4.59 us -> 3.73 us  [per_device(): call(functools.partial(local_first_kernel, links=links), 'local_first', (...]
  transfers between devices with their start and end apart: 6 -> 6, of which waited for: 2 -> 2; matrix products, arithmetic and copies ran while one was open for 0% -> 0% of each run, Pallas kernels for 17% -> 16%
where the time goes in v6:
time: 73.9 us; the launch traced here: 73.6 us
  blocking collectives  36.2 us (49%)
  starting transfers between devices  20.1 us (27%)
  Pallas kernels  14.6 us (20%)
  between operations  1.01 us (1%)
  loops' own time  0.81 us (1%)
  waiting for transfers between devices  0.75 us (1%)
    all_to_all x1, blocking collectives, per_device(): sums = jnp.sum(lax.all_to_all(sums, 'region', 0, 0), axis=0)  23.6 us
    all_to_all x1, blocking collectives, per_device(): lax.all_to_all(jnp.broadcast_to(sums[None], (subs, 4, 128)), 'sub', 0, 0)  12.7 us
    ppermute x3, starting transfers between devices, swap_mate(): lax.ppermute(array, AXES, [(i, i ^ 1) for i in range(lax.axis_size(AXES))])  12.6 us
    ppermute x3, starting transfers between devices, swap_next(): lax.ppermute(array, AXES, [(i, i + 1 if i % 2 else i - 1) for i in range(...  7.49 us
    pallas_call x1, Pallas kernels, per_device(): call(functools.partial(local_first_kernel, links=links), 'local_first', (...  3.73 us
    pallas_call x1, Pallas kernels, per_device(): call(functools.partial(next_first_kernel, links=links), 'next_first', (la...  2.34 us
  transfers between devices with their start and end apart: 6, of which 2 were waited for; matrix products, arithmetic and copies ran while one was open for 0% of the time, Pallas kernels for 16%

profile of v6, /device:TPU:1, one launch (start us, length us, event | category | flops | bytes accessed | tf_op | source)
XLA Modules:
  0.0 73.6 jit_solution(4155598912506446272)
XLA Ops:
  0.6 1.1 %pack.1 = (f32[72,768]{1,0:T(8,128)S(1)}, f32[72,768]{1,0:T(8,128)S(1)}, f32[8,1024]{1,0:T(8,128)S(1)}) custom-call(f32[3,1024]{1,0:T(4,128)} %coords.1, s32[3,4]{1,0:T(4,128)} %pair.1, f32[64,1024]{1,0:T(8,128)} %probes.3), custom_call_target="tpu_custom_call" | custom-call | tf_op jit(solution)/shard_map/pack/pallas_call | solution.py:572
  1.7 8.8 %collective-permute-start.3 = (f32[72,768]{1,0:T(8,128)S(1)}, f32[72,768]{1,0:T(8,128)S(1)}, u32[]{:S(2)}, u32[]{:S(2)}) collective-permute-start(f32[72,768]{1,0:T(8,128)S(1)} %get-tuple-element.312), channel_id=1, source_target_pairs={{0,1},{1,0},{2,3},{3,2},{4,5},{5,4},{6,7},{7,6},{8,9},{9,8},{10,11... | collective-permute-start | bytes 663560 | tf_op jit(solution)/shard_map/ppermute | solution.py:548
  10.5 1.9 %collective-permute-start.4 = (f32[72,768]{1,0:T(8,128)S(1)}, f32[72,768]{1,0:T(8,128)S(1)}, u32[]{:S(2)}, u32[]{:S(2)}) collective-permute-start(f32[72,768]{1,0:T(8,128)S(1)} %get-tuple-element.315), channel_id=1, source_target_pairs={{1,2},{2,1},{3,4},{4,3},{5,6},{6,5},{7,8},{8,7},{9,10},{10,9},{11,... | collective-permute-start | bytes 663560 | tf_op jit(solution)/shard_map/ppermute | solution.py:552
  12.4 3.7 %local_first.1 = (bf16[1024,1024]{1,0:T(8,128)(2,1)S(1)}, bf16[1024,1024]{1,0:T(8,128)(2,1)S(1)}, f32[64,1024]{1,0:T(8,128)S(1)}, f32[64,1024]{1,0:T(8,128)S(1)}, f32[3,1024,128]{2,1,0:T(8,128)S(1)}) custom-call(f32[8,1024]{1,0:T(8,128)S(1)} %get-tuple-element.309.own, f32[1,1024]{1,0:T(1,128)} %bitcast.97, f32[64,1024]{1,0:T(8,128)} %probes.3), custom_call_target="tpu_custom_call" | custom-call | tf_op jit(solution)/shard_map/local_first/pallas_call | solution.py:580
  16.2 0.0 collective-permute-done.3.received.mate
  16.2 0.9 %mate_first.1 = (bf16[512,512]{1,0:T(8,128)(2,1)S(1)}, bf16[512,512]{1,0:T(8,128)(2,1)S(1)}, f32[64,1024]{1,0:T(8,128)S(1)}, f32[72,768]{1,0:T(8,128)S(1)}) custom-call(f32[8,1024]{1,0:T(8,128)S(1)} %get-tuple-element.309.own, f32[64,1024]{1,0:T(8,128)S(1)} %get-tuple-element.311.partial, f32[72,768]{1,0:T(8,128)S(1)} %collective-permute-done.3.received.mate, ...), custom_call_target="tpu_custom_call" | custom-call | tf_op jit(solution)/shard_map/mate_first/pallas_call | solution.py:594
  17.1 0.0 copy-start.3
  17.1 3.6 %collective-permute-start.6 = (f32[72,768]{1,0:T(8,128)S(1)}, f32[72,768]{1,0:T(8,128)S(1)}, u32[]{:S(2)}, u32[]{:S(2)}) collective-permute-start(f32[72,768]{1,0:T(8,128)S(1)} %get-tuple-element.323), channel_id=1, source_target_pairs={{1,2},{2,1},{3,4},{4,3},{5,6},{6,5},{7,8},{8,7},{9,10},{10,9},{11,... | collective-permute-start | bytes 663560 | tf_op jit(solution)/shard_map/ppermute | solution.py:552
  20.8 0.0 collective-permute-done.4.received
  20.8 2.3 %next_first.1 = (bf16[256,768]{1,0:T(8,128)(2,1)S(1)}, bf16[256,768]{1,0:T(8,128)(2,1)S(1)}, bf16[768,768]{1,0:T(8,128)(2,1)S(1)}, bf16[768,768]{1,0:T(8,128)(2,...) custom-call(f32[8,1024]{1,0:T(8,128)S(1)} %get-tuple-element.309.own, f32[64,1024]{1,0:T(8,128)S(1)} %get-tuple-element.314.partial, ...), custom_call_target="tpu_custom_call" | custom-call | tf_op jit(solution)/shard_map/next_first/pallas_call | solution.py:602
  23.1 1.9 %collective-permute-start.5 = (f32[64,768]{1,0:T(8,128)S(1)}, f32[64,768]{1,0:T(8,128)S(1)}, u32[]{:S(2)}, u32[]{:S(2)}) collective-permute-start(f32[64,768]{1,0:T(8,128)S(1)} %get-tuple-element.319), channel_id=1, source_target_pairs={{0,1},{1,0},{2,3},{3,2},{4,5},{5,4},{6,7},{7,6},{8,9},{9,8},{10,11... | collective-permute-start | bytes 589832 | tf_op jit(solution)/shard_map/ppermute | solution.py:548
  25.1 0.0 copy-done.3
  25.1 1.0 %local_second.1.partial = f32[64,1024]{1,0:T(8,128)S(1)} custom-call(f32[1,1024]{1,0:T(1,128)S(1)} %bitcast.98, f32[64,1024]{1,0:T(8,128)S(1)} %get-tuple-element.316.second, bf16[1024,1024]{1,0:T(8,128)(2,1)S(1)} %get-tuple-element.317.k_high, bf16[1024,1024]{1,0:T(8,128)(2,1)S(1)} %get-tuple-element.318.k_low), custom_call_target="tpu_custom_call" | custom-call | tf_op jit(solution)/shard_map/local_second/pallas_call | solution.py:611
  26.1 0.4 collective-permute-done.5.mate
  26.5 0.4 mate_second.1
  26.9 1.9 %collective-permute-start.8 = (f32[72,768]{1,0:T(8,128)S(1)}, f32[72,768]{1,0:T(8,128)S(1)}, u32[]{:S(2)}, u32[]{:S(2)}) collective-permute-start(f32[72,768]{1,0:T(8,128)S(1)} %get-tuple-element.331), channel_id=1, source_target_pairs={{1,2},{2,1},{3,4},{4,3},{5,6},{6,5},{7,8},{8,7},{9,10},{10,9},{11,... | collective-permute-start | bytes 663560 | tf_op jit(solution)/shard_map/ppermute | solution.py:552
  28.8 0.0 collective-permute-done.6.ahead
  28.8 1.4 %next_second.1 = (f32[64,1024]{1,0:T(8,128)S(1)}, f32[64,768]{1,0:T(8,128)S(1)}, f32[64,768]{1,0:T(8,128)S(1)}) custom-call(f32[64,1024]{1,0:T(8,128)S(1)} %get-tuple-element.322.partial, f32[64,1024]{1,0:T(8,128)S(1)} %get-tuple-element.310.first, f32[64,1024]{1,0:T(8,128)S(1)} %get-tuple-element.316.second, f32[64,768]{1,0:T(8,128)S(1)} %collective-permute-done.5.mate, ...), custom_call_target="tpu_custom_call" | custom-call | tf_op jit(solution)/shard_map/next_second/pallas_call | solution.py:618
  30.2 1.9 %collective-permute-start.7 = (f32[64,768]{1,0:T(8,128)S(1)}, f32[64,768]{1,0:T(8,128)S(1)}, u32[]{:S(2)}, u32[]{:S(2)}) collective-permute-start(f32[64,768]{1,0:T(8,128)S(1)} %get-tuple-element.330), channel_id=1, source_target_pairs={{0,1},{1,0},{2,3},{3,2},{4,5},{5,4},{6,7},{7,6},{8,9},{9,8},{10,11... | collective-permute-start | bytes 589832 | tf_op jit(solution)/shard_map/ppermute | solution.py:548
  32.1 1.0 %local_third.1 = (f32[64,1024]{1,0:T(8,128)S(1)}, f32[64,128]{1,0:T(8,128)S(1)}) custom-call(f32[1,1024]{1,0:T(1,128)S(1)} %bitcast.99, f32[64,1024]{1,0:T(8,128)S(1)} %get-tuple-element.310.first, f32[64,1024]{1,0:T(8,128)S(1)} %get-tuple-element.316.second, f32[64,1024]{1,0:T(8,128)S(1)} %get-tuple-element.328.third, ...), custom_call_target="tpu_custom_call" | custom-call | tf_op jit(solution)/shard_map/local_third/pallas_call | solution.py:627
  33.2 0.4 collective-permute-done.7.mate
  33.5 0.6 mate_third.1.partial
  34.2 0.0 collective-permute-done.8.after
  34.2 0.0 copy-start.2
  34.2 0.0 copy-start.4
  34.2 0.0 copy-start.5
  34.2 0.9 %next_third.1 = (f32[64,1024]{1,0:T(8,128)S(1)}, f32[32,4,128]{2,1,0:T(4,128)S(1)}) custom-call(f32[64,1024]{1,0:T(8,128)S(1)} %mate_third.1.partial, f32[72,768]{1,0:T(8,128)S(1)} %collective-permute-done.8.after, f32[64,768]{1,0:T(8,128)S(1)} %get-tuple-element.332.given, bf16[768,768]{1,0:T(8,128)(2,1)S(1)} %get-tuple-element.326.k_high, ...), custom_call_target="tpu_custom_call" | custom-call | tf_op jit(solution)/shard_map/next_third/pallas_call | solution.py:634
  35.1 23.6 %all_to_all.10 = f32[32,4,128]{2,1,0:T(4,128)S(1)} all-to-all(f32[32,4,128]{2,1,0:T(4,128)S(1)} %get-tuple-element.334), channel_id=1, replica_groups=mesh['region'=32,'sub'=16] {'region'}, dimensions={0} | all-to-all | bytes 131072 | tf_op jit(solution)/shard_map/all_to_all | solution.py:642
  58.7 12.7 %all_to_all.11.sums = f32[16,4,128]{2,1,0:T(4,128)S(1)} all-to-all(f32[16,4,128]{2,1,0:T(4,128)S(1)} %broadcast_in_dim.5), channel_id=1, replica_groups=mesh['region'=32,'sub'=16] {'sub'}, dimensions={0} | all-to-all | bytes 65536 | tf_op jit(solution)/shard_map/all_to_all | solution.py:643
  71.4 1.2 %finish.1 = (f32[64,1024]{1,0:T(8,128)}, f32[64,1024]{1,0:T(8,128)}, f32[1,1]{1,0:T(1,128)}) custom-call(f32[16,4,128]{2,1,0:T(4,128)S(1)} %all_to_all.11.sums, f32[64,1024]{1,0:T(8,128)S(1)} %get-tuple-element.310.first, f32[64,1024]{1,0:T(8,128)S(1)} %get-tuple-element.316.second, f32[64,1024]{1,0:T(8,128)S(1)} %get-tuple-element.328.third, ...), custom_call_target="tpu_custom_call" | custom-call | tf_op jit(solution)/shard_map/finish/pallas_call | solution.py:644
  72.6 0.0 copy-done.2
  72.6 0.0 copy-done.4
  72.6 0.0 copy-done.5
  72.6 0.8 %while.35 = (f32[1,1]{1,0:T(1,128)}, f32[64,1024]{1,0:T(8,128)}, f32[64,1024]{1,0:T(8,128)}, f32[64,1024]{1,0:T(8,128)S(1)}, f32[3,1024]{1,0:T(4,128)S(1)}, /*in...) while((f32[1,1]{1,0:T(1,128)}, f32[64,1024]{1,0:T(8,128)}, f32[64,1024]{1,0:T(8,128)}, ...), condition=%region_10.11_spmd, body=%region_1.10_spmd | while | flops 1439929600 | bytes 21131516 | solution.py:656
  (2 shorter events, 0.1 us)
Async XLA Ops:
  1.7 14.5 %collective-permute-start.3 = (f32[72,768]{1,0:T(8,128)S(1)}, f32[72,768]{1,0:T(8,128)S(1)}, u32[]{:S(2)}, u32[]{:S(2)}) collective-permute-start(f32[72,768]{1,0:T(8,128)S(1)} %get-tuple-element.312), channel_id=1, source_target_pairs={{0,1},{1,0},{2,3},{3,2},{4,5},{5,4},{6,7},{7,6},{8,9},{9,8},{10,11... | collective-permute-start | bytes 663560 | tf_op jit(solution)/shard_map/ppermute | solution.py:548
  10.5 10.3 %collective-permute-start.4 = (f32[72,768]{1,0:T(8,128)S(1)}, f32[72,768]{1,0:T(8,128)S(1)}, u32[]{:S(2)}, u32[]{:S(2)}) collective-permute-start(f32[72,768]{1,0:T(8,128)S(1)} %get-tuple-element.315), channel_id=1, source_target_pairs={{1,2},{2,1},{3,4},{4,3},{5,6},{6,5},{7,8},{8,7},{9,10},{10,9},{11,... | collective-permute-start | bytes 663560 | tf_op jit(solution)/shard_map/ppermute | solution.py:552
  17.1 8.0 %copy-start.3 = (f32[1024]{0:T(1024)S(1)}, f32[1024]{0:T(1024)}, u32[]{:S(2)}) copy-start(f32[1024]{0:T(1024)} %param.17) | copy-start | bytes 12292
  17.1 11.7 %collective-permute-start.6 = (f32[72,768]{1,0:T(8,128)S(1)}, f32[72,768]{1,0:T(8,128)S(1)}, u32[]{:S(2)}, u32[]{:S(2)}) collective-permute-start(f32[72,768]{1,0:T(8,128)S(1)} %get-tuple-element.323), channel_id=1, source_target_pairs={{1,2},{2,1},{3,4},{4,3},{5,6},{6,5},{7,8},{8,7},{9,10},{10,9},{11,... | collective-permute-start | bytes 663560 | tf_op jit(solution)/shard_map/ppermute | solution.py:552
  23.1 3.3 %collective-permute-start.5 = (f32[64,768]{1,0:T(8,128)S(1)}, f32[64,768]{1,0:T(8,128)S(1)}, u32[]{:S(2)}, u32[]{:S(2)}) collective-permute-start(f32[64,768]{1,0:T(8,128)S(1)} %get-tuple-element.319), channel_id=1, source_target_pairs={{0,1},{1,0},{2,3},{3,2},{4,5},{5,4},{6,7},{7,6},{8,9},{9,8},{10,11... | collective-permute-start | bytes 589832 | tf_op jit(solution)/shard_map/ppermute | solution.py:548
  26.9 7.3 %collective-permute-start.8 = (f32[72,768]{1,0:T(8,128)S(1)}, f32[72,768]{1,0:T(8,128)S(1)}, u32[]{:S(2)}, u32[]{:S(2)}) collective-permute-start(f32[72,768]{1,0:T(8,128)S(1)} %get-tuple-element.331), channel_id=1, source_target_pairs={{1,2},{2,1},{3,4},{4,3},{5,6},{6,5},{7,8},{8,7},{9,10},{10,9},{11,... | collective-permute-start | bytes 663560 | tf_op jit(solution)/shard_map/ppermute | solution.py:552
  30.2 3.3 %collective-permute-start.7 = (f32[64,768]{1,0:T(8,128)S(1)}, f32[64,768]{1,0:T(8,128)S(1)}, u32[]{:S(2)}, u32[]{:S(2)}) collective-permute-start(f32[64,768]{1,0:T(8,128)S(1)} %get-tuple-element.330), channel_id=1, source_target_pairs={{0,1},{1,0},{2,3},{3,2},{4,5},{5,4},{6,7},{7,6},{8,9},{9,8},{10,11... | collective-permute-start | bytes 589832 | tf_op jit(solution)/shard_map/ppermute | solution.py:548
  34.2 38.4 %copy-start.2 = (f32[64,1024]{1,0:T(8,128)S(1)}, f32[64,1024]{1,0:T(8,128)}, u32[]{:S(2)}) copy-start(f32[64,1024]{1,0:T(8,128)} %probes.3) | copy-start | bytes 786436
  34.2 38.4 %copy-start.4 = (f32[3,1024]{1,0:T(4,128)S(1)}, f32[3,1024]{1,0:T(4,128)}, u32[]{:S(2)}) copy-start(f32[3,1024]{1,0:T(4,128)} %coords.1) | copy-start | bytes 36868
  34.2 38.4 %copy-start.5 = (s32[3,4]{1,0:T(4,128)S(1)}, s32[3,4]{1,0:T(4,128)}, u32[]{:S(2)}) copy-start(s32[3,4]{1,0:T(4,128)} %pair.1) | copy-start | bytes 148

commit v7 on v6

--- a/solution.py
+++ b/solution.py
@@ -135,6 +135,7 @@
     low, high = extra[:, 0:span], extra[:, here - span :]
     to_mate[rows : rows + 8, :] = jnp.where(right, high, low)
     to_next[rows : rows + 8, :] = jnp.where(right, low, high)
+    to_next[rows + 8 :, :] = jnp.zeros((to_next.shape[0] - rows - 8, span), F32)
     copies[2].wait()
     copies[3].wait()
 
@@ -276,10 +277,9 @@
         step()
 
 
-def halo_rows(right, own, received, rows, links, ns):
+def halo_rows(right, own, received, at, rows, links, ns):
     length = received.shape[1] // links
     blocks = own.shape[1] // length
-    at = received.shape[0] - 8
     place = [pl.ds(halo_place(right, links, length, h), length) for h in range(links)]
     for h in range(max(ns)):
         for d in range(1, 3):
@@ -362,7 +362,7 @@
     right = is_right(True)
     length = halves.shape[1] // links
     ns = range(1, links)
-    halo_rows(right, own, received, rows, links, ns)
+    halo_rows(right, own, received, out.shape[0], rows, links, ns)
     out[...] = partial[...]
     tables = table_rows(k_high, k_low, ns, length)
     for step in fill_halo(right, received, columns, tables, out, halves, rows, links, []):
@@ -393,8 +393,8 @@
     out[...] = partial[...]
     left, right = is_right(True), is_right(False)
     late, ns = range(links, links + 1), range(1, links + 1)
-    halo_rows(left, own, mate, mate_rows, links, late)
-    halo_rows(right, own, received, rows, links, ns)
+    halo_rows(left, own, mate, out.shape[0], mate_rows, links, late)
+    halo_rows(right, own, received, out.shape[0], rows, links, ns)
     tables = table_rows(mate_high, mate_low, late, length)
     steps = fill_halo(left, mate, columns, tables, out, mate_halves, mate_rows, links, [])
     tables = table_rows(k_high, k_low, ns, length)
@@ -562,6 +562,7 @@
     whole = jax.ShapeDtypeStruct((rows, here), F32)
     part = jax.ShapeDtypeStruct((rows, span), F32)
     packed = jax.ShapeDtypeStruct((rows + 8, span), F32)
+    wide_packed = jax.ShapeDtypeStruct((rows + 16, span), F32)
     wide_part = jax.ShapeDtypeStruct((rows + 8, span), F32)
     sums_table = jax.ShapeDtypeStruct((rows, 128), F32)
     local_table = jax.ShapeDtypeStruct((here, here), BF16)
@@ -572,7 +573,7 @@
     to_mate, to_next, own = call(
         pack_kernel,
         "pack",
-        (packed, packed, jax.ShapeDtypeStruct((8, here), F32)),
+        (packed, wide_packed, jax.ShapeDtypeStruct((8, here), F32)),
         [ANY, ANY, ANY],
         [pltpu.VMEM((3, here), F32), pltpu.SMEM((links, blocks), jnp.int32), pltpu.SemaphoreType.DMA((4,))],
     )(coords, pair_list, probes)

time: 73.9 us -> 73.4 us (level)
  starting transfers between devices: 20.1 us -> 18.9 us
  blocking collectives: 36.2 us -> 37 us
    ppermute x3, starting transfers between devices: 12.6 us -> 8.71 us  [swap_mate(): lax.ppermute(array, AXES, [(i, i ^ 1) for i in range(lax.axis_size(AXES))])]
    ppermute x3, starting transfers between devices: 7.49 us -> 10.2 us  [swap_next(): lax.ppermute(array, AXES, [(i, i + 1 if i % 2 else i - 1) for i in range(...]
where the time goes in v7:
time: 73.4 us; the launch traced here: 73 us
  blocking collectives  37 us (50%)
  starting transfers between devices  18.9 us (26%)
  Pallas kernels  14.6 us (20%)
  between operations  1 us (1%)
  loops' own time  0.81 us (1%)
  waiting for transfers between devices  0.74 us (1%)
    all_to_all x1, blocking collectives, per_device(): sums = jnp.sum(lax.all_to_all(sums, 'region', 0, 0), axis=0)  24.1 us
    all_to_all x1, blocking collectives, per_device(): lax.all_to_all(jnp.broadcast_to(sums[None], (subs, 4, 128)), 'sub', 0, 0)  12.8 us
    ppermute x3, starting transfers between devices, swap_next(): lax.ppermute(array, AXES, [(i, i + 1 if i % 2 else i - 1) for i in range(...  10.2 us
    ppermute x3, starting transfers between devices, swap_mate(): lax.ppermute(array, AXES, [(i, i ^ 1) for i in range(lax.axis_size(AXES))])  8.71 us
    pallas_call x1, Pallas kernels, per_device(): call(functools.partial(local_first_kernel, links=links), 'local_first', (...  3.73 us
    pallas_call x1, Pallas kernels, per_device(): call(functools.partial(next_first_kernel, links=links), 'next_first', (la...  2.34 us
  transfers between devices with their start and end apart: 6, of which 2 were waited for; matrix products, arithmetic and copies ran while one was open for 0% of the time, Pallas kernels for 16%

profile of v7, /device:TPU:1, one launch (start us, length us, event | category | flops | bytes accessed | tf_op | source)
XLA Modules:
  0.0 73.0 jit_solution(17116033220019734557)
XLA Ops:
  0.6 1.1 %pack.1 = (f32[72,768]{1,0:T(8,128)S(1)}, f32[80,768]{1,0:T(8,128)S(1)}, f32[8,1024]{1,0:T(8,128)S(1)}) custom-call(f32[3,1024]{1,0:T(4,128)} %coords.1, s32[3,4]{1,0:T(4,128)} %pair.1, f32[64,1024]{1,0:T(8,128)} %probes.3), custom_call_target="tpu_custom_call" | custom-call | tf_op jit(solution)/shard_map/pack/pallas_call | solution.py:573
  1.7 4.6 %collective-permute-start.4 = (f32[80,768]{1,0:T(8,128)S(1)}, f32[80,768]{1,0:T(8,128)S(1)}, u32[]{:S(2)}, u32[]{:S(2)}) collective-permute-start(f32[80,768]{1,0:T(8,128)S(1)} %get-tuple-element.315), channel_id=1, source_target_pairs={{1,2},{2,1},{3,4},{4,3},{5,6},{6,5},{7,8},{8,7},{9,10},{10,9},{11,... | collective-permute-start | bytes 737288 | tf_op jit(solution)/shard_map/ppermute | solution.py:552
  6.3 4.9 %collective-permute-start.3 = (f32[72,768]{1,0:T(8,128)S(1)}, f32[72,768]{1,0:T(8,128)S(1)}, u32[]{:S(2)}, u32[]{:S(2)}) collective-permute-start(f32[72,768]{1,0:T(8,128)S(1)} %get-tuple-element.312), channel_id=1, source_target_pairs={{0,1},{1,0},{2,3},{3,2},{4,5},{5,4},{6,7},{7,6},{8,9},{9,8},{10,11... | collective-permute-start | bytes 663560 | tf_op jit(solution)/shard_map/ppermute | solution.py:548
  11.2 3.7 %local_first.1 = (bf16[1024,1024]{1,0:T(8,128)(2,1)S(1)}, bf16[1024,1024]{1,0:T(8,128)(2,1)S(1)}, f32[64,1024]{1,0:T(8,128)S(1)}, f32[64,1024]{1,0:T(8,128)S(1)}, f32[3,1024,128]{2,1,0:T(8,128)S(1)}) custom-call(f32[8,1024]{1,0:T(8,128)S(1)} %get-tuple-element.309.own, f32[1,1024]{1,0:T(1,128)} %bitcast.97, f32[64,1024]{1,0:T(8,128)} %probes.3), custom_call_target="tpu_custom_call" | custom-call | tf_op jit(solution)/shard_map/local_first/pallas_call | solution.py:581
  14.9 0.0 collective-permute-done.3.received.mate
  14.9 0.9 %mate_first.1 = (bf16[512,512]{1,0:T(8,128)(2,1)S(1)}, bf16[512,512]{1,0:T(8,128)(2,1)S(1)}, f32[64,1024]{1,0:T(8,128)S(1)}, f32[72,768]{1,0:T(8,128)S(1)}) custom-call(f32[8,1024]{1,0:T(8,128)S(1)} %get-tuple-element.309.own, f32[64,1024]{1,0:T(8,128)S(1)} %get-tuple-element.311.partial, f32[72,768]{1,0:T(8,128)S(1)} %collective-permute-done.3.received.mate, ...), custom_call_target="tpu_custom_call" | custom-call | tf_op jit(solution)/shard_map/mate_first/pallas_call | solution.py:595
  15.9 0.0 copy-start.3
  15.9 1.9 %collective-permute-start.6 = (f32[72,768]{1,0:T(8,128)S(1)}, f32[72,768]{1,0:T(8,128)S(1)}, u32[]{:S(2)}, u32[]{:S(2)}) collective-permute-start(f32[72,768]{1,0:T(8,128)S(1)} %get-tuple-element.323), channel_id=1, source_target_pairs={{1,2},{2,1},{3,4},{4,3},{5,6},{6,5},{7,8},{8,7},{9,10},{10,9},{11,... | collective-permute-start | bytes 663560 | tf_op jit(solution)/shard_map/ppermute | solution.py:552
  17.8 0.0 collective-permute-done.4.received
  17.8 2.3 %next_first.1 = (bf16[256,768]{1,0:T(8,128)(2,1)S(1)}, bf16[256,768]{1,0:T(8,128)(2,1)S(1)}, bf16[768,768]{1,0:T(8,128)(2,1)S(1)}, bf16[768,768]{1,0:T(8,128)(2,...) custom-call(f32[8,1024]{1,0:T(8,128)S(1)} %get-tuple-element.309.own, f32[64,1024]{1,0:T(8,128)S(1)} %get-tuple-element.314.partial, ...), custom_call_target="tpu_custom_call" | custom-call | tf_op jit(solution)/shard_map/next_first/pallas_call | solution.py:603
  20.2 1.9 %collective-permute-start.5 = (f32[64,768]{1,0:T(8,128)S(1)}, f32[64,768]{1,0:T(8,128)S(1)}, u32[]{:S(2)}, u32[]{:S(2)}) collective-permute-start(f32[64,768]{1,0:T(8,128)S(1)} %get-tuple-element.319), channel_id=1, source_target_pairs={{0,1},{1,0},{2,3},{3,2},{4,5},{5,4},{6,7},{7,6},{8,9},{9,8},{10,11... | collective-permute-start | bytes 589832 | tf_op jit(solution)/shard_map/ppermute | solution.py:548
  22.1 0.0 copy-done.3
  22.1 1.0 %local_second.1.partial = f32[64,1024]{1,0:T(8,128)S(1)} custom-call(f32[1,1024]{1,0:T(1,128)S(1)} %bitcast.98, f32[64,1024]{1,0:T(8,128)S(1)} %get-tuple-element.316.second, bf16[1024,1024]{1,0:T(8,128)(2,1)S(1)} %get-tuple-element.317.k_high, bf16[1024,1024]{1,0:T(8,128)(2,1)S(1)} %get-tuple-element.318.k_low), custom_call_target="tpu_custom_call" | custom-call | tf_op jit(solution)/shard_map/local_second/pallas_call | solution.py:612
  23.1 0.4 collective-permute-done.5.mate
  23.5 0.4 mate_second.1
  23.9 3.6 %collective-permute-start.8 = (f32[72,768]{1,0:T(8,128)S(1)}, f32[72,768]{1,0:T(8,128)S(1)}, u32[]{:S(2)}, u32[]{:S(2)}) collective-permute-start(f32[72,768]{1,0:T(8,128)S(1)} %get-tuple-element.331), channel_id=1, source_target_pairs={{1,2},{2,1},{3,4},{4,3},{5,6},{6,5},{7,8},{8,7},{9,10},{10,9},{11,... | collective-permute-start | bytes 663560 | tf_op jit(solution)/shard_map/ppermute | solution.py:552
  27.6 0.0 collective-permute-done.6.ahead
  27.6 1.4 %next_second.1 = (f32[64,1024]{1,0:T(8,128)S(1)}, f32[64,768]{1,0:T(8,128)S(1)}, f32[64,768]{1,0:T(8,128)S(1)}) custom-call(f32[64,1024]{1,0:T(8,128)S(1)} %get-tuple-element.322.partial, f32[64,1024]{1,0:T(8,128)S(1)} %get-tuple-element.310.first, f32[64,1024]{1,0:T(8,128)S(1)} %get-tuple-element.316.second, f32[64,768]{1,0:T(8,128)S(1)} %collective-permute-done.5.mate, ...), custom_call_target="tpu_custom_call" | custom-call | tf_op jit(solution)/shard_map/next_second/pallas_call | solution.py:619
  29.0 1.9 %collective-permute-start.7 = (f32[64,768]{1,0:T(8,128)S(1)}, f32[64,768]{1,0:T(8,128)S(1)}, u32[]{:S(2)}, u32[]{:S(2)}) collective-permute-start(f32[64,768]{1,0:T(8,128)S(1)} %get-tuple-element.330), channel_id=1, source_target_pairs={{0,1},{1,0},{2,3},{3,2},{4,5},{5,4},{6,7},{7,6},{8,9},{9,8},{10,11... | collective-permute-start | bytes 589832 | tf_op jit(solution)/shard_map/ppermute | solution.py:548
  30.9 1.0 %local_third.1 = (f32[64,1024]{1,0:T(8,128)S(1)}, f32[64,128]{1,0:T(8,128)S(1)}) custom-call(f32[1,1024]{1,0:T(1,128)S(1)} %bitcast.99, f32[64,1024]{1,0:T(8,128)S(1)} %get-tuple-element.310.first, f32[64,1024]{1,0:T(8,128)S(1)} %get-tuple-element.316.second, f32[64,1024]{1,0:T(8,128)S(1)} %get-tuple-element.328.third, ...), custom_call_target="tpu_custom_call" | custom-call | tf_op jit(solution)/shard_map/local_third/pallas_call | solution.py:628
  31.9 0.4 collective-permute-done.7.mate
  32.3 0.6 mate_third.1.partial
  32.9 0.0 collective-permute-done.8.after
  32.9 0.0 copy-start.2
  33.0 0.0 copy-start.4
  33.0 0.0 copy-start.5
  33.0 0.9 %next_third.1 = (f32[64,1024]{1,0:T(8,128)S(1)}, f32[32,4,128]{2,1,0:T(4,128)S(1)}) custom-call(f32[64,1024]{1,0:T(8,128)S(1)} %mate_third.1.partial, f32[72,768]{1,0:T(8,128)S(1)} %collective-permute-done.8.after, f32[64,768]{1,0:T(8,128)S(1)} %get-tuple-element.332.given, bf16[768,768]{1,0:T(8,128)(2,1)S(1)} %get-tuple-element.326.k_high, ...), custom_call_target="tpu_custom_call" | custom-call | tf_op jit(solution)/shard_map/next_third/pallas_call | solution.py:635
  33.9 24.1 %all_to_all.10 = f32[32,4,128]{2,1,0:T(4,128)S(1)} all-to-all(f32[32,4,128]{2,1,0:T(4,128)S(1)} %get-tuple-element.334), channel_id=1, replica_groups=mesh['region'=32,'sub'=16] {'region'}, dimensions={0} | all-to-all | bytes 131072 | tf_op jit(solution)/shard_map/all_to_all | solution.py:643
  58.0 12.8 %all_to_all.11.sums = f32[16,4,128]{2,1,0:T(4,128)S(1)} all-to-all(f32[16,4,128]{2,1,0:T(4,128)S(1)} %broadcast_in_dim.5), channel_id=1, replica_groups=mesh['region'=32,'sub'=16] {'sub'}, dimensions={0} | all-to-all | bytes 65536 | tf_op jit(solution)/shard_map/all_to_all | solution.py:644
  70.9 1.2 %finish.1 = (f32[64,1024]{1,0:T(8,128)}, f32[64,1024]{1,0:T(8,128)}, f32[1,1]{1,0:T(1,128)}) custom-call(f32[16,4,128]{2,1,0:T(4,128)S(1)} %all_to_all.11.sums, f32[64,1024]{1,0:T(8,128)S(1)} %get-tuple-element.310.first, f32[64,1024]{1,0:T(8,128)S(1)} %get-tuple-element.316.second, f32[64,1024]{1,0:T(8,128)S(1)} %get-tuple-element.328.third, ...), custom_call_target="tpu_custom_call" | custom-call | tf_op jit(solution)/shard_map/finish/pallas_call | solution.py:645
  72.0 0.0 copy-done.2
  72.1 0.0 copy-done.4
  72.1 0.0 copy-done.5
  72.1 0.8 %while.35 = (f32[1,1]{1,0:T(1,128)}, f32[64,1024]{1,0:T(8,128)}, f32[64,1024]{1,0:T(8,128)}, f32[64,1024]{1,0:T(8,128)S(1)}, f32[3,1024]{1,0:T(4,128)S(1)}, /*in...) while((f32[1,1]{1,0:T(1,128)}, f32[64,1024]{1,0:T(8,128)}, f32[64,1024]{1,0:T(8,128)}, ...), condition=%region_10.11_spmd, body=%region_1.10_spmd | while | flops 1439929600 | bytes 21131516 | solution.py:657
  (2 shorter events, 0.1 us)
Async XLA Ops:
  1.7 16.1 %collective-permute-start.4 = (f32[80,768]{1,0:T(8,128)S(1)}, f32[80,768]{1,0:T(8,128)S(1)}, u32[]{:S(2)}, u32[]{:S(2)}) collective-permute-start(f32[80,768]{1,0:T(8,128)S(1)} %get-tuple-element.315), channel_id=1, source_target_pairs={{1,2},{2,1},{3,4},{4,3},{5,6},{6,5},{7,8},{8,7},{9,10},{10,9},{11,... | collective-permute-start | bytes 737288 | tf_op jit(solution)/shard_map/ppermute | solution.py:552
  6.3 8.6 %collective-permute-start.3 = (f32[72,768]{1,0:T(8,128)S(1)}, f32[72,768]{1,0:T(8,128)S(1)}, u32[]{:S(2)}, u32[]{:S(2)}) collective-permute-start(f32[72,768]{1,0:T(8,128)S(1)} %get-tuple-element.312), channel_id=1, source_target_pairs={{0,1},{1,0},{2,3},{3,2},{4,5},{5,4},{6,7},{7,6},{8,9},{9,8},{10,11... | collective-permute-start | bytes 663560 | tf_op jit(solution)/shard_map/ppermute | solution.py:548
  15.9 6.2 %copy-start.3 = (f32[1024]{0:T(1024)S(1)}, f32[1024]{0:T(1024)}, u32[]{:S(2)}) copy-start(f32[1024]{0:T(1024)} %param.17) | copy-start | bytes 12292
  15.9 11.7 %collective-permute-start.6 = (f32[72,768]{1,0:T(8,128)S(1)}, f32[72,768]{1,0:T(8,128)S(1)}, u32[]{:S(2)}, u32[]{:S(2)}) collective-permute-start(f32[72,768]{1,0:T(8,128)S(1)} %get-tuple-element.323), channel_id=1, source_target_pairs={{1,2},{2,1},{3,4},{4,3},{5,6},{6,5},{7,8},{8,7},{9,10},{10,9},{11,... | collective-permute-start | bytes 663560 | tf_op jit(solution)/shard_map/ppermute | solution.py:552
  20.2 3.3 %collective-permute-start.5 = (f32[64,768]{1,0:T(8,128)S(1)}, f32[64,768]{1,0:T(8,128)S(1)}, u32[]{:S(2)}, u32[]{:S(2)}) collective-permute-start(f32[64,768]{1,0:T(8,128)S(1)} %get-tuple-element.319), channel_id=1, source_target_pairs={{0,1},{1,0},{2,3},{3,2},{4,5},{5,4},{6,7},{7,6},{8,9},{9,8},{10,11... | collective-permute-start | bytes 589832 | tf_op jit(solution)/shard_map/ppermute | solution.py:548
  23.9 9.0 %collective-permute-start.8 = (f32[72,768]{1,0:T(8,128)S(1)}, f32[72,768]{1,0:T(8,128)S(1)}, u32[]{:S(2)}, u32[]{:S(2)}) collective-permute-start(f32[72,768]{1,0:T(8,128)S(1)} %get-tuple-element.331), channel_id=1, source_target_pairs={{1,2},{2,1},{3,4},{4,3},{5,6},{6,5},{7,8},{8,7},{9,10},{10,9},{11,... | collective-permute-start | bytes 663560 | tf_op jit(solution)/shard_map/ppermute | solution.py:552
  29.0 3.3 %collective-permute-start.7 = (f32[64,768]{1,0:T(8,128)S(1)}, f32[64,768]{1,0:T(8,128)S(1)}, u32[]{:S(2)}, u32[]{:S(2)}) collective-permute-start(f32[64,768]{1,0:T(8,128)S(1)} %get-tuple-element.330), channel_id=1, source_target_pairs={{0,1},{1,0},{2,3},{3,2},{4,5},{5,4},{6,7},{7,6},{8,9},{9,8},{10,11... | collective-permute-start | bytes 589832 | tf_op jit(solution)/shard_map/ppermute | solution.py:548
  32.9 39.1 %copy-start.2 = (f32[64,1024]{1,0:T(8,128)S(1)}, f32[64,1024]{1,0:T(8,128)}, u32[]{:S(2)}) copy-start(f32[64,1024]{1,0:T(8,128)} %probes.3) | copy-start | bytes 786436
  33.0 39.1 %copy-start.4 = (f32[3,1024]{1,0:T(4,128)S(1)}, f32[3,1024]{1,0:T(4,128)}, u32[]{:S(2)}) copy-start(f32[3,1024]{1,0:T(4,128)} %coords.1) | copy-start | bytes 36868
  33.0 39.1 %copy-start.5 = (s32[3,4]{1,0:T(4,128)S(1)}, s32[3,4]{1,0:T(4,128)}, u32[]{:S(2)}) copy-start(s32[3,4]{1,0:T(4,128)} %pair.1) | copy-start | bytes 148

commit v8 on v7

--- a/solution.py
+++ b/solution.py
@@ -140,13 +140,13 @@
     copies[3].wait()
 
 
-def column_steps(columns, at, block):
+def column_steps(columns, at, load):
     def fill(d, turned):
         size = turned.shape[0]
         columns[d, at : at + size, :] = jnp.broadcast_to(turned[:, d : d + 1], (size, 128))
 
     def step():
-        turned = jnp.transpose(block)
+        turned = jnp.transpose(load())
         for d in range(3):
             fill(d, turned)
 
@@ -242,7 +242,7 @@
     return steps
 
 
-def local_first_kernel(own, noise, probes, k_high, k_low, out, first, columns, halves, rows, sem, *, links):
+def local_first_kernel(own, noise, probes, k_high, k_low, out, first, halves, columns, rows, sem, *, links):
     here = own.shape[1]
     blocks = links + 1
     length = here // blocks
@@ -254,7 +254,7 @@
     for j in range(blocks):
         half = length // 2
         for at in (j * length, j * length + half):
-            steps += column_steps(columns, at, 4.0 * own[:, at : at + half])
+            steps += column_steps(columns, at, lambda at=at: 4.0 * own[:, at : at + half])
     for step in steps[0:2]:
         step()
     steps = steps[2:]
@@ -277,54 +277,67 @@
         step()
 
 
-def halo_rows(right, own, received, at, rows, links, ns):
+def halo_columns(right, received, at, columns, links, h):
+    length = received.shape[1] // links
+    half = length // 2
+    steps = []
+    for part in range(2):
+        place = pl.ds(pl.multiple_of(halo_place(right, links, length, h) + part * half, 128), half)
+        steps += column_steps(columns, h * length + part * half, lambda place=place: 4.0 * received[at : at + 8, place])
+    return steps
+
+
+def own_rows(right, own, received, at, rows, links, pieces):
     length = received.shape[1] // links
     blocks = own.shape[1] // length
-    place = [pl.ds(halo_place(right, links, length, h), length) for h in range(links)]
-    for h in range(max(ns)):
+    for n in sorted({n for _, ns in pieces for n in ns}):
+        mine = pl.ds(own_place(right, blocks, links, length, n), length)
+        lanes = slice((n - 1) * length, n * length)
         for d in range(1, 3):
-            coord = 4.0 * received[at + d : at + d + 1, place[h]]
-            rows[d, :, h * length : (h + 1) * length] = jnp.broadcast_to(coord, (8, length))
-    for n in ns:
-        mine = own_place(right, blocks, links, length, n)
-        for h in range(n):
+            rows[d, :, lanes] = jnp.broadcast_to(4.0 * own[d : d + 1, mine], (8, length))
+        for h, ns in pieces:
+            if n not in ns:
+                continue
             k = links - n + h
-            ours = own[3 + k : 4 + k, pl.ds(mine, length)]
-            theirs = received[at + 3 + k : at + 4 + k, place[h]]
-            coord = 4.0 * received[at : at + 1, place[h]]
+            ours = own[3 + k : 4 + k, mine]
+            theirs = received[at + 3 + k : at + 4 + k, pl.ds(halo_place(right, links, length, h), length)]
+            coord = 4.0 * own[0:1, mine]
             coord = jnp.where(jnp.where(right, ours, theirs) == 1.0, coord, coord + FAR)
-            rows[2 + n, :, h * length : (h + 1) * length] = jnp.broadcast_to(coord, (8, length))
-
-
-def fill_halo(right, received, columns, tables, out, halves, rows, links, beside):
+            rows[3 + h, :, lanes] = jnp.broadcast_to(coord, (8, length))
+
+
+def fill_halo(right, received, columns, pieces, out, halves, rows, links, beside):
     probe_count = out.shape[0]
     length = received.shape[1] // links
     blocks = out.shape[1] // length
-    for h in range(max(tables)):
+    for h in range(max(h for h, _, _ in pieces) + 1):
         place = pl.ds(halo_place(right, links, length, h), length)
         store_halves(halves, h * length, received[0:probe_count, place])
 
-    def product(n, h):
+    def product(h, n, k_high, k_low, lanes):
         own = pl.ds(own_place(right, blocks, links, length, n), length)
         at = slice(h * length, (h + 1) * length)
-        k_high, k_low = tables[n]
 
         def step():
-            out[:, own] = out[:, own] + multiply(halves[:, at], k_high[:, at], k_low[:, at], turned=True)
+            out[:, own] = out[:, own] + multiply(halves[:, at], k_high[:, lanes], k_low[:, lanes])
 
         return step
 
-    for n in sorted(tables, reverse=True):
-        mine = own_place(right, blocks, links, length, n)
-        k_high, k_low = tables[n]
-        fill_tiles(k_high, k_low, 0, columns, mine, length, rows, 2 + n, slice(0, n * length), 0, beside)
-        beside = [product(n, h) for h in range(n)]
+    for h, ns, (k_high, k_low) in pieces:
+        lanes = slice((ns[0] - 1) * length, ns[-1] * length)
+        fill_tiles(k_high, k_low, 0, columns, h * length, length, rows, 3 + h, lanes, 0, beside)
+        beside = []
+        for n in ns:
+            beside.append(product(h, n, k_high, k_low, slice((n - ns[0]) * length, (n - ns[0] + 1) * length)))
     return beside
 
 
-def table_rows(k_high, k_low, ns, length):
-    parts = {n: (pl.ds((n - ns[0]) * length, length), slice(0, n * length)) for n in ns}
-    return {n: (k_high.at[part], k_low.at[part]) for n, part in parts.items()}
+def part_of(tables, rows, lanes):
+    return tuple(table.at[rows, lanes] for table in tables)
+
+
+def early_tables(tables, links, length):
+    return {n: part_of(tables, slice(0, n * length), slice((n - 1) * length, n * length)) for n in range(1, links)}
 
 
 def halo_product(right, load, tables, out, halves, links):
@@ -334,20 +347,21 @@
         store_halves(halves, h * length, load(pl.ds(halo_place(right, links, length, h), length)))
     for n, (k_high, k_low) in tables.items():
         own = pl.ds(own_place(right, blocks, links, length, n), length)
-        out[:, own] = out[:, own] + multiply(halves[:, 0 : n * length], k_high[...], k_low[...], turned=True)
-
-
-def own_product(right, vector, k_high, k_low, out, halves, blocks):
+        out[:, own] = out[:, own] + multiply(halves[:, 0 : n * length], k_high[...], k_low[...])
+
+
+def own_product(right, vector, tables, out, halves, blocks):
     span = out.shape[1]
     length = vector.shape[1] // blocks
     links = span // length
+    k_high, k_low = tables
     for n in range(1, links + 1):
         own = pl.ds(own_place(right, blocks, links, length, n), length)
         store_halves(halves, (n - 1) * length, vector[:, own])
     for h in range(links):
         deep, at = slice(h * length, span), slice(h * length, (h + 1) * length)
         place = pl.ds(halo_place(right, links, length, h), length)
-        out[:, place] = multiply(halves[:, deep], k_high[deep, at], k_low[deep, at])
+        out[:, place] = multiply(halves[:, deep], k_high[at, deep], k_low[at, deep], turned=True)
 
 
 def store_send(right, vector, send):
@@ -358,14 +372,43 @@
         send[rows:, :] = jnp.zeros((send.shape[0] - rows, span), F32)
 
 
-def mate_first_kernel(own, partial, received, columns, k_high, k_low, out, to_next, halves, rows, *, links):
+def store_tiles(right, vector, send):
+    here, count = vector.shape[1], vector.shape[0] // 8
+    wide = (send.shape[0] - 1) // count
+    start = send_place(right, here, wide * 128)
+    for c in range(wide):
+        lanes = pl.ds(pl.multiple_of(start + c * 128, 128), 128)
+        send[c * count : (c + 1) * count] = vector[:, lanes].reshape(count, 8, 128)
+    send[wide * count :] = jnp.zeros((1, 8, 128), F32)
+
+
+def load_tiles(received, rows, at):
+    count = rows // 8
+    parts = []
+    for c in range(at.size // 128):
+        tile = (at.start // 128 + c) * count
+        parts.append(received[pl.ds(tile, count)].reshape(rows, 128))
+    return jnp.concatenate(parts, axis=1)
+
+
+def mate_first_kernel(own, partial, received, k_high, k_low, out, to_next, columns, halves, rows, *, links):
     right = is_right(True)
     length = halves.shape[1] // links
-    ns = range(1, links)
-    halo_rows(right, own, received, out.shape[0], rows, links, ns)
+    at = out.shape[0]
+    pieces = [(h, range(h + 1, links)) for h in range(links - 1)]
+    steps = []
+    for h in range(links):
+        steps += halo_columns(right, received, at, columns, links, h)
+    for step in steps[0:2]:
+        step()
+    own_rows(right, own, received, at, rows, links, pieces)
     out[...] = partial[...]
-    tables = table_rows(k_high, k_low, ns, length)
-    for step in fill_halo(right, received, columns, tables, out, halves, rows, links, []):
+    tables = (k_high, k_low)
+    pieces = [
+        (h, ns, part_of(tables, slice(h * length, (h + 1) * length), slice(h * length, (links - 1) * length)))
+        for h, ns in pieces
+    ]
+    for step in fill_halo(right, received, columns, pieces, out, halves, rows, links, steps[2:]):
         step()
     store_send(is_right(False), out, to_next)
 
@@ -374,8 +417,8 @@
     own,
     partial,
     mate,
+    mate_columns,
     received,
-    columns,
     mate_high,
     mate_low,
     k_high,
@@ -386,19 +429,30 @@
     mate_rows,
     halves,
     rows,
+    columns,
     *,
     links,
 ):
     length = halves.shape[1] // links
+    at = out.shape[0]
     out[...] = partial[...]
     left, right = is_right(True), is_right(False)
-    late, ns = range(links, links + 1), range(1, links + 1)
-    halo_rows(left, own, mate, out.shape[0], mate_rows, links, late)
-    halo_rows(right, own, received, out.shape[0], rows, links, ns)
-    tables = table_rows(mate_high, mate_low, late, length)
-    steps = fill_halo(left, mate, columns, tables, out, mate_halves, mate_rows, links, [])
-    tables = table_rows(k_high, k_low, ns, length)
-    for step in fill_halo(right, received, columns, tables, out, halves, rows, links, steps):
+    late = [(h, range(links, links + 1)) for h in range(links)]
+    all_of = [(h, range(h + 1, links + 1)) for h in range(links)]
+    own_rows(left, own, mate, at, mate_rows, links, late)
+    own_rows(right, own, received, at, rows, links, all_of)
+    steps = []
+    for h in range(links):
+        steps += halo_columns(right, received, at, columns, links, h)
+    tables = (mate_high, mate_low)
+    pieces = [(h, ns, part_of(tables, slice(h * length, (h + 1) * length), slice(0, length))) for h, ns in late]
+    steps = fill_halo(left, mate, mate_columns, pieces, out, mate_halves, mate_rows, links, steps)
+    tables = (k_high, k_low)
+    pieces = [
+        (h, ns, part_of(tables, slice(h * length, (h + 1) * length), slice(h * length, links * length)))
+        for h, ns in all_of
+    ]
+    for step in fill_halo(right, received, columns, pieces, out, halves, rows, links, steps):
         step()
     store_send(is_right(True), out, to_mate)
 
@@ -418,8 +472,11 @@
     local_product(noise, second, k_high, k_low, out, halves, length)
 
 
-def local_third_kernel(noise, first, second, third, k_high, k_low, out, table, halves, *, length):
+def local_third_kernel(
+    noise, first, second, third, k_high, k_low, next_high, next_low, out, given, table, halves, own_halves, *, length
+):
     local_product(noise, third, k_high, k_low, out, halves, length)
+    own_product(is_right(False), second, (next_high, next_low), given, own_halves, out.shape[1] // length)
     terms = ((0, first, first), (1, first, second), (2, second, second), (3, second, third), (4, third, third))
     table[...] = add_sums(jnp.zeros(table.shape, F32), terms)
 
@@ -427,24 +484,26 @@
 def mate_second_kernel(partial, mate, k_high, k_low, out, to_next, halves, *, links):
     length = halves.shape[1] // links
     out[...] = partial[...]
-    tables = table_rows(k_high, k_low, range(1, links), length)
+    tables = early_tables((k_high, k_low), links, length)
     halo_product(is_right(True), lambda at: mate[:, at], tables, out, halves, links)
-    store_send(is_right(False), out, to_next)
+    store_tiles(is_right(False), out, to_next)
+
+
+def next_tables(tables, links, length):
+    return {n: part_of(tables, slice(0, n * length), slice((n - 1) * length, n * length)) for n in range(1, links + 1)}
 
 
 def next_second_kernel(
-    partial, first, second, mate, ahead, mate_high, mate_low, k_high, k_low, out, given, to_mate, halves, *, links
+    partial, first, mate, ahead, mate_high, mate_low, k_high, k_low, out, to_mate, halves, given, *, links
 ):
     length = halves.shape[1] // links
     right = is_right(False)
     out[...] = partial[...]
-    tables = table_rows(mate_high, mate_low, range(links, links + 1), length)
-    halo_product(is_right(True), lambda at: mate[:, at], tables, out, halves, links)
-    own_product(right, first, k_high, k_low, given, halves, links + 1)
-    tables = table_rows(k_high, k_low, range(1, links + 1), length)
+    halo_product(is_right(True), lambda at: mate[:, at], {links: (mate_high, mate_low)}, out, halves, links)
+    own_product(right, first, (k_high, k_low), given, halves, links + 1)
+    tables = next_tables((k_high, k_low), links, length)
     halo_product(right, received_share(ahead, given), tables, out, halves, links)
     store_send(is_right(True), out, to_mate)
-    own_product(right, second, k_high, k_low, given, halves, links + 1)
 
 
 def received_share(received, given):
@@ -454,16 +513,17 @@
 def mate_third_kernel(partial, mate, early_high, early_low, late_high, late_low, out, halves, *, links):
     length = halves.shape[1] // links
     out[...] = partial[...]
-    tables = table_rows(early_high, early_low, range(1, links), length)
-    tables.update(table_rows(late_high, late_low, range(links, links + 1), length))
+    tables = early_tables((early_high, early_low), links, length)
+    tables[links] = (late_high, late_low)
     halo_product(is_right(True), lambda at: mate[:, at], tables, out, halves, links)
 
 
 def next_third_kernel(partial, after, given, k_high, k_low, third, table, out, sums, halves, *, links):
     length = halves.shape[1] // links
     out[...] = partial[...]
-    tables = table_rows(k_high, k_low, range(1, links + 1), length)
-    halo_product(is_right(False), received_share(after, given), tables, out, halves, links)
+    tables = next_tables((k_high, k_low), links, length)
+    share = lambda at: load_tiles(after, out.shape[0], at) + given[:, at]
+    halo_product(is_right(False), share, tables, out, halves, links)
     full = add_sums(table[...], ((5, third, out), (6, out, out)))
     turned = jnp.transpose(full)[0:8, :]
     compact = jnp.concatenate([turned[0:4], turned[4:8]], axis=1)
@@ -564,6 +624,7 @@
     packed = jax.ShapeDtypeStruct((rows + 8, span), F32)
     wide_packed = jax.ShapeDtypeStruct((rows + 16, span), F32)
     wide_part = jax.ShapeDtypeStruct((rows + 8, span), F32)
+    tiled_part = jax.ShapeDtypeStruct((rows // 8 * (span // 128) + 1, 8, 128), F32)
     sums_table = jax.ShapeDtypeStruct((rows, 128), F32)
     local_table = jax.ShapeDtypeStruct((here, here), BF16)
     halo_table = jax.ShapeDtypeStruct((span, span), BF16)
@@ -578,56 +639,62 @@
         [pltpu.VMEM((3, here), F32), pltpu.SMEM((links, blocks), jnp.int32), pltpu.SemaphoreType.DMA((4,))],
     )(coords, pair_list, probes)
     mate, beyond = swap_mate(to_mate), swap_next(to_next)
-    k_high, k_low, partial, first, columns = call(
+    k_high, k_low, partial, first = call(
         functools.partial(local_first_kernel, links=links),
         "local_first",
-        (local_table, local_table, whole, whole, jax.ShapeDtypeStruct((3, here, 128), F32)),
+        (local_table, local_table, whole, whole),
         [VMEM, VMEM, ANY],
         [
             local_halves,
+            pltpu.VMEM((3, here, 128), F32),
             pltpu.VMEM((3 + blocks, 8, here), F32),
             pltpu.SemaphoreType.DMA((1,)),
         ],
     )(own, noise, probes)
     halo_scratch = [halo_halves, pltpu.VMEM((3 + links, 8, span), F32)]
     early_table = jax.ShapeDtypeStruct((span - length, span - length), BF16)
-    late_table = jax.ShapeDtypeStruct((length, span), BF16)
-    early_high, early_low, partial, to_next = call(
+    late_table = jax.ShapeDtypeStruct((span, length), BF16)
+    halo_columns_of = jax.ShapeDtypeStruct((3, span, 128), F32)
+    early_high, early_low, partial, to_next, mate_columns = call(
         functools.partial(mate_first_kernel, links=links),
         "mate_first",
-        (early_table, early_table, whole, wide_part),
-        [VMEM] * 4,
+        (early_table, early_table, whole, wide_part, halo_columns_of),
+        [VMEM] * 3,
         halo_scratch,
-    )(own, partial, mate, columns)
+    )(own, partial, mate)
     ahead = swap_next(to_next)
     late_high, late_low, next_high, next_low, second, to_mate = call(
         functools.partial(next_first_kernel, links=links),
         "next_first",
         (late_table, late_table, halo_table, halo_table, whole, part),
         [VMEM] * 5,
-        halo_scratch + halo_scratch,
-    )(own, partial, mate, beyond, columns)
+        halo_scratch + halo_scratch + [pltpu.VMEM((3, span, 128), F32)],
+    )(own, partial, mate, mate_columns, beyond)
 
     mate = swap_mate(to_mate)
     partial = call(
         functools.partial(local_second_kernel, length=length), "local_second", whole, [VMEM] * 4, [local_halves]
     )(noise, second, k_high, k_low)
     partial, to_next = call(
-        functools.partial(mate_second_kernel, links=links), "mate_second", (whole, wide_part), [VMEM] * 4, [halo_halves]
+        functools.partial(mate_second_kernel, links=links), "mate_second", (whole, tiled_part), [VMEM] * 4, [halo_halves]
     )(partial, mate, early_high, early_low)
     after = swap_next(to_next)
-    third, given, to_mate = call(
+    third, to_mate = call(
         functools.partial(next_second_kernel, links=links),
         "next_second",
-        (whole, part, part),
-        [VMEM] * 9,
-        [halo_halves],
-    )(partial, first, second, mate, ahead, late_high, late_low, next_high, next_low)
+        (whole, part),
+        [VMEM] * 8,
+        [halo_halves, pltpu.VMEM((rows, span), F32)],
+    )(partial, first, mate, ahead, late_high, late_low, next_high, next_low)
 
     mate = swap_mate(to_mate)
-    partial, table = call(
-        functools.partial(local_third_kernel, length=length), "local_third", (whole, sums_table), [VMEM] * 6, [local_halves]
-    )(noise, first, second, third, k_high, k_low)
+    partial, given, table = call(
+        functools.partial(local_third_kernel, length=length),
+        "local_third",
+        (whole, part, sums_table),
+        [VMEM] * 8,
+        [local_halves, halo_halves],
+    )(noise, first, second, third, k_high, k_low, next_high, next_low)
     regions, subs = lax.axis_size("region"), lax.axis_size("sub")
     partial = call(
         functools.partial(mate_third_kernel, links=links), "mate_third", whole, [VMEM] * 6, [halo_halves]

time: 73.4 us -> 73.2 us (level)
  transfers between devices with their start and end apart: 6 -> 6, of which waited for: 2 -> 1; matrix products, arithmetic and copies ran while one was open for 0% -> 0% of each run, Pallas kernels for 16% -> 16%
where the time goes in v8:
time: 73.2 us; the launch traced here: 72.8 us
  blocking collectives  37.3 us (51%)
  starting transfers between devices  18.9 us (26%)
  Pallas kernels  14.4 us (20%)
  between operations  1.01 us (1%)
  loops' own time  0.81 us (1%)
    all_to_all x1, blocking collectives, per_device(): sums = jnp.sum(lax.all_to_all(sums, 'region', 0, 0), axis=0)  24.6 us
    all_to_all x1, blocking collectives, per_device(): lax.all_to_all(jnp.broadcast_to(sums[None], (subs, 4, 128)), 'sub', 0, 0)  12.6 us
    ppermute x3, starting transfers between devices, swap_next(): lax.ppermute(array, AXES, [(i, i + 1 if i % 2 else i - 1) for i in range(...  10.2 us
    ppermute x3, starting transfers between devices, swap_mate(): lax.ppermute(array, AXES, [(i, i ^ 1) for i in range(lax.axis_size(AXES))])  8.71 us
    pallas_call x1, Pallas kernels, per_device(): call(functools.partial(local_first_kernel, links=links), 'local_first', (...  3.75 us
    pallas_call x1, Pallas kernels, per_device(): call(functools.partial(next_first_kernel, links=links), 'next_first', (la...  2.27 us
    pallas_call x1, Pallas kernels, per_device(): call(functools.partial(local_third_kernel, length=length), 'local_third',...  1.52 us
  transfers between devices with their start and end apart: 6, of which 1 were waited for; matrix products, arithmetic and copies ran while one was open for 0% of the time, Pallas kernels for 16%

profile of v8, /device:TPU:1, one launch (start us, length us, event | category | flops | bytes accessed | tf_op | source)
XLA Modules:
  0.0 72.8 jit_solution(2249039810398491452)
XLA Ops:
  0.6 1.1 %pack.1 = (f32[72,768]{1,0:T(8,128)S(1)}, f32[80,768]{1,0:T(8,128)S(1)}, f32[8,1024]{1,0:T(8,128)S(1)}) custom-call(f32[3,1024]{1,0:T(4,128)} %coords.1, s32[3,4]{1,0:T(4,128)} %pair.1, f32[64,1024]{1,0:T(8,128)} %probes.3), custom_call_target="tpu_custom_call" | custom-call | tf_op jit(solution)/shard_map/pack/pallas_call | solution.py:634
  1.7 4.6 %collective-permute-start.4 = (f32[80,768]{1,0:T(8,128)S(1)}, f32[80,768]{1,0:T(8,128)S(1)}, u32[]{:S(2)}, u32[]{:S(2)}) collective-permute-start(f32[80,768]{1,0:T(8,128)S(1)} %get-tuple-element.315), channel_id=1, source_target_pairs={{1,2},{2,1},{3,4},{4,3},{5,6},{6,5},{7,8},{8,7},{9,10},{10,9},{11,... | collective-permute-start | bytes 737288 | tf_op jit(solution)/shard_map/ppermute | solution.py:612
  6.3 4.9 %collective-permute-start.3 = (f32[72,768]{1,0:T(8,128)S(1)}, f32[72,768]{1,0:T(8,128)S(1)}, u32[]{:S(2)}, u32[]{:S(2)}) collective-permute-start(f32[72,768]{1,0:T(8,128)S(1)} %get-tuple-element.312), channel_id=1, source_target_pairs={{0,1},{1,0},{2,3},{3,2},{4,5},{5,4},{6,7},{7,6},{8,9},{9,8},{10,11... | collective-permute-start | bytes 663560 | tf_op jit(solution)/shard_map/ppermute | solution.py:608
  11.2 3.8 %local_first.1 = (bf16[1024,1024]{1,0:T(8,128)(2,1)S(1)}, bf16[1024,1024]{1,0:T(8,128)(2,1)S(1)}, f32[64,1024]{1,0:T(8,128)S(1)}, f32[64,1024]{1,0:T(8,128)S(1)}) custom-call(f32[8,1024]{1,0:T(8,128)S(1)} %get-tuple-element.309.own, f32[1,1024]{1,0:T(1,128)} %bitcast.97, f32[64,1024]{1,0:T(8,128)} %probes.3), custom_call_target="tpu_custom_call" | custom-call | tf_op jit(solution)/shard_map/local_first/pallas_call | solution.py:642
  15.0 0.0 collective-permute-done.3.received.mate
  15.0 0.0 copy-start.3
  15.0 1.2 %mate_first.1 = (bf16[512,512]{1,0:T(8,128)(2,1)S(1)}, bf16[512,512]{1,0:T(8,128)(2,1)S(1)}, f32[64,1024]{1,0:T(8,128)S(1)}, f32[72,768]{1,0:T(8,128)S(1)}, f32[3,768,128]{2,1,0:T(8,128)S(1)}) custom-call(f32[8,1024]{1,0:T(8,128)S(1)} %get-tuple-element.309.own, f32[64,1024]{1,0:T(8,128)S(1)} %get-tuple-element.311.partial, ...), custom_call_target="tpu_custom_call" | custom-call | tf_op jit(solution)/shard_map/mate_first/pallas_call | solution.py:658
  16.1 1.9 %collective-permute-start.6 = (f32[72,768]{1,0:T(8,128)S(1)}, f32[72,768]{1,0:T(8,128)S(1)}, u32[]{:S(2)}, u32[]{:S(2)}) collective-permute-start(f32[72,768]{1,0:T(8,128)S(1)} %get-tuple-element.323), channel_id=1, source_target_pairs={{1,2},{2,1},{3,4},{4,3},{5,6},{6,5},{7,8},{8,7},{9,10},{10,9},{11,... | collective-permute-start | bytes 663560 | tf_op jit(solution)/shard_map/ppermute | solution.py:612
  18.1 0.0 collective-permute-done.4.received
  18.1 2.3 %next_first.1 = (bf16[768,256]{1,0:T(8,128)(2,1)S(1)}, bf16[768,256]{1,0:T(8,128)(2,1)S(1)}, bf16[768,768]{1,0:T(8,128)(2,1)S(1)}, bf16[768,768]{1,0:T(8,128)(2,...) custom-call(f32[8,1024]{1,0:T(8,128)S(1)} %get-tuple-element.309.own, f32[64,1024]{1,0:T(8,128)S(1)} %get-tuple-element.313.partial, ...), custom_call_target="tpu_custom_call" | custom-call | tf_op jit(solution)/shard_map/next_first/pallas_call | solution.py:666
  20.4 1.9 %collective-permute-start.5 = (f32[64,768]{1,0:T(8,128)S(1)}, f32[64,768]{1,0:T(8,128)S(1)}, u32[]{:S(2)}, u32[]{:S(2)}) collective-permute-start(f32[64,768]{1,0:T(8,128)S(1)} %get-tuple-element.319), channel_id=1, source_target_pairs={{0,1},{1,0},{2,3},{3,2},{4,5},{5,4},{6,7},{7,6},{8,9},{9,8},{10,11... | collective-permute-start | bytes 589832 | tf_op jit(solution)/shard_map/ppermute | solution.py:608
  22.3 0.0 copy-done.3
  22.3 1.0 %local_second.1.partial = f32[64,1024]{1,0:T(8,128)S(1)} custom-call(f32[1,1024]{1,0:T(1,128)S(1)} %bitcast.98, f32[64,1024]{1,0:T(8,128)S(1)} %get-tuple-element.316.second, bf16[1024,1024]{1,0:T(8,128)(2,1)S(1)} %get-tuple-element.317.k_high, bf16[1024,1024]{1,0:T(8,128)(2,1)S(1)} %get-tuple-element.318.k_low), custom_call_target="tpu_custom_call" | custom-call | tf_op jit(solution)/shard_map/local_second/pallas_call | solution.py:675
  23.3 0.4 collective-permute-done.5.mate
  23.7 0.3 mate_second.1
  24.0 3.6 %collective-permute-start.8 = (f32[49,8,128]{2,1,0:T(8,128)S(1)}, f32[49,8,128]{2,1,0:T(8,128)S(1)}, u32[]{:S(2)}, u32[]{:S(2)}) collective-permute-start(f32[49,8,128]{2,1,0:T(8,128)S(1)} %get-tuple-element.331), channel_id=1, source_target_pairs={{1,2},{2,1},{3,4},{4,3},{5,6},{6,5},{7,8},{8,7},{9,10},{10,9},{11,... | collective-permute-start | bytes 602120 | tf_op jit(solution)/shard_map/ppermute | solution.py:612
  27.6 0.0 collective-permute-done.6.ahead
  27.6 1.2 %next_second.1 = (f32[64,1024]{1,0:T(8,128)S(1)}, f32[64,768]{1,0:T(8,128)S(1)}) custom-call(f32[64,1024]{1,0:T(8,128)S(1)} %get-tuple-element.322.partial, f32[64,1024]{1,0:T(8,128)S(1)} %get-tuple-element.310.first, f32[64,768]{1,0:T(8,128)S(1)} %collective-permute-done.5.mate, f32[72,768]{1,0:T(8,128)S(1)} %collective-permute-done.6.ahead, ...), custom_call_target="tpu_custom_call" | custom-call | tf_op jit(solution)/shard_map/next_second/pallas_call | solution.py:682
  28.8 1.9 %collective-permute-start.7 = (f32[64,768]{1,0:T(8,128)S(1)}, f32[64,768]{1,0:T(8,128)S(1)}, u32[]{:S(2)}, u32[]{:S(2)}) collective-permute-start(f32[64,768]{1,0:T(8,128)S(1)} %get-tuple-element.330), channel_id=1, source_target_pairs={{0,1},{1,0},{2,3},{3,2},{4,5},{5,4},{6,7},{7,6},{8,9},{9,8},{10,11... | collective-permute-start | bytes 589832 | tf_op jit(solution)/shard_map/ppermute | solution.py:608
  30.7 1.5 %local_third.1 = (f32[64,1024]{1,0:T(8,128)S(1)}, f32[64,768]{1,0:T(8,128)S(1)}, f32[64,128]{1,0:T(8,128)S(1)}) custom-call(f32[1,1024]{1,0:T(1,128)S(1)} %bitcast.99, f32[64,1024]{1,0:T(8,128)S(1)} %get-tuple-element.310.first, f32[64,1024]{1,0:T(8,128)S(1)} %get-tuple-element.316.second, f32[64,1024]{1,0:T(8,128)S(1)} %get-tuple-element.328.third, ...), custom_call_target="tpu_custom_call" | custom-call | tf_op jit(solution)/shard_map/local_third/pallas_call | solution.py:691
  32.3 0.0 collective-permute-done.7.mate
  32.3 0.4 mate_third.1.partial
  32.7 0.0 collective-permute-done.8.after
  32.7 0.6 next_third.1
  33.3 0.0 copy-start.2
  33.3 0.0 copy-start.4
  33.3 0.0 copy-start.5
  33.3 24.6 %all_to_all.10 = f32[32,4,128]{2,1,0:T(4,128)S(1)} all-to-all(f32[32,4,128]{2,1,0:T(4,128)S(1)} %get-tuple-element.334), channel_id=1, replica_groups=mesh['region'=32,'sub'=16] {'region'}, dimensions={0} | all-to-all | bytes 131072 | tf_op jit(solution)/shard_map/all_to_all | solution.py:710
  58.0 12.6 %all_to_all.11.sums = f32[16,4,128]{2,1,0:T(4,128)S(1)} all-to-all(f32[16,4,128]{2,1,0:T(4,128)S(1)} %broadcast_in_dim.5), channel_id=1, replica_groups=mesh['region'=32,'sub'=16] {'sub'}, dimensions={0} | all-to-all | bytes 65536 | tf_op jit(solution)/shard_map/all_to_all | solution.py:711
  70.7 1.2 %finish.1 = (f32[64,1024]{1,0:T(8,128)}, f32[64,1024]{1,0:T(8,128)}, f32[1,1]{1,0:T(1,128)}) custom-call(f32[16,4,128]{2,1,0:T(4,128)S(1)} %all_to_all.11.sums, f32[64,1024]{1,0:T(8,128)S(1)} %get-tuple-element.310.first, f32[64,1024]{1,0:T(8,128)S(1)} %get-tuple-element.316.second, f32[64,1024]{1,0:T(8,128)S(1)} %get-tuple-element.328.third, ...), custom_call_target="tpu_custom_call" | custom-call | tf_op jit(solution)/shard_map/finish/pallas_call | solution.py:712
  71.8 0.0 copy-done.2
  71.9 0.0 copy-done.4
  71.9 0.0 copy-done.5
  71.9 0.8 %while.35 = (f32[1,1]{1,0:T(1,128)}, f32[64,1024]{1,0:T(8,128)}, f32[64,1024]{1,0:T(8,128)}, f32[64,1024]{1,0:T(8,128)S(1)}, f32[3,1024]{1,0:T(4,128)S(1)}, /*in...) while((f32[1,1]{1,0:T(1,128)}, f32[64,1024]{1,0:T(8,128)}, f32[64,1024]{1,0:T(8,128)}, ...), condition=%region_10.11_spmd, body=%region_1.10_spmd | while | flops 1439929600 | bytes 21131516 | solution.py:724
  (2 shorter events, 0.1 us)
Async XLA Ops:
  1.7 16.4 %collective-permute-start.4 = (f32[80,768]{1,0:T(8,128)S(1)}, f32[80,768]{1,0:T(8,128)S(1)}, u32[]{:S(2)}, u32[]{:S(2)}) collective-permute-start(f32[80,768]{1,0:T(8,128)S(1)} %get-tuple-element.315), channel_id=1, source_target_pairs={{1,2},{2,1},{3,4},{4,3},{5,6},{6,5},{7,8},{8,7},{9,10},{10,9},{11,... | collective-permute-start | bytes 737288 | tf_op jit(solution)/shard_map/ppermute | solution.py:612
  6.3 8.6 %collective-permute-start.3 = (f32[72,768]{1,0:T(8,128)S(1)}, f32[72,768]{1,0:T(8,128)S(1)}, u32[]{:S(2)}, u32[]{:S(2)}) collective-permute-start(f32[72,768]{1,0:T(8,128)S(1)} %get-tuple-element.312), channel_id=1, source_target_pairs={{0,1},{1,0},{2,3},{3,2},{4,5},{5,4},{6,7},{7,6},{8,9},{9,8},{10,11... | collective-permute-start | bytes 663560 | tf_op jit(solution)/shard_map/ppermute | solution.py:608
  15.0 7.3 %copy-start.3 = (f32[1024]{0:T(1024)S(1)}, f32[1024]{0:T(1024)}, u32[]{:S(2)}) copy-start(f32[1024]{0:T(1024)} %param.17) | copy-start | bytes 12292
  16.1 11.5 %collective-permute-start.6 = (f32[72,768]{1,0:T(8,128)S(1)}, f32[72,768]{1,0:T(8,128)S(1)}, u32[]{:S(2)}, u32[]{:S(2)}) collective-permute-start(f32[72,768]{1,0:T(8,128)S(1)} %get-tuple-element.323), channel_id=1, source_target_pairs={{1,2},{2,1},{3,4},{4,3},{5,6},{6,5},{7,8},{8,7},{9,10},{10,9},{11,... | collective-permute-start | bytes 663560 | tf_op jit(solution)/shard_map/ppermute | solution.py:612
  20.4 3.3 %collective-permute-start.5 = (f32[64,768]{1,0:T(8,128)S(1)}, f32[64,768]{1,0:T(8,128)S(1)}, u32[]{:S(2)}, u32[]{:S(2)}) collective-permute-start(f32[64,768]{1,0:T(8,128)S(1)} %get-tuple-element.319), channel_id=1, source_target_pairs={{0,1},{1,0},{2,3},{3,2},{4,5},{5,4},{6,7},{7,6},{8,9},{9,8},{10,11... | collective-permute-start | bytes 589832 | tf_op jit(solution)/shard_map/ppermute | solution.py:608
  24.0 8.7 %collective-permute-start.8 = (f32[49,8,128]{2,1,0:T(8,128)S(1)}, f32[49,8,128]{2,1,0:T(8,128)S(1)}, u32[]{:S(2)}, u32[]{:S(2)}) collective-permute-start(f32[49,8,128]{2,1,0:T(8,128)S(1)} %get-tuple-element.331), channel_id=1, source_target_pairs={{1,2},{2,1},{3,4},{4,3},{5,6},{6,5},{7,8},{8,7},{9,10},{10,9},{11,... | collective-permute-start | bytes 602120 | tf_op jit(solution)/shard_map/ppermute | solution.py:612
  28.8 3.5 %collective-permute-start.7 = (f32[64,768]{1,0:T(8,128)S(1)}, f32[64,768]{1,0:T(8,128)S(1)}, u32[]{:S(2)}, u32[]{:S(2)}) collective-permute-start(f32[64,768]{1,0:T(8,128)S(1)} %get-tuple-element.330), channel_id=1, source_target_pairs={{0,1},{1,0},{2,3},{3,2},{4,5},{5,4},{6,7},{7,6},{8,9},{9,8},{10,11... | collective-permute-start | bytes 589832 | tf_op jit(solution)/shard_map/ppermute | solution.py:608
  33.3 38.5 %copy-start.2 = (f32[64,1024]{1,0:T(8,128)S(1)}, f32[64,1024]{1,0:T(8,128)}, u32[]{:S(2)}) copy-start(f32[64,1024]{1,0:T(8,128)} %probes.3) | copy-start | bytes 786436
  33.3 38.5 %copy-start.4 = (f32[3,1024]{1,0:T(4,128)S(1)}, f32[3,1024]{1,0:T(4,128)}, u32[]{:S(2)}) copy-start(f32[3,1024]{1,0:T(4,128)} %coords.1) | copy-start | bytes 36868
  33.3 38.5 %copy-start.5 = (s32[3,4]{1,0:T(4,128)S(1)}, s32[3,4]{1,0:T(4,128)}, u32[]{:S(2)}) copy-start(s32[3,4]{1,0:T(4,128)} %pair.1) | copy-start | bytes 148

commit v9 on v8

--- a/solution.py
+++ b/solution.py
@@ -109,7 +109,7 @@
     return copies
 
 
-def pack_kernel(coords, pair, probes, to_mate, to_next, own, points, flags, sem):
+def pack_kernel(coords, pair, noise, probes, to_mate, to_next, own, points, flags, variance, sem):
     links, blocks = pair.shape
     here = coords.shape[1]
     length = here // blocks
@@ -119,25 +119,26 @@
         [
             pltpu.make_async_copy(pair, flags, sem.at[0]),
             pltpu.make_async_copy(coords, points, sem.at[1]),
+            pltpu.make_async_copy(noise, variance, sem.at[4]),
             pltpu.make_async_copy(probes.at[:, pl.ds(place[0], span)], to_mate.at[0:rows], sem.at[2]),
             pltpu.make_async_copy(probes.at[:, pl.ds(place[1], span)], to_next.at[0:rows], sem.at[3]),
         ]
     )
-    copies[0].wait()
-    copies[1].wait()
+    for copy in copies[0:3]:
+        copy.wait()
     right = is_right(True)
     extra = [points[...]]
     for k in range(links):
         flag = [flags[k, b].astype(F32) for b in range(blocks)]
         extra.append(jnp.concatenate([jnp.full((1, length), f, F32) for f in flag], axis=1))
-    extra = jnp.concatenate(extra + [jnp.zeros((8 - 3 - links, here), F32)], axis=0)
+    extra = jnp.concatenate(extra + [variance[...], jnp.zeros((8 - 4 - links, here), F32)], axis=0)
     own[...] = extra
     low, high = extra[:, 0:span], extra[:, here - span :]
     to_mate[rows : rows + 8, :] = jnp.where(right, high, low)
     to_next[rows : rows + 8, :] = jnp.where(right, low, high)
     to_next[rows + 8 :, :] = jnp.zeros((to_next.shape[0] - rows - 8, span), F32)
-    copies[2].wait()
     copies[3].wait()
+    copies[4].wait()
 
 
 def column_steps(columns, at, load):
@@ -206,8 +207,9 @@
     return most[0:rows] + (most[rows : 2 * rows] + rest)
 
 
-def local_product(noise, vector, k_high, k_low, out, halves, length):
+def local_product(own, vector, k_high, k_low, out, halves, length):
     here = vector.shape[1]
+    noise = own[3 + here // length - 1 : 3 + here // length, :]
     store_halves(halves, 0, vector[...])
     for start in range(0, here, length):
         stop = start + length
@@ -242,7 +244,8 @@
     return steps
 
 
-def local_first_kernel(own, noise, probes, k_high, k_low, out, first, halves, columns, rows, sem, *, links):
+def local_first_kernel(own, probes, k_high, k_low, out, first, halves, columns, rows, sem, *, links):
+    noise = own[3 + links : 4 + links, :]
     here = own.shape[1]
     blocks = links + 1
     length = here // blocks
@@ -271,7 +274,7 @@
         if i == 0:
             copy.wait()
             store_halves(halves, 0, first[...])
-            out[...] = (noise[...] - SHIFT) * first[...]
+            out[...] = (noise - SHIFT) * first[...]
         steps = row_steps(halves, k_high, k_low, out, start, length)
     for step in steps:
         step()
@@ -468,14 +471,14 @@
     return table
 
 
-def local_second_kernel(noise, second, k_high, k_low, out, halves, *, length):
-    local_product(noise, second, k_high, k_low, out, halves, length)
+def local_second_kernel(own, second, k_high, k_low, out, halves, *, length):
+    local_product(own, second, k_high, k_low, out, halves, length)
 
 
 def local_third_kernel(
-    noise, first, second, third, k_high, k_low, next_high, next_low, out, given, table, halves, own_halves, *, length
+    own, first, second, third, k_high, k_low, next_high, next_low, out, given, table, halves, own_halves, *, length
 ):
-    local_product(noise, third, k_high, k_low, out, halves, length)
+    local_product(own, third, k_high, k_low, out, halves, length)
     own_product(is_right(False), second, (next_high, next_low), given, own_halves, out.shape[1] // length)
     terms = ((0, first, first), (1, first, second), (2, second, second), (3, second, third), (4, third, third))
     table[...] = add_sums(jnp.zeros(table.shape, F32), terms)
@@ -635,22 +638,27 @@
         pack_kernel,
         "pack",
         (packed, wide_packed, jax.ShapeDtypeStruct((8, here), F32)),
-        [ANY, ANY, ANY],
-        [pltpu.VMEM((3, here), F32), pltpu.SMEM((links, blocks), jnp.int32), pltpu.SemaphoreType.DMA((4,))],
-    )(coords, pair_list, probes)
+        [ANY] * 4,
+        [
+            pltpu.VMEM((3, here), F32),
+            pltpu.SMEM((links, blocks), jnp.int32),
+            pltpu.VMEM((1, here), F32),
+            pltpu.SemaphoreType.DMA((5,)),
+        ],
+    )(coords, pair_list, noise, probes)
     mate, beyond = swap_mate(to_mate), swap_next(to_next)
     k_high, k_low, partial, first = call(
         functools.partial(local_first_kernel, links=links),
         "local_first",
         (local_table, local_table, whole, whole),
-        [VMEM, VMEM, ANY],
+        [VMEM, ANY],
         [
             local_halves,
             pltpu.VMEM((3, here, 128), F32),
             pltpu.VMEM((3 + blocks, 8, here), F32),
             pltpu.SemaphoreType.DMA((1,)),
         ],
-    )(own, noise, probes)
+    )(own, probes)
     halo_scratch = [halo_halves, pltpu.VMEM((3 + links, 8, span), F32)]
     early_table = jax.ShapeDtypeStruct((span - length, span - length), BF16)
     late_table = jax.ShapeDtypeStruct((span, length), BF16)
@@ -674,7 +682,7 @@
     mate = swap_mate(to_mate)
     partial = call(
         functools.partial(local_second_kernel, length=length), "local_second", whole, [VMEM] * 4, [local_halves]
-    )(noise, second, k_high, k_low)
+    )(own, second, k_high, k_low)
     partial, to_next = call(
         functools.partial(mate_second_kernel, links=links), "mate_second", (whole, tiled_part), [VMEM] * 4, [halo_halves]
     )(partial, mate, early_high, early_low)
@@ -694,7 +702,7 @@
         (whole, part, sums_table),
         [VMEM] * 8,
         [local_halves, halo_halves],
-    )(noise, first, second, third, k_high, k_low, next_high, next_low)
+    )(own, first, second, third, k_high, k_low, next_high, next_low)
     regions, subs = lax.axis_size("region"), lax.axis_size("sub")
     partial = call(
         functools.partial(mate_third_kernel, links=links), "mate_third", whole, [VMEM] * 6, [halo_halves]

time: 73.2 us -> 72.6 us (level)
  transfers between devices with their start and end apart: 6 -> 6, of which waited for: 1 -> 1; matrix products, arithmetic and copies ran while one was open for 0% -> 0% of each run, Pallas kernels for 16% -> 15%
where the time goes in v9:
time: 72.6 us; the launch traced here: 72.2 us
  blocking collectives  37.2 us (51%)
  starting transfers between devices  18.9 us (26%)
  Pallas kernels  13.8 us (19%)
  between operations  1 us (1%)
  loops' own time  0.81 us (1%)
    all_to_all x1, blocking collectives, per_device(): sums = jnp.sum(lax.all_to_all(sums, 'region', 0, 0), axis=0)  24.6 us
    all_to_all x1, blocking collectives, per_device(): lax.all_to_all(jnp.broadcast_to(sums[None], (subs, 4, 128)), 'sub', 0, 0)  12.6 us
    ppermute x3, starting transfers between devices, swap_next(): lax.ppermute(array, AXES, [(i, i + 1 if i % 2 else i - 1) for i in range(...  10.2 us
    ppermute x3, starting transfers between devices, swap_mate(): lax.ppermute(array, AXES, [(i, i ^ 1) for i in range(lax.axis_size(AXES))])  8.71 us
    pallas_call x1, Pallas kernels, per_device(): call(functools.partial(local_first_kernel, links=links), 'local_first', (...  3.08 us
    pallas_call x1, Pallas kernels, per_device(): call(functools.partial(next_first_kernel, links=links), 'next_first', (la...  2.28 us
    pallas_call x1, Pallas kernels, per_device(): call(functools.partial(local_third_kernel, length=length), 'local_third',...  1.52 us
  transfers between devices with their start and end apart: 6, of which 1 were waited for; matrix products, arithmetic and copies ran while one was open for 0% of the time, Pallas kernels for 15%

profile of v9, /device:TPU:1, one launch (start us, length us, event | category | flops | bytes accessed | tf_op | source)
XLA Modules:
  0.0 72.2 jit_solution(1958605943842903619)
XLA Ops:
  0.6 1.1 %pack.1 = (f32[72,768]{1,0:T(8,128)S(1)}, f32[80,768]{1,0:T(8,128)S(1)}, f32[8,1024]{1,0:T(8,128)S(1)}) custom-call(f32[3,1024]{1,0:T(4,128)} %coords.1, s32[3,4]{1,0:T(4,128)} %pair.1, f32[1,1024]{1,0:T(1,128)} %bitcast.97, f32[64,1024]{1,0:T(8,128)} %probes.3), custom_call_target="tpu_custom_call" | custom-call | tf_op jit(solution)/shard_map/pack/pallas_call | solution.py:637
  1.7 4.6 %collective-permute-start.4 = (f32[80,768]{1,0:T(8,128)S(1)}, f32[80,768]{1,0:T(8,128)S(1)}, u32[]{:S(2)}, u32[]{:S(2)}) collective-permute-start(f32[80,768]{1,0:T(8,128)S(1)} %get-tuple-element.315), channel_id=1, source_target_pairs={{1,2},{2,1},{3,4},{4,3},{5,6},{6,5},{7,8},{8,7},{9,10},{10,9},{11,... | collective-permute-start | bytes 737288 | tf_op jit(solution)/shard_map/ppermute | solution.py:615
  6.3 4.9 %collective-permute-start.3 = (f32[72,768]{1,0:T(8,128)S(1)}, f32[72,768]{1,0:T(8,128)S(1)}, u32[]{:S(2)}, u32[]{:S(2)}) collective-permute-start(f32[72,768]{1,0:T(8,128)S(1)} %get-tuple-element.312), channel_id=1, source_target_pairs={{0,1},{1,0},{2,3},{3,2},{4,5},{5,4},{6,7},{7,6},{8,9},{9,8},{10,11... | collective-permute-start | bytes 663560 | tf_op jit(solution)/shard_map/ppermute | solution.py:611
  11.2 3.1 %local_first.1 = (bf16[1024,1024]{1,0:T(8,128)(2,1)S(1)}, bf16[1024,1024]{1,0:T(8,128)(2,1)S(1)}, f32[64,1024]{1,0:T(8,128)S(1)}, f32[64,1024]{1,0:T(8,128)S(1)}) custom-call(f32[8,1024]{1,0:T(8,128)S(1)} %get-tuple-element.309.own, f32[64,1024]{1,0:T(8,128)} %probes.3), custom_call_target="tpu_custom_call" | custom-call | tf_op jit(solution)/shard_map/local_first/pallas_call | solution.py:650
  14.3 0.0 collective-permute-done.3.received.mate
  14.3 1.2 %mate_first.1 = (bf16[512,512]{1,0:T(8,128)(2,1)S(1)}, bf16[512,512]{1,0:T(8,128)(2,1)S(1)}, f32[64,1024]{1,0:T(8,128)S(1)}, f32[72,768]{1,0:T(8,128)S(1)}, f32[3,768,128]{2,1,0:T(8,128)S(1)}) custom-call(f32[8,1024]{1,0:T(8,128)S(1)} %get-tuple-element.309.own, f32[64,1024]{1,0:T(8,128)S(1)} %get-tuple-element.311.partial, ...), custom_call_target="tpu_custom_call" | custom-call | tf_op jit(solution)/shard_map/mate_first/pallas_call | solution.py:666
  15.5 1.9 %collective-permute-start.6 = (f32[72,768]{1,0:T(8,128)S(1)}, f32[72,768]{1,0:T(8,128)S(1)}, u32[]{:S(2)}, u32[]{:S(2)}) collective-permute-start(f32[72,768]{1,0:T(8,128)S(1)} %get-tuple-element.323), channel_id=1, source_target_pairs={{1,2},{2,1},{3,4},{4,3},{5,6},{6,5},{7,8},{8,7},{9,10},{10,9},{11,... | collective-permute-start | bytes 663560 | tf_op jit(solution)/shard_map/ppermute | solution.py:615
  17.4 0.0 collective-permute-done.4.received
  17.4 2.3 %next_first.1 = (bf16[768,256]{1,0:T(8,128)(2,1)S(1)}, bf16[768,256]{1,0:T(8,128)(2,1)S(1)}, bf16[768,768]{1,0:T(8,128)(2,1)S(1)}, bf16[768,768]{1,0:T(8,128)(2,...) custom-call(f32[8,1024]{1,0:T(8,128)S(1)} %get-tuple-element.309.own, f32[64,1024]{1,0:T(8,128)S(1)} %get-tuple-element.313.partial, ...), custom_call_target="tpu_custom_call" | custom-call | tf_op jit(solution)/shard_map/next_first/pallas_call | solution.py:674
  19.7 1.9 %collective-permute-start.5 = (f32[64,768]{1,0:T(8,128)S(1)}, f32[64,768]{1,0:T(8,128)S(1)}, u32[]{:S(2)}, u32[]{:S(2)}) collective-permute-start(f32[64,768]{1,0:T(8,128)S(1)} %get-tuple-element.319), channel_id=1, source_target_pairs={{0,1},{1,0},{2,3},{3,2},{4,5},{5,4},{6,7},{7,6},{8,9},{9,8},{10,11... | collective-permute-start | bytes 589832 | tf_op jit(solution)/shard_map/ppermute | solution.py:611
  21.6 1.0 %local_second.1.partial = f32[64,1024]{1,0:T(8,128)S(1)} custom-call(f32[8,1024]{1,0:T(8,128)S(1)} %get-tuple-element.309.own, f32[64,1024]{1,0:T(8,128)S(1)} %get-tuple-element.316.second, bf16[1024,1024]{1,0:T(8,128)(2,1)S(1)} %get-tuple-element.317.k_high, bf16[1024,1024]{1,0:T(8,128)(2,1)S(1)} %get-tuple-element.318.k_low), custom_call_target="tpu_custom_call" | custom-call | tf_op jit(solution)/shard_map/local_second/pallas_call | solution.py:683
  22.7 0.4 collective-permute-done.5.mate
  23.0 0.3 mate_second.1
  23.3 3.6 %collective-permute-start.8 = (f32[49,8,128]{2,1,0:T(8,128)S(1)}, f32[49,8,128]{2,1,0:T(8,128)S(1)}, u32[]{:S(2)}, u32[]{:S(2)}) collective-permute-start(f32[49,8,128]{2,1,0:T(8,128)S(1)} %get-tuple-element.331), channel_id=1, source_target_pairs={{1,2},{2,1},{3,4},{4,3},{5,6},{6,5},{7,8},{8,7},{9,10},{10,9},{11,... | collective-permute-start | bytes 602120 | tf_op jit(solution)/shard_map/ppermute | solution.py:615
  27.0 0.0 collective-permute-done.6.ahead
  27.0 1.2 %next_second.1 = (f32[64,1024]{1,0:T(8,128)S(1)}, f32[64,768]{1,0:T(8,128)S(1)}) custom-call(f32[64,1024]{1,0:T(8,128)S(1)} %get-tuple-element.322.partial, f32[64,1024]{1,0:T(8,128)S(1)} %get-tuple-element.310.first, f32[64,768]{1,0:T(8,128)S(1)} %collective-permute-done.5.mate, f32[72,768]{1,0:T(8,128)S(1)} %collective-permute-done.6.ahead, ...), custom_call_target="tpu_custom_call" | custom-call | tf_op jit(solution)/shard_map/next_second/pallas_call | solution.py:690
  28.2 1.9 %collective-permute-start.7 = (f32[64,768]{1,0:T(8,128)S(1)}, f32[64,768]{1,0:T(8,128)S(1)}, u32[]{:S(2)}, u32[]{:S(2)}) collective-permute-start(f32[64,768]{1,0:T(8,128)S(1)} %get-tuple-element.330), channel_id=1, source_target_pairs={{0,1},{1,0},{2,3},{3,2},{4,5},{5,4},{6,7},{7,6},{8,9},{9,8},{10,11... | collective-permute-start | bytes 589832 | tf_op jit(solution)/shard_map/ppermute | solution.py:611
  30.1 1.5 %local_third.1 = (f32[64,1024]{1,0:T(8,128)S(1)}, f32[64,768]{1,0:T(8,128)S(1)}, f32[64,128]{1,0:T(8,128)S(1)}) custom-call(f32[8,1024]{1,0:T(8,128)S(1)} %get-tuple-element.309.own, f32[64,1024]{1,0:T(8,128)S(1)} %get-tuple-element.310.first, f32[64,1024]{1,0:T(8,128)S(1)} %get-tuple-element.316.second, f32[64,1024]{1,0:T(8,128)S(1)} %get-tuple-element.328.third, ...), custom_call_target="tpu_custom_call" | custom-call | tf_op jit(solution)/shard_map/local_third/pallas_call | solution.py:699
  31.6 0.0 collective-permute-done.7.mate
  31.6 0.4 mate_third.1.partial
  32.0 0.0 collective-permute-done.8.after
  32.0 0.6 next_third.1
  32.7 0.0 copy-start.2
  32.7 0.0 copy-start.3
  32.7 0.0 copy-start.4
  32.7 0.0 copy-start.5
  32.7 24.6 %all_to_all.10 = f32[32,4,128]{2,1,0:T(4,128)S(1)} all-to-all(f32[32,4,128]{2,1,0:T(4,128)S(1)} %get-tuple-element.334), channel_id=1, replica_groups=mesh['region'=32,'sub'=16] {'region'}, dimensions={0} | all-to-all | bytes 131072 | tf_op jit(solution)/shard_map/all_to_all | solution.py:718
  57.4 12.6 %all_to_all.11.sums = f32[16,4,128]{2,1,0:T(4,128)S(1)} all-to-all(f32[16,4,128]{2,1,0:T(4,128)S(1)} %broadcast_in_dim.5), channel_id=1, replica_groups=mesh['region'=32,'sub'=16] {'sub'}, dimensions={0} | all-to-all | bytes 65536 | tf_op jit(solution)/shard_map/all_to_all | solution.py:719
  70.0 1.2 %finish.1 = (f32[64,1024]{1,0:T(8,128)}, f32[64,1024]{1,0:T(8,128)}, f32[1,1]{1,0:T(1,128)}) custom-call(f32[16,4,128]{2,1,0:T(4,128)S(1)} %all_to_all.11.sums, f32[64,1024]{1,0:T(8,128)S(1)} %get-tuple-element.310.first, f32[64,1024]{1,0:T(8,128)S(1)} %get-tuple-element.316.second, f32[64,1024]{1,0:T(8,128)S(1)} %get-tuple-element.328.third, ...), custom_call_target="tpu_custom_call" | custom-call | tf_op jit(solution)/shard_map/finish/pallas_call | solution.py:720
  71.2 0.0 copy-done.2
  71.2 0.0 copy-done.3
  71.2 0.0 copy-done.4
  71.2 0.0 copy-done.5
  71.3 0.8 %while.35 = (f32[1,1]{1,0:T(1,128)}, f32[64,1024]{1,0:T(8,128)}, f32[64,1024]{1,0:T(8,128)}, f32[64,1024]{1,0:T(8,128)S(1)}, f32[3,1024]{1,0:T(4,128)S(1)}, /*in...) while((f32[1,1]{1,0:T(1,128)}, f32[64,1024]{1,0:T(8,128)}, f32[64,1024]{1,0:T(8,128)}, ...), condition=%region_10.11_spmd, body=%region_1.10_spmd | while | flops 1439929600 | bytes 21131516 | solution.py:732
  (2 shorter events, 0.1 us)
Async XLA Ops:
  1.7 15.7 %collective-permute-start.4 = (f32[80,768]{1,0:T(8,128)S(1)}, f32[80,768]{1,0:T(8,128)S(1)}, u32[]{:S(2)}, u32[]{:S(2)}) collective-permute-start(f32[80,768]{1,0:T(8,128)S(1)} %get-tuple-element.315), channel_id=1, source_target_pairs={{1,2},{2,1},{3,4},{4,3},{5,6},{6,5},{7,8},{8,7},{9,10},{10,9},{11,... | collective-permute-start | bytes 737288 | tf_op jit(solution)/shard_map/ppermute | solution.py:615
  6.3 8.0 %collective-permute-start.3 = (f32[72,768]{1,0:T(8,128)S(1)}, f32[72,768]{1,0:T(8,128)S(1)}, u32[]{:S(2)}, u32[]{:S(2)}) collective-permute-start(f32[72,768]{1,0:T(8,128)S(1)} %get-tuple-element.312), channel_id=1, source_target_pairs={{0,1},{1,0},{2,3},{3,2},{4,5},{5,4},{6,7},{7,6},{8,9},{9,8},{10,11... | collective-permute-start | bytes 663560 | tf_op jit(solution)/shard_map/ppermute | solution.py:611
  15.5 11.5 %collective-permute-start.6 = (f32[72,768]{1,0:T(8,128)S(1)}, f32[72,768]{1,0:T(8,128)S(1)}, u32[]{:S(2)}, u32[]{:S(2)}) collective-permute-start(f32[72,768]{1,0:T(8,128)S(1)} %get-tuple-element.323), channel_id=1, source_target_pairs={{1,2},{2,1},{3,4},{4,3},{5,6},{6,5},{7,8},{8,7},{9,10},{10,9},{11,... | collective-permute-start | bytes 663560 | tf_op jit(solution)/shard_map/ppermute | solution.py:615
  19.7 3.3 %collective-permute-start.5 = (f32[64,768]{1,0:T(8,128)S(1)}, f32[64,768]{1,0:T(8,128)S(1)}, u32[]{:S(2)}, u32[]{:S(2)}) collective-permute-start(f32[64,768]{1,0:T(8,128)S(1)} %get-tuple-element.319), channel_id=1, source_target_pairs={{0,1},{1,0},{2,3},{3,2},{4,5},{5,4},{6,7},{7,6},{8,9},{9,8},{10,11... | collective-permute-start | bytes 589832 | tf_op jit(solution)/shard_map/ppermute | solution.py:611
  23.3 8.7 %collective-permute-start.8 = (f32[49,8,128]{2,1,0:T(8,128)S(1)}, f32[49,8,128]{2,1,0:T(8,128)S(1)}, u32[]{:S(2)}, u32[]{:S(2)}) collective-permute-start(f32[49,8,128]{2,1,0:T(8,128)S(1)} %get-tuple-element.331), channel_id=1, source_target_pairs={{1,2},{2,1},{3,4},{4,3},{5,6},{6,5},{7,8},{8,7},{9,10},{10,9},{11,... | collective-permute-start | bytes 602120 | tf_op jit(solution)/shard_map/ppermute | solution.py:615
  28.2 3.5 %collective-permute-start.7 = (f32[64,768]{1,0:T(8,128)S(1)}, f32[64,768]{1,0:T(8,128)S(1)}, u32[]{:S(2)}, u32[]{:S(2)}) collective-permute-start(f32[64,768]{1,0:T(8,128)S(1)} %get-tuple-element.330), channel_id=1, source_target_pairs={{0,1},{1,0},{2,3},{3,2},{4,5},{5,4},{6,7},{7,6},{8,9},{9,8},{10,11... | collective-permute-start | bytes 589832 | tf_op jit(solution)/shard_map/ppermute | solution.py:611
  32.7 38.5 %copy-start.2 = (f32[64,1024]{1,0:T(8,128)S(1)}, f32[64,1024]{1,0:T(8,128)}, u32[]{:S(2)}) copy-start(f32[64,1024]{1,0:T(8,128)} %probes.3) | copy-start | bytes 786436
  32.7 38.5 %copy-start.3 = (f32[1024]{0:T(1024)S(1)}, f32[1024]{0:T(1024)}, u32[]{:S(2)}) copy-start(f32[1024]{0:T(1024)} %param.17) | copy-start | bytes 12292
  32.7 38.5 %copy-start.4 = (f32[3,1024]{1,0:T(4,128)S(1)}, f32[3,1024]{1,0:T(4,128)}, u32[]{:S(2)}) copy-start(f32[3,1024]{1,0:T(4,128)} %coords.1) | copy-start | bytes 36868
  32.7 38.5 %copy-start.5 = (s32[3,4]{1,0:T(4,128)S(1)}, s32[3,4]{1,0:T(4,128)}, u32[]{:S(2)}) copy-start(s32[3,4]{1,0:T(4,128)} %pair.1) | copy-start | bytes 148

commit v10 on v9

--- a/solution.py
+++ b/solution.py
@@ -460,15 +460,15 @@
     store_send(is_right(True), out, to_mate)
 
 
-def add_sums(table, terms):
-    lane = lax.broadcasted_iota(jnp.int32, table.shape, 1)
-    for power, left, right in terms:
+def sum_rows(terms):
+    rows = []
+    for left, right in terms:
         part = None
         for at in range(0, left.shape[1], 128):
             term = left[:, at : at + 128] * right[:, at : at + 128]
             part = term if part is None else part + term
-        table = jnp.where(lane == power, jnp.sum(part, axis=1, keepdims=True), table)
-    return table
+        rows.append(jnp.sum(jnp.transpose(part), axis=0, keepdims=True))
+    return rows
 
 
 def local_second_kernel(own, second, k_high, k_low, out, halves, *, length):
@@ -480,8 +480,8 @@
 ):
     local_product(own, third, k_high, k_low, out, halves, length)
     own_product(is_right(False), second, (next_high, next_low), given, own_halves, out.shape[1] // length)
-    terms = ((0, first, first), (1, first, second), (2, second, second), (3, second, third), (4, third, third))
-    table[...] = add_sums(jnp.zeros(table.shape, F32), terms)
+    found = sum_rows(((first, first), (first, second), (second, second), (second, third), (third, third)))
+    table[...] = jnp.concatenate(found + [jnp.zeros_like(found[0])] * 3, axis=0)
 
 
 def mate_second_kernel(partial, mate, k_high, k_low, out, to_next, halves, *, links):
@@ -527,9 +527,9 @@
     tables = next_tables((k_high, k_low), links, length)
     share = lambda at: load_tiles(after, out.shape[0], at) + given[:, at]
     halo_product(is_right(False), share, tables, out, halves, links)
-    full = add_sums(table[...], ((5, third, out), (6, out, out)))
-    turned = jnp.transpose(full)[0:8, :]
-    compact = jnp.concatenate([turned[0:4], turned[4:8]], axis=1)
+    late = sum_rows(((third, out), (out, out)))
+    upper = jnp.concatenate([table[4:5, :]] + late + [jnp.zeros_like(late[0])], axis=0)
+    compact = jnp.concatenate([table[0:4, :], upper], axis=1)
     sums[...] = jnp.broadcast_to(compact[None], sums.shape)
 
 
@@ -628,7 +628,7 @@
     wide_packed = jax.ShapeDtypeStruct((rows + 16, span), F32)
     wide_part = jax.ShapeDtypeStruct((rows + 8, span), F32)
     tiled_part = jax.ShapeDtypeStruct((rows // 8 * (span // 128) + 1, 8, 128), F32)
-    sums_table = jax.ShapeDtypeStruct((rows, 128), F32)
+    sums_table = jax.ShapeDtypeStruct((8, rows), F32)
     local_table = jax.ShapeDtypeStruct((here, here), BF16)
     halo_table = jax.ShapeDtypeStruct((span, span), BF16)
     local_halves = pltpu.VMEM((2 * rows, here), BF16)

time: 72.6 us -> 72.6 us (level)
  no operation moved by 1% of the time
where the time goes in v10:
time: 72.6 us; the launch traced here: 72.2 us
  blocking collectives  37.2 us (51%)
  starting transfers between devices  18.9 us (26%)
  Pallas kernels  13.8 us (19%)
  between operations  1 us (1%)
  loops' own time  0.81 us (1%)
    all_to_all x1, blocking collectives, per_device(): sums = jnp.sum(lax.all_to_all(sums, 'region', 0, 0), axis=0)  24.6 us
    all_to_all x1, blocking collectives, per_device(): lax.all_to_all(jnp.broadcast_to(sums[None], (subs, 4, 128)), 'sub', 0, 0)  12.6 us
    ppermute x3, starting transfers between devices, swap_next(): lax.ppermute(array, AXES, [(i, i + 1 if i % 2 else i - 1) for i in range(...  10.2 us
    ppermute x3, starting transfers between devices, swap_mate(): lax.ppermute(array, AXES, [(i, i ^ 1) for i in range(lax.axis_size(AXES))])  8.71 us
    pallas_call x1, Pallas kernels, per_device(): call(functools.partial(local_first_kernel, links=links), 'local_first', (...  3.13 us
    pallas_call x1, Pallas kernels, per_device(): call(functools.partial(next_first_kernel, links=links), 'next_first', (la...  2.28 us
    pallas_call x1, Pallas kernels, per_device(): call(functools.partial(local_third_kernel, length=length), 'local_third',...  1.53 us
  transfers between devices with their start and end apart: 6, of which 1 were waited for; matrix products, arithmetic and copies ran while one was open for 0% of the time, Pallas kernels for 15%

profile of v10, /device:TPU:1, one launch (start us, length us, event | category | flops | bytes accessed | tf_op | source)
XLA Modules:
  0.0 72.2 jit_solution(17248011578691303533)
XLA Ops:
  0.6 1.1 %pack.1 = (f32[72,768]{1,0:T(8,128)S(1)}, f32[80,768]{1,0:T(8,128)S(1)}, f32[8,1024]{1,0:T(8,128)S(1)}) custom-call(f32[3,1024]{1,0:T(4,128)} %coords.1, s32[3,4]{1,0:T(4,128)} %pair.1, f32[1,1024]{1,0:T(1,128)} %bitcast.97, f32[64,1024]{1,0:T(8,128)} %probes.3), custom_call_target="tpu_custom_call" | custom-call | tf_op jit(solution)/shard_map/pack/pallas_call | solution.py:637
  1.7 4.6 %collective-permute-start.4 = (f32[80,768]{1,0:T(8,128)S(1)}, f32[80,768]{1,0:T(8,128)S(1)}, u32[]{:S(2)}, u32[]{:S(2)}) collective-permute-start(f32[80,768]{1,0:T(8,128)S(1)} %get-tuple-element.315), channel_id=1, source_target_pairs={{1,2},{2,1},{3,4},{4,3},{5,6},{6,5},{7,8},{8,7},{9,10},{10,9},{11,... | collective-permute-start | bytes 737288 | tf_op jit(solution)/shard_map/ppermute | solution.py:615
  6.3 4.9 %collective-permute-start.3 = (f32[72,768]{1,0:T(8,128)S(1)}, f32[72,768]{1,0:T(8,128)S(1)}, u32[]{:S(2)}, u32[]{:S(2)}) collective-permute-start(f32[72,768]{1,0:T(8,128)S(1)} %get-tuple-element.312), channel_id=1, source_target_pairs={{0,1},{1,0},{2,3},{3,2},{4,5},{5,4},{6,7},{7,6},{8,9},{9,8},{10,11... | collective-permute-start | bytes 663560 | tf_op jit(solution)/shard_map/ppermute | solution.py:611
  11.2 3.1 %local_first.1 = (bf16[1024,1024]{1,0:T(8,128)(2,1)S(1)}, bf16[1024,1024]{1,0:T(8,128)(2,1)S(1)}, f32[64,1024]{1,0:T(8,128)S(1)}, f32[64,1024]{1,0:T(8,128)S(1)}) custom-call(f32[8,1024]{1,0:T(8,128)S(1)} %get-tuple-element.309.own, f32[64,1024]{1,0:T(8,128)} %probes.3), custom_call_target="tpu_custom_call" | custom-call | tf_op jit(solution)/shard_map/local_first/pallas_call | solution.py:650
  14.4 0.0 collective-permute-done.3.received.mate
  14.4 1.2 %mate_first.1 = (bf16[512,512]{1,0:T(8,128)(2,1)S(1)}, bf16[512,512]{1,0:T(8,128)(2,1)S(1)}, f32[64,1024]{1,0:T(8,128)S(1)}, f32[72,768]{1,0:T(8,128)S(1)}, f32[3,768,128]{2,1,0:T(8,128)S(1)}) custom-call(f32[8,1024]{1,0:T(8,128)S(1)} %get-tuple-element.309.own, f32[64,1024]{1,0:T(8,128)S(1)} %get-tuple-element.311.partial, ...), custom_call_target="tpu_custom_call" | custom-call | tf_op jit(solution)/shard_map/mate_first/pallas_call | solution.py:666
  15.5 1.9 %collective-permute-start.6 = (f32[72,768]{1,0:T(8,128)S(1)}, f32[72,768]{1,0:T(8,128)S(1)}, u32[]{:S(2)}, u32[]{:S(2)}) collective-permute-start(f32[72,768]{1,0:T(8,128)S(1)} %get-tuple-element.323), channel_id=1, source_target_pairs={{1,2},{2,1},{3,4},{4,3},{5,6},{6,5},{7,8},{8,7},{9,10},{10,9},{11,... | collective-permute-start | bytes 663560 | tf_op jit(solution)/shard_map/ppermute | solution.py:615
  17.5 0.0 collective-permute-done.4.received
  17.5 2.3 %next_first.1 = (bf16[768,256]{1,0:T(8,128)(2,1)S(1)}, bf16[768,256]{1,0:T(8,128)(2,1)S(1)}, bf16[768,768]{1,0:T(8,128)(2,1)S(1)}, bf16[768,768]{1,0:T(8,128)(2,...) custom-call(f32[8,1024]{1,0:T(8,128)S(1)} %get-tuple-element.309.own, f32[64,1024]{1,0:T(8,128)S(1)} %get-tuple-element.313.partial, ...), custom_call_target="tpu_custom_call" | custom-call | tf_op jit(solution)/shard_map/next_first/pallas_call | solution.py:674
  19.8 1.9 %collective-permute-start.5 = (f32[64,768]{1,0:T(8,128)S(1)}, f32[64,768]{1,0:T(8,128)S(1)}, u32[]{:S(2)}, u32[]{:S(2)}) collective-permute-start(f32[64,768]{1,0:T(8,128)S(1)} %get-tuple-element.319), channel_id=1, source_target_pairs={{0,1},{1,0},{2,3},{3,2},{4,5},{5,4},{6,7},{7,6},{8,9},{9,8},{10,11... | collective-permute-start | bytes 589832 | tf_op jit(solution)/shard_map/ppermute | solution.py:611
  21.7 1.0 %local_second.1.partial = f32[64,1024]{1,0:T(8,128)S(1)} custom-call(f32[8,1024]{1,0:T(8,128)S(1)} %get-tuple-element.309.own, f32[64,1024]{1,0:T(8,128)S(1)} %get-tuple-element.316.second, bf16[1024,1024]{1,0:T(8,128)(2,1)S(1)} %get-tuple-element.317.k_high, bf16[1024,1024]{1,0:T(8,128)(2,1)S(1)} %get-tuple-element.318.k_low), custom_call_target="tpu_custom_call" | custom-call | tf_op jit(solution)/shard_map/local_second/pallas_call | solution.py:683
  22.7 0.4 collective-permute-done.5.mate
  23.1 0.3 mate_second.1
  23.4 3.6 %collective-permute-start.8 = (f32[49,8,128]{2,1,0:T(8,128)S(1)}, f32[49,8,128]{2,1,0:T(8,128)S(1)}, u32[]{:S(2)}, u32[]{:S(2)}) collective-permute-start(f32[49,8,128]{2,1,0:T(8,128)S(1)} %get-tuple-element.331), channel_id=1, source_target_pairs={{1,2},{2,1},{3,4},{4,3},{5,6},{6,5},{7,8},{8,7},{9,10},{10,9},{11,... | collective-permute-start | bytes 602120 | tf_op jit(solution)/shard_map/ppermute | solution.py:615
  27.0 0.0 collective-permute-done.6.ahead
  27.0 1.2 %next_second.1 = (f32[64,1024]{1,0:T(8,128)S(1)}, f32[64,768]{1,0:T(8,128)S(1)}) custom-call(f32[64,1024]{1,0:T(8,128)S(1)} %get-tuple-element.322.partial, f32[64,1024]{1,0:T(8,128)S(1)} %get-tuple-element.310.first, f32[64,768]{1,0:T(8,128)S(1)} %collective-permute-done.5.mate, f32[72,768]{1,0:T(8,128)S(1)} %collective-permute-done.6.ahead, ...), custom_call_target="tpu_custom_call" | custom-call | tf_op jit(solution)/shard_map/next_second/pallas_call | solution.py:690
  28.2 1.9 %collective-permute-start.7 = (f32[64,768]{1,0:T(8,128)S(1)}, f32[64,768]{1,0:T(8,128)S(1)}, u32[]{:S(2)}, u32[]{:S(2)}) collective-permute-start(f32[64,768]{1,0:T(8,128)S(1)} %get-tuple-element.330), channel_id=1, source_target_pairs={{0,1},{1,0},{2,3},{3,2},{4,5},{5,4},{6,7},{7,6},{8,9},{9,8},{10,11... | collective-permute-start | bytes 589832 | tf_op jit(solution)/shard_map/ppermute | solution.py:611
  30.1 1.5 %local_third.1 = (f32[64,1024]{1,0:T(8,128)S(1)}, f32[64,768]{1,0:T(8,128)S(1)}, f32[8,64]{1,0:T(8,128)S(1)}) custom-call(f32[8,1024]{1,0:T(8,128)S(1)} %get-tuple-element.309.own, f32[64,1024]{1,0:T(8,128)S(1)} %get-tuple-element.310.first, f32[64,1024]{1,0:T(8,128)S(1)} %get-tuple-element.316.second, f32[64,1024]{1,0:T(8,128)S(1)} %get-tuple-element.328.third, ...), custom_call_target="tpu_custom_call" | custom-call | tf_op jit(solution)/shard_map/local_third/pallas_call | solution.py:699
  31.7 0.0 collective-permute-done.7.mate
  31.7 0.4 mate_third.1.partial
  32.1 0.0 collective-permute-done.8.after
  32.1 0.6 next_third.1
  32.7 0.0 copy-start.2
  32.7 0.0 copy-start.3
  32.7 0.0 copy-start.4
  32.7 0.0 copy-start.5
  32.7 24.6 %all_to_all.10 = f32[32,4,128]{2,1,0:T(4,128)S(1)} all-to-all(f32[32,4,128]{2,1,0:T(4,128)S(1)} %get-tuple-element.334), channel_id=1, replica_groups=mesh['region'=32,'sub'=16] {'region'}, dimensions={0} | all-to-all | bytes 131072 | tf_op jit(solution)/shard_map/all_to_all | solution.py:718
  57.4 12.6 %all_to_all.11.sums = f32[16,4,128]{2,1,0:T(4,128)S(1)} all-to-all(f32[16,4,128]{2,1,0:T(4,128)S(1)} %broadcast_in_dim.5), channel_id=1, replica_groups=mesh['region'=32,'sub'=16] {'sub'}, dimensions={0} | all-to-all | bytes 65536 | tf_op jit(solution)/shard_map/all_to_all | solution.py:719
  70.0 1.2 %finish.1 = (f32[64,1024]{1,0:T(8,128)}, f32[64,1024]{1,0:T(8,128)}, f32[1,1]{1,0:T(1,128)}) custom-call(f32[16,4,128]{2,1,0:T(4,128)S(1)} %all_to_all.11.sums, f32[64,1024]{1,0:T(8,128)S(1)} %get-tuple-element.310.first, f32[64,1024]{1,0:T(8,128)S(1)} %get-tuple-element.316.second, f32[64,1024]{1,0:T(8,128)S(1)} %get-tuple-element.328.third, ...), custom_call_target="tpu_custom_call" | custom-call | tf_op jit(solution)/shard_map/finish/pallas_call | solution.py:720
  71.2 0.0 copy-done.2
  71.2 0.0 copy-done.3
  71.3 0.0 copy-done.4
  71.3 0.0 copy-done.5
  71.3 0.8 %while.35 = (f32[1,1]{1,0:T(1,128)}, f32[64,1024]{1,0:T(8,128)}, f32[64,1024]{1,0:T(8,128)}, f32[64,1024]{1,0:T(8,128)S(1)}, f32[3,1024]{1,0:T(4,128)S(1)}, /*in...) while((f32[1,1]{1,0:T(1,128)}, f32[64,1024]{1,0:T(8,128)}, f32[64,1024]{1,0:T(8,128)}, ...), condition=%region_10.11_spmd, body=%region_1.10_spmd | while | flops 1439929600 | bytes 21131516 | solution.py:732
  (2 shorter events, 0.1 us)
Async XLA Ops:
  1.7 15.7 %collective-permute-start.4 = (f32[80,768]{1,0:T(8,128)S(1)}, f32[80,768]{1,0:T(8,128)S(1)}, u32[]{:S(2)}, u32[]{:S(2)}) collective-permute-start(f32[80,768]{1,0:T(8,128)S(1)} %get-tuple-element.315), channel_id=1, source_target_pairs={{1,2},{2,1},{3,4},{4,3},{5,6},{6,5},{7,8},{8,7},{9,10},{10,9},{11,... | collective-permute-start | bytes 737288 | tf_op jit(solution)/shard_map/ppermute | solution.py:615
  6.3 8.0 %collective-permute-start.3 = (f32[72,768]{1,0:T(8,128)S(1)}, f32[72,768]{1,0:T(8,128)S(1)}, u32[]{:S(2)}, u32[]{:S(2)}) collective-permute-start(f32[72,768]{1,0:T(8,128)S(1)} %get-tuple-element.312), channel_id=1, source_target_pairs={{0,1},{1,0},{2,3},{3,2},{4,5},{5,4},{6,7},{7,6},{8,9},{9,8},{10,11... | collective-permute-start | bytes 663560 | tf_op jit(solution)/shard_map/ppermute | solution.py:611
  15.5 11.5 %collective-permute-start.6 = (f32[72,768]{1,0:T(8,128)S(1)}, f32[72,768]{1,0:T(8,128)S(1)}, u32[]{:S(2)}, u32[]{:S(2)}) collective-permute-start(f32[72,768]{1,0:T(8,128)S(1)} %get-tuple-element.323), channel_id=1, source_target_pairs={{1,2},{2,1},{3,4},{4,3},{5,6},{6,5},{7,8},{8,7},{9,10},{10,9},{11,... | collective-permute-start | bytes 663560 | tf_op jit(solution)/shard_map/ppermute | solution.py:615
  19.8 3.3 %collective-permute-start.5 = (f32[64,768]{1,0:T(8,128)S(1)}, f32[64,768]{1,0:T(8,128)S(1)}, u32[]{:S(2)}, u32[]{:S(2)}) collective-permute-start(f32[64,768]{1,0:T(8,128)S(1)} %get-tuple-element.319), channel_id=1, source_target_pairs={{0,1},{1,0},{2,3},{3,2},{4,5},{5,4},{6,7},{7,6},{8,9},{9,8},{10,11... | collective-permute-start | bytes 589832 | tf_op jit(solution)/shard_map/ppermute | solution.py:611
  23.4 8.7 %collective-permute-start.8 = (f32[49,8,128]{2,1,0:T(8,128)S(1)}, f32[49,8,128]{2,1,0:T(8,128)S(1)}, u32[]{:S(2)}, u32[]{:S(2)}) collective-permute-start(f32[49,8,128]{2,1,0:T(8,128)S(1)} %get-tuple-element.331), channel_id=1, source_target_pairs={{1,2},{2,1},{3,4},{4,3},{5,6},{6,5},{7,8},{8,7},{9,10},{10,9},{11,... | collective-permute-start | bytes 602120 | tf_op jit(solution)/shard_map/ppermute | solution.py:615
  28.2 3.5 %collective-permute-start.7 = (f32[64,768]{1,0:T(8,128)S(1)}, f32[64,768]{1,0:T(8,128)S(1)}, u32[]{:S(2)}, u32[]{:S(2)}) collective-permute-start(f32[64,768]{1,0:T(8,128)S(1)} %get-tuple-element.330), channel_id=1, source_target_pairs={{0,1},{1,0},{2,3},{3,2},{4,5},{5,4},{6,7},{7,6},{8,9},{9,8},{10,11... | collective-permute-start | bytes 589832 | tf_op jit(solution)/shard_map/ppermute | solution.py:611
  32.7 38.5 %copy-start.2 = (f32[64,1024]{1,0:T(8,128)S(1)}, f32[64,1024]{1,0:T(8,128)}, u32[]{:S(2)}) copy-start(f32[64,1024]{1,0:T(8,128)} %probes.3) | copy-start | bytes 786436
  32.7 38.5 %copy-start.3 = (f32[1024]{0:T(1024)S(1)}, f32[1024]{0:T(1024)}, u32[]{:S(2)}) copy-start(f32[1024]{0:T(1024)} %param.17) | copy-start | bytes 12292
  32.7 38.5 %copy-start.4 = (f32[3,1024]{1,0:T(4,128)S(1)}, f32[3,1024]{1,0:T(4,128)}, u32[]{:S(2)}) copy-start(f32[3,1024]{1,0:T(4,128)} %coords.1) | copy-start | bytes 36868
  32.7 38.5 %copy-start.5 = (s32[3,4]{1,0:T(4,128)S(1)}, s32[3,4]{1,0:T(4,128)}, u32[]{:S(2)}) copy-start(s32[3,4]{1,0:T(4,128)} %pair.1) | copy-start | bytes 148

commit v11 on v10

--- a/solution.py
+++ b/solution.py
@@ -471,8 +471,9 @@
     return rows
 
 
-def local_second_kernel(own, second, k_high, k_low, out, halves, *, length):
+def local_second_kernel(own, first, second, k_high, k_low, next_high, next_low, out, given, halves, own_halves, *, length):
     local_product(own, second, k_high, k_low, out, halves, length)
+    own_product(is_right(False), first, (next_high, next_low), given, own_halves, out.shape[1] // length)
 
 
 def local_third_kernel(
@@ -497,13 +498,12 @@
 
 
 def next_second_kernel(
-    partial, first, mate, ahead, mate_high, mate_low, k_high, k_low, out, to_mate, halves, given, *, links
+    partial, mate, ahead, given, mate_high, mate_low, k_high, k_low, out, to_mate, halves, *, links
 ):
     length = halves.shape[1] // links
     right = is_right(False)
     out[...] = partial[...]
     halo_product(is_right(True), lambda at: mate[:, at], {links: (mate_high, mate_low)}, out, halves, links)
-    own_product(right, first, (k_high, k_low), given, halves, links + 1)
     tables = next_tables((k_high, k_low), links, length)
     halo_product(right, received_share(ahead, given), tables, out, halves, links)
     store_send(is_right(True), out, to_mate)
@@ -680,9 +680,13 @@
     )(own, partial, mate, mate_columns, beyond)
 
     mate = swap_mate(to_mate)
-    partial = call(
-        functools.partial(local_second_kernel, length=length), "local_second", whole, [VMEM] * 4, [local_halves]
-    )(own, second, k_high, k_low)
+    partial, given = call(
+        functools.partial(local_second_kernel, length=length),
+        "local_second",
+        (whole, part),
+        [VMEM] * 7,
+        [local_halves, halo_halves],
+    )(own, first, second, k_high, k_low, next_high, next_low)
     partial, to_next = call(
         functools.partial(mate_second_kernel, links=links), "mate_second", (whole, tiled_part), [VMEM] * 4, [halo_halves]
     )(partial, mate, early_high, early_low)
@@ -692,8 +696,8 @@
         "next_second",
         (whole, part),
         [VMEM] * 8,
-        [halo_halves, pltpu.VMEM((rows, span), F32)],
-    )(partial, first, mate, ahead, late_high, late_low, next_high, next_low)
+        [halo_halves],
+    )(partial, mate, ahead, given, late_high, late_low, next_high, next_low)
 
     mate = swap_mate(to_mate)
     partial, given, table = call(

time: 72.6 us -> 72.7 us (level)
  transfers between devices with their start and end apart: 6 -> 6, of which waited for: 1 -> 0; matrix products, arithmetic and copies ran while one was open for 0% -> 0% of each run, Pallas kernels for 15% -> 15%
where the time goes in v11:
time: 72.7 us; the launch traced here: 72.3 us
  blocking collectives  37.8 us (52%)
  starting transfers between devices  18.9 us (26%)
  Pallas kernels  13.7 us (19%)
  between operations  1.01 us (1%)
  loops' own time  0.82 us (1%)
    all_to_all x1, blocking collectives, per_device(): sums = jnp.sum(lax.all_to_all(sums, 'region', 0, 0), axis=0)  24.7 us
    all_to_all x1, blocking collectives, per_device(): lax.all_to_all(jnp.broadcast_to(sums[None], (subs, 4, 128)), 'sub', 0, 0)  13.2 us
    ppermute x3, starting transfers between devices, swap_next(): lax.ppermute(array, AXES, [(i, i + 1 if i % 2 else i - 1) for i in range(...  10.2 us
    ppermute x3, starting transfers between devices, swap_mate(): lax.ppermute(array, AXES, [(i, i ^ 1) for i in range(lax.axis_size(AXES))])  8.71 us
    pallas_call x1, Pallas kernels, per_device(): call(functools.partial(local_first_kernel, links=links), 'local_first', (...  3.13 us
    pallas_call x1, Pallas kernels, per_device(): call(functools.partial(next_first_kernel, links=links), 'next_first', (la...  2.28 us
    pallas_call x1, Pallas kernels, per_device(): call(functools.partial(local_third_kernel, length=length), 'local_third',...  1.53 us
    pallas_call x1, Pallas kernels, per_device(): call(functools.partial(local_second_kernel, length=length), 'local_second...  1.51 us
  transfers between devices with their start and end apart: 6, of which 0 were waited for; matrix products, arithmetic and copies ran while one was open for 0% of the time, Pallas kernels for 15%

profile of v11, /device:TPU:1, one launch (start us, length us, event | category | flops | bytes accessed | tf_op | source)
XLA Modules:
  0.0 72.3 jit_solution(7254047407284114558)
XLA Ops:
  0.6 1.1 %pack.1 = (f32[72,768]{1,0:T(8,128)S(1)}, f32[80,768]{1,0:T(8,128)S(1)}, f32[8,1024]{1,0:T(8,128)S(1)}) custom-call(f32[3,1024]{1,0:T(4,128)} %coords.1, s32[3,4]{1,0:T(4,128)} %pair.1, f32[1,1024]{1,0:T(1,128)} %bitcast.97, f32[64,1024]{1,0:T(8,128)} %probes.3), custom_call_target="tpu_custom_call" | custom-call | tf_op jit(solution)/shard_map/pack/pallas_call | solution.py:637
  1.7 4.6 %collective-permute-start.4 = (f32[80,768]{1,0:T(8,128)S(1)}, f32[80,768]{1,0:T(8,128)S(1)}, u32[]{:S(2)}, u32[]{:S(2)}) collective-permute-start(f32[80,768]{1,0:T(8,128)S(1)} %get-tuple-element.317), channel_id=1, source_target_pairs={{1,2},{2,1},{3,4},{4,3},{5,6},{6,5},{7,8},{8,7},{9,10},{10,9},{11,... | collective-permute-start | bytes 737288 | tf_op jit(solution)/shard_map/ppermute | solution.py:615
  6.3 4.9 %collective-permute-start.3 = (f32[72,768]{1,0:T(8,128)S(1)}, f32[72,768]{1,0:T(8,128)S(1)}, u32[]{:S(2)}, u32[]{:S(2)}) collective-permute-start(f32[72,768]{1,0:T(8,128)S(1)} %get-tuple-element.314), channel_id=1, source_target_pairs={{0,1},{1,0},{2,3},{3,2},{4,5},{5,4},{6,7},{7,6},{8,9},{9,8},{10,11... | collective-permute-start | bytes 663560 | tf_op jit(solution)/shard_map/ppermute | solution.py:611
  11.2 3.1 %local_first.1 = (bf16[1024,1024]{1,0:T(8,128)(2,1)S(1)}, bf16[1024,1024]{1,0:T(8,128)(2,1)S(1)}, f32[64,1024]{1,0:T(8,128)S(1)}, f32[64,1024]{1,0:T(8,128)S(1)}) custom-call(f32[8,1024]{1,0:T(8,128)S(1)} %get-tuple-element.311.own, f32[64,1024]{1,0:T(8,128)} %probes.3), custom_call_target="tpu_custom_call" | custom-call | tf_op jit(solution)/shard_map/local_first/pallas_call | solution.py:650
  14.4 0.0 collective-permute-done.3.received.mate
  14.4 1.2 %mate_first.1 = (bf16[512,512]{1,0:T(8,128)(2,1)S(1)}, bf16[512,512]{1,0:T(8,128)(2,1)S(1)}, f32[64,1024]{1,0:T(8,128)S(1)}, f32[72,768]{1,0:T(8,128)S(1)}, f32[3,768,128]{2,1,0:T(8,128)S(1)}) custom-call(f32[8,1024]{1,0:T(8,128)S(1)} %get-tuple-element.311.own, f32[64,1024]{1,0:T(8,128)S(1)} %get-tuple-element.313.partial, ...), custom_call_target="tpu_custom_call" | custom-call | tf_op jit(solution)/shard_map/mate_first/pallas_call | solution.py:666
  15.5 1.9 %collective-permute-start.6 = (f32[72,768]{1,0:T(8,128)S(1)}, f32[72,768]{1,0:T(8,128)S(1)}, u32[]{:S(2)}, u32[]{:S(2)}) collective-permute-start(f32[72,768]{1,0:T(8,128)S(1)} %get-tuple-element.328), channel_id=1, source_target_pairs={{1,2},{2,1},{3,4},{4,3},{5,6},{6,5},{7,8},{8,7},{9,10},{10,9},{11,... | collective-permute-start | bytes 663560 | tf_op jit(solution)/shard_map/ppermute | solution.py:615
  17.5 0.0 collective-permute-done.4.received
  17.5 2.3 %next_first.1 = (bf16[768,256]{1,0:T(8,128)(2,1)S(1)}, bf16[768,256]{1,0:T(8,128)(2,1)S(1)}, bf16[768,768]{1,0:T(8,128)(2,1)S(1)}, bf16[768,768]{1,0:T(8,128)(2,...) custom-call(f32[8,1024]{1,0:T(8,128)S(1)} %get-tuple-element.311.own, f32[64,1024]{1,0:T(8,128)S(1)} %get-tuple-element.315.partial, ...), custom_call_target="tpu_custom_call" | custom-call | tf_op jit(solution)/shard_map/next_first/pallas_call | solution.py:674
  19.8 1.9 %collective-permute-start.5 = (f32[64,768]{1,0:T(8,128)S(1)}, f32[64,768]{1,0:T(8,128)S(1)}, u32[]{:S(2)}, u32[]{:S(2)}) collective-permute-start(f32[64,768]{1,0:T(8,128)S(1)} %get-tuple-element.324), channel_id=1, source_target_pairs={{0,1},{1,0},{2,3},{3,2},{4,5},{5,4},{6,7},{7,6},{8,9},{9,8},{10,11... | collective-permute-start | bytes 589832 | tf_op jit(solution)/shard_map/ppermute | solution.py:611
  21.7 1.5 %local_second.1 = (f32[64,1024]{1,0:T(8,128)S(1)}, f32[64,768]{1,0:T(8,128)S(1)}) custom-call(f32[8,1024]{1,0:T(8,128)S(1)} %get-tuple-element.311.own, f32[64,1024]{1,0:T(8,128)S(1)} %get-tuple-element.312.first, f32[64,1024]{1,0:T(8,128)S(1)} %get-tuple-element.318.second, bf16[1024,1024]{1,0:T(8,128)(2,1)S(1)} %get-tuple-element.319.k_high, ...), custom_call_target="tpu_custom_call" | custom-call | tf_op jit(solution)/shard_map/local_second/pallas_call | solution.py:683
  23.2 0.0 collective-permute-done.5.mate
  23.2 0.3 mate_second.1
  23.5 3.6 %collective-permute-start.8 = (f32[49,8,128]{2,1,0:T(8,128)S(1)}, f32[49,8,128]{2,1,0:T(8,128)S(1)}, u32[]{:S(2)}, u32[]{:S(2)}) collective-permute-start(f32[49,8,128]{2,1,0:T(8,128)S(1)} %get-tuple-element.335), channel_id=1, source_target_pairs={{1,2},{2,1},{3,4},{4,3},{5,6},{6,5},{7,8},{8,7},{9,10},{10,9},{11,... | collective-permute-start | bytes 602120 | tf_op jit(solution)/shard_map/ppermute | solution.py:615
  27.2 0.0 collective-permute-done.6.ahead
  27.2 0.5 next_second.1
  27.7 1.9 %collective-permute-start.7 = (f32[64,768]{1,0:T(8,128)S(1)}, f32[64,768]{1,0:T(8,128)S(1)}, u32[]{:S(2)}, u32[]{:S(2)}) collective-permute-start(f32[64,768]{1,0:T(8,128)S(1)} %get-tuple-element.334), channel_id=1, source_target_pairs={{0,1},{1,0},{2,3},{3,2},{4,5},{5,4},{6,7},{7,6},{8,9},{9,8},{10,11... | collective-permute-start | bytes 589832 | tf_op jit(solution)/shard_map/ppermute | solution.py:611
  29.6 1.5 %local_third.1 = (f32[64,1024]{1,0:T(8,128)S(1)}, f32[64,768]{1,0:T(8,128)S(1)}, f32[8,64]{1,0:T(8,128)S(1)}) custom-call(f32[8,1024]{1,0:T(8,128)S(1)} %get-tuple-element.311.own, f32[64,1024]{1,0:T(8,128)S(1)} %get-tuple-element.312.first, f32[64,1024]{1,0:T(8,128)S(1)} %get-tuple-element.318.second, f32[64,1024]{1,0:T(8,128)S(1)} %get-tuple-element.332.third, ...), custom_call_target="tpu_custom_call" | custom-call | tf_op jit(solution)/shard_map/local_third/pallas_call | solution.py:703
  31.2 0.0 collective-permute-done.7.mate
  31.2 0.4 mate_third.1.partial
  31.6 0.0 collective-permute-done.8.after
  31.6 0.6 next_third.1
  32.2 0.0 copy-start.2
  32.2 0.0 copy-start.3
  32.2 0.0 copy-start.4
  32.2 0.0 copy-start.5
  32.2 24.7 %all_to_all.10 = f32[32,4,128]{2,1,0:T(4,128)S(1)} all-to-all(f32[32,4,128]{2,1,0:T(4,128)S(1)} %get-tuple-element.338), channel_id=1, replica_groups=mesh['region'=32,'sub'=16] {'region'}, dimensions={0} | all-to-all | bytes 131072 | tf_op jit(solution)/shard_map/all_to_all | solution.py:722
  57.0 13.2 %all_to_all.11.sums = f32[16,4,128]{2,1,0:T(4,128)S(1)} all-to-all(f32[16,4,128]{2,1,0:T(4,128)S(1)} %broadcast_in_dim.5), channel_id=1, replica_groups=mesh['region'=32,'sub'=16] {'sub'}, dimensions={0} | all-to-all | bytes 65536 | tf_op jit(solution)/shard_map/all_to_all | solution.py:723
  70.1 1.2 %finish.1 = (f32[64,1024]{1,0:T(8,128)}, f32[64,1024]{1,0:T(8,128)}, f32[1,1]{1,0:T(1,128)}) custom-call(f32[16,4,128]{2,1,0:T(4,128)S(1)} %all_to_all.11.sums, f32[64,1024]{1,0:T(8,128)S(1)} %get-tuple-element.312.first, f32[64,1024]{1,0:T(8,128)S(1)} %get-tuple-element.318.second, f32[64,1024]{1,0:T(8,128)S(1)} %get-tuple-element.332.third, ...), custom_call_target="tpu_custom_call" | custom-call | tf_op jit(solution)/shard_map/finish/pallas_call | solution.py:724
  71.3 0.0 copy-done.2
  71.3 0.0 copy-done.3
  71.3 0.0 copy-done.4
  71.3 0.0 copy-done.5
  71.4 0.8 %while.35 = (f32[1,1]{1,0:T(1,128)}, f32[64,1024]{1,0:T(8,128)}, f32[64,1024]{1,0:T(8,128)}, f32[64,1024]{1,0:T(8,128)S(1)}, f32[3,1024]{1,0:T(4,128)S(1)}, /*in...) while((f32[1,1]{1,0:T(1,128)}, f32[64,1024]{1,0:T(8,128)}, f32[64,1024]{1,0:T(8,128)}, ...), condition=%region_10.11_spmd, body=%region_1.10_spmd | while | flops 1439929600 | bytes 21131516 | solution.py:736
  (2 shorter events, 0.1 us)
Async XLA Ops:
  1.7 15.7 %collective-permute-start.4 = (f32[80,768]{1,0:T(8,128)S(1)}, f32[80,768]{1,0:T(8,128)S(1)}, u32[]{:S(2)}, u32[]{:S(2)}) collective-permute-start(f32[80,768]{1,0:T(8,128)S(1)} %get-tuple-element.317), channel_id=1, source_target_pairs={{1,2},{2,1},{3,4},{4,3},{5,6},{6,5},{7,8},{8,7},{9,10},{10,9},{11,... | collective-permute-start | bytes 737288 | tf_op jit(solution)/shard_map/ppermute | solution.py:615
  6.3 8.0 %collective-permute-start.3 = (f32[72,768]{1,0:T(8,128)S(1)}, f32[72,768]{1,0:T(8,128)S(1)}, u32[]{:S(2)}, u32[]{:S(2)}) collective-permute-start(f32[72,768]{1,0:T(8,128)S(1)} %get-tuple-element.314), channel_id=1, source_target_pairs={{0,1},{1,0},{2,3},{3,2},{4,5},{5,4},{6,7},{7,6},{8,9},{9,8},{10,11... | collective-permute-start | bytes 663560 | tf_op jit(solution)/shard_map/ppermute | solution.py:611
  15.5 11.6 %collective-permute-start.6 = (f32[72,768]{1,0:T(8,128)S(1)}, f32[72,768]{1,0:T(8,128)S(1)}, u32[]{:S(2)}, u32[]{:S(2)}) collective-permute-start(f32[72,768]{1,0:T(8,128)S(1)} %get-tuple-element.328), channel_id=1, source_target_pairs={{1,2},{2,1},{3,4},{4,3},{5,6},{6,5},{7,8},{8,7},{9,10},{10,9},{11,... | collective-permute-start | bytes 663560 | tf_op jit(solution)/shard_map/ppermute | solution.py:615
  19.8 3.4 %collective-permute-start.5 = (f32[64,768]{1,0:T(8,128)S(1)}, f32[64,768]{1,0:T(8,128)S(1)}, u32[]{:S(2)}, u32[]{:S(2)}) collective-permute-start(f32[64,768]{1,0:T(8,128)S(1)} %get-tuple-element.324), channel_id=1, source_target_pairs={{0,1},{1,0},{2,3},{3,2},{4,5},{5,4},{6,7},{7,6},{8,9},{9,8},{10,11... | collective-permute-start | bytes 589832 | tf_op jit(solution)/shard_map/ppermute | solution.py:611
  23.5 8.1 %collective-permute-start.8 = (f32[49,8,128]{2,1,0:T(8,128)S(1)}, f32[49,8,128]{2,1,0:T(8,128)S(1)}, u32[]{:S(2)}, u32[]{:S(2)}) collective-permute-start(f32[49,8,128]{2,1,0:T(8,128)S(1)} %get-tuple-element.335), channel_id=1, source_target_pairs={{1,2},{2,1},{3,4},{4,3},{5,6},{6,5},{7,8},{8,7},{9,10},{10,9},{11,... | collective-permute-start | bytes 602120 | tf_op jit(solution)/shard_map/ppermute | solution.py:615
  27.7 3.5 %collective-permute-start.7 = (f32[64,768]{1,0:T(8,128)S(1)}, f32[64,768]{1,0:T(8,128)S(1)}, u32[]{:S(2)}, u32[]{:S(2)}) collective-permute-start(f32[64,768]{1,0:T(8,128)S(1)} %get-tuple-element.334), channel_id=1, source_target_pairs={{0,1},{1,0},{2,3},{3,2},{4,5},{5,4},{6,7},{7,6},{8,9},{9,8},{10,11... | collective-permute-start | bytes 589832 | tf_op jit(solution)/shard_map/ppermute | solution.py:611
  32.2 39.1 %copy-start.2 = (f32[64,1024]{1,0:T(8,128)S(1)}, f32[64,1024]{1,0:T(8,128)}, u32[]{:S(2)}) copy-start(f32[64,1024]{1,0:T(8,128)} %probes.3) | copy-start | bytes 786436
  32.2 39.1 %copy-start.3 = (f32[1024]{0:T(1024)S(1)}, f32[1024]{0:T(1024)}, u32[]{:S(2)}) copy-start(f32[1024]{0:T(1024)} %param.17) | copy-start | bytes 12292
  32.2 39.1 %copy-start.4 = (f32[3,1024]{1,0:T(4,128)S(1)}, f32[3,1024]{1,0:T(4,128)}, u32[]{:S(2)}) copy-start(f32[3,1024]{1,0:T(4,128)} %coords.1) | copy-start | bytes 36868
  32.2 39.1 %copy-start.5 = (s32[3,4]{1,0:T(4,128)S(1)}, s32[3,4]{1,0:T(4,128)}, u32[]{:S(2)}) copy-start(s32[3,4]{1,0:T(4,128)} %pair.1) | copy-start | bytes 148
